TPU v7x, 32 devices: a whole 2x2x4 slice. The times are simulated.
32 devices in a mesh: gx: 16 (over z, x, core), gy: 2 (over y).
Axes of the slice: x: 2, y: 2, z: 4, core: 2. Of those that a mesh axis runs over, the one named last changes fastest.
Arguments:
- initial: float32 [64, 256, 512], P('gx', 'gy'), may hold values from -4 to 4
- kappa: float32 [64, 256, 512], P('gx', 'gy'), may hold values from 0.04 to 0.12
- velocity: float32 [64, 256, 512], P('gx', 'gy'), may hold values from 0.05 to 0.2
- rate: float32 [64, 256, 512], P('gx', 'gy'), may hold values from 0.05 to 0.3
Outputs:
- final: float32 [64, 256, 512], P('gx', 'gy')
All inputs are finite; a program needn't handle non-finite values.
Results may differ from a plain program's by a relative error of at most 0.00002.
Values sent between devices are 32-bit elements; how exact they have to be, the bound alone decides.
No kernel may reach another device: no remote copies, remote signals or barrier semaphores. Data moves between devices by JAX's collectives and lax.ppermute only.
A program may use at most 64 MiB of HBM per device.

v0:
```python
import jax
import jax.numpy as jnp
from jax import lax
from jax.sharding import PartitionSpec as P

STEPS = 4
ITERS = 2


robin_p = 0.6


def extended(cells, sides, width):
    for axis, dim in sides:
        count = lax.axis_size(axis)
        ends = count - 1
        head = lax.slice_in_dim(cells, 0, width, axis=dim)
        tail = lax.slice_in_dim(cells, cells.shape[dim] - width, cells.shape[dim], axis=dim)
        cells = jnp.concatenate(
            [
                lax.ppermute(tail, axis, [(i, (i + 1) % count) for i in range(ends)]),
                cells,
                lax.ppermute(head, axis, [((i + 1) % count, i) for i in range(ends)]),
            ],
            axis=dim,
        )
    return cells


def passed_along(value, axis, steps):
    count = lax.axis_size(axis)
    pairs = [(source, (source + steps) % count) for source in range(count)]
    return lax.ppermute(value, axis, pairs)


def make_ghosts(field, data_left, data_right):
    first = field[0]
    last = field[-1]
    ghost_left = (data_left + first * (1.0 - robin_p / 2)) / (1.0 + robin_p / 2)
    ghost_right = (data_right + last * (1.0 - robin_p / 2)) / (1.0 + robin_p / 2)
    return (first, ghost_left, last, ghost_right)


def stencil(center, minus_x, plus_x, upper, lower, kappa, velocity, rate):
    plus_z = jnp.pad(center[:, :, 1:], ((0, 0), (0, 0), (0, 1)))
    minus_z = jnp.pad(center[:, :, :-1], ((0, 0), (0, 0), (1, 0)))
    lap = plus_x + minus_x
    lap = lap + upper + lower
    lap = lap + plus_z + minus_z
    lap = lap - 6.0 * center
    react = rate * center**3 / (1.0 + center * center)
    return center + kappa * lap - velocity * (center - minus_x) - react


def advance(field, kappa, velocity, rate, data_left, data_right):
    first, ghost_left, last, ghost_right = make_ghosts(field, data_left, data_right)
    widened = extended(field, (("gy", 1),), 1)
    minus_x = jnp.concatenate([ghost_left[None], field[:-1]], axis=0)
    plus_x = jnp.concatenate([field[1:], ghost_right[None]], axis=0)
    updated = stencil(
        field, minus_x, plus_x, widened[:, 2:], widened[:, :-2], kappa, velocity, rate
    )
    return (updated, first, ghost_left, last, ghost_right)


def combine_data(value, ghost):
    return value - ghost + robin_p * (value + ghost) / 2


def local(initial, kappa, velocity, rate):
    rows_own = initial.shape[1]
    start, kappa_w, velocity_w, rate_w = (initial, kappa, velocity, rate)
    margin = 0
    full_rows = rows_own + 2 * margin
    zero_plane = jnp.zeros((full_rows, initial.shape[2]), jnp.float32)
    data_left = jnp.stack([zero_plane] * STEPS)
    data_right = jnp.stack([zero_plane] * STEPS)
    field = start
    for sweep in range(ITERS):
        field = start
        firsts, lefts, lasts, rights = ([], [], [], [])
        for step in range(STEPS):
            field, first, ghost_left, last, ghost_right = advance(
                field, kappa_w, velocity_w, rate_w, data_left[step], data_right[step]
            )
            firsts.append(first)
            lefts.append(ghost_left)
            lasts.append(last)
            rights.append(ghost_right)
        if sweep + 1 < ITERS:
            backward = jnp.stack([jnp.stack(firsts), jnp.stack(lefts)])
            forward = jnp.stack([jnp.stack(lasts), jnp.stack(rights)])
            got_next = passed_along(backward, "gx", -1)
            got_prev = passed_along(forward, "gx", 1)
            data_right = combine_data(got_next[0], got_next[1])
            data_left = combine_data(got_prev[0], got_prev[1])
    return field


def solution(mesh):
    placed = (P("gx", "gy", None), P("gx", "gy", None), P("gx", "gy", None), P("gx", "gy", None))
    return jax.shard_map(
        local, mesh=mesh, in_specs=placed, out_specs=P("gx", "gy", None), check_vma=False
    )
```

profile of v0, /device:TPU:14, one launch (start us, length us, event | category | flops | bytes accessed | tf_op | source)
XLA Modules:
  0.0 107.8 jit_solution(14208034068405390911)
XLA Ops:
  0.0 1.0 fusion.117
  1.0 2.4 %collective-permute-start = (f32[4,1,512]{2,1,0:T(1,128)S(1)}, f32[4,1,512]{2,1,0:T(1,128)S(1)}, u32[]{:S(2)}, u32[]{:S(2)}) collective-permute-start(f32[4,1,512]{2,1,0:T(1,128)S(1)} %get-tuple-element.63), channel_id=1, source_target_pairs={{1,0},{3,2},{5,4},{7,6},{9,8},{11,10},{13,12},{15,14},{17,16},{19,... | collective-permute-start | bytes 24584 | tf_op jit(solution)/shard_map/ppermute | solution.py:23
  3.4 1.3 %collective-permute-start.1 = (f32[4,1,512]{2,1,0:T(1,128)S(1)}, f32[4,1,512]{2,1,0:T(1,128)S(1)}, u32[]{:S(2)}, u32[]{:S(2)}) collective-permute-start(f32[4,1,512]{2,1,0:T(1,128)S(1)} %get-tuple-element.64), channel_id=1, source_target_pairs={{0,1},{2,3},{4,5},{6,7},{8,9},{10,11},{12,13},{14,15},{16,17},{18,... | collective-permute-start | bytes 24584 | tf_op jit(solution)/shard_map/ppermute | solution.py:21
  4.7 1.5 %fusion.116 = (f32[3,128,512]{2,1,0:T(8,128)S(1)}, f32[3,128,512]{2,1,0:T(8,128)S(1)}) fusion(f32[4,128,512]{2,1,0:T(8,128)} %param.4), kind=kLoop, calls=%fused_computation.184 | loop fusion | bytes 3145728 | tf_op jit(solution)/shard_map/slice | solution.py:58
  6.2 0.0 copy-start
  6.2 0.0 copy-start.1
  6.2 0.0 copy-start.2
  6.2 0.4 fusion.115
  6.6 0.1 fusion.105
  6.8 0.0 collective-permute-done
  6.8 2.2 %collective-permute-done.1 = f32[4,1,512]{2,1,0:T(1,128)S(1)} collective-permute-done((f32[4,1,512]{2,1,0:T(1,128)S(1)}, f32[4,1,512]{2,1,0:T(1,128)S(1)}, u32[]{:S(2)}, u32[]{:S(2)}) %collective-permute-start.1) | collective-permute-done | bytes 8224 | tf_op jit(solution)/shard_map/ppermute | solution.py:21
  9.0 1.1 %fusion.19 = f32[4,128,512]{2,1,0:T(8,128)S(1)} fusion(f32[4,128,512]{2,1,0:T(8,128)S(1)} %copy-done.3, f32[4,128,512]{2,1,0:T(8,128)S(1)} %copy-done.1, f32[3,128,512]{2,1,0:T(8,128)S(1)} %get-tuple-element.62, f32[4,1,512]{2,1,0:T(1,128)S(1)} %collective-permute-done.1, f32[4,1,512]{2,1,0:T(1,128)S(1)} %collective-permute-done, ...), kind=kLoop, calls=%fused_computation.38 | loop fusion | flops 5767168 | bytes 9449472 | tf_op jit(solution)/shard_map/sub | solution.py:52
  10.1 0.2 fusion.113
  10.3 0.4 fusion.112
  10.7 3.7 %collective-permute-start.2 = (f32[4,1,512]{2,1,0:T(1,128)S(1)}, f32[4,1,512]{2,1,0:T(1,128)S(1)}, u32[]{:S(2)}, u32[]{:S(2)}) collective-permute-start(f32[4,1,512]{2,1,0:T(1,128)S(1)} %get-tuple-element.57), channel_id=1, source_target_pairs={{1,0},{3,2},{5,4},{7,6},{9,8},{11,10},{13,12},{15,14},{17,16},{19,... | collective-permute-start | bytes 24584 | tf_op jit(solution)/shard_map/ppermute | solution.py:23
  14.3 1.3 %collective-permute-start.3 = (f32[4,1,512]{2,1,0:T(1,128)S(1)}, f32[4,1,512]{2,1,0:T(1,128)S(1)}, u32[]{:S(2)}, u32[]{:S(2)}) collective-permute-start(f32[4,1,512]{2,1,0:T(1,128)S(1)} %get-tuple-element.58), channel_id=1, source_target_pairs={{0,1},{2,3},{4,5},{6,7},{8,9},{10,11},{12,13},{14,15},{16,17},{18,... | collective-permute-start | bytes 24584 | tf_op jit(solution)/shard_map/ppermute | solution.py:21
  15.6 0.1 fusion.106
  15.8 0.0 collective-permute-done.2
  15.8 4.1 %collective-permute-done.3 = f32[4,1,512]{2,1,0:T(1,128)S(1)} collective-permute-done((f32[4,1,512]{2,1,0:T(1,128)S(1)}, f32[4,1,512]{2,1,0:T(1,128)S(1)}, u32[]{:S(2)}, u32[]{:S(2)}) %collective-permute-start.3) | collective-permute-done | bytes 8224 | tf_op jit(solution)/shard_map/ppermute | solution.py:21
  19.9 1.1 %fusion.27 = f32[4,128,512]{2,1,0:T(8,128)S(1)} fusion(f32[4,128,512]{2,1,0:T(8,128)S(1)} %copy-done, f32[4,128,512]{2,1,0:T(8,128)S(1)} %fusion.19, f32[4,128,512]{2,1,0:T(8,128)S(1)} %copy-done.1, f32[4,1,512]{2,1,0:T(1,128)S(1)} %collective-permute-done.3, f32[4,1,512]{2,1,0:T(1,128)S(1)} %collective-permute-done.2, ...), kind=kLoop, calls=%fused_computation.46 | loop fusion | flops 5767168 | bytes 9449472 | tf_op jit(solution)/shard_map/sub | solution.py:52
  21.0 0.2 fusion.110
  21.2 0.4 fusion.109
  21.6 1.6 %collective-permute-start.4 = (f32[4,1,512]{2,1,0:T(1,128)S(1)}, f32[4,1,512]{2,1,0:T(1,128)S(1)}, u32[]{:S(2)}, u32[]{:S(2)}) collective-permute-start(f32[4,1,512]{2,1,0:T(1,128)S(1)} %get-tuple-element.51), channel_id=1, source_target_pairs={{1,0},{3,2},{5,4},{7,6},{9,8},{11,10},{13,12},{15,14},{17,16},{19,... | collective-permute-start | bytes 24584 | tf_op jit(solution)/shard_map/ppermute | solution.py:23
  23.3 1.3 %collective-permute-start.5 = (f32[4,1,512]{2,1,0:T(1,128)S(1)}, f32[4,1,512]{2,1,0:T(1,128)S(1)}, u32[]{:S(2)}, u32[]{:S(2)}) collective-permute-start(f32[4,1,512]{2,1,0:T(1,128)S(1)} %get-tuple-element.52), channel_id=1, source_target_pairs={{0,1},{2,3},{4,5},{6,7},{8,9},{10,11},{12,13},{14,15},{16,17},{18,... | collective-permute-start | bytes 24584 | tf_op jit(solution)/shard_map/ppermute | solution.py:21
  24.6 0.1 fusion.107
  24.7 0.0 collective-permute-done.4
  24.7 4.1 %collective-permute-done.5 = f32[4,1,512]{2,1,0:T(1,128)S(1)} collective-permute-done((f32[4,1,512]{2,1,0:T(1,128)S(1)}, f32[4,1,512]{2,1,0:T(1,128)S(1)}, u32[]{:S(2)}, u32[]{:S(2)}) %collective-permute-start.5) | collective-permute-done | bytes 8224 | tf_op jit(solution)/shard_map/ppermute | solution.py:21
  28.8 1.1 %fusion.30 = f32[4,128,512]{2,1,0:T(8,128)S(1)} fusion(f32[4,128,512]{2,1,0:T(8,128)S(1)} %copy-done, f32[4,128,512]{2,1,0:T(8,128)S(1)} %fusion.27, f32[4,128,512]{2,1,0:T(8,128)S(1)} %copy-done.1, f32[4,1,512]{2,1,0:T(1,128)S(1)} %collective-permute-done.5, f32[4,1,512]{2,1,0:T(1,128)S(1)} %collective-permute-done.4, ...), kind=kLoop, calls=%fused_computation.49 | loop fusion | flops 5767168 | bytes 9449472 | tf_op jit(solution)/shard_map/sub | solution.py:52
  29.9 0.1 fusion.108
  30.1 0.2 fusion.22
  30.2 0.2 pad_maximum_fusion
  30.5 0.1 collective-permute-start.6
  30.6 0.2 maximum_bitcast_fusion.1
  30.7 0.2 pad_maximum_fusion.1
  31.0 0.5 collective-permute-start.7
  31.5 45.0 %collective-permute-done.6 = f32[2,4,128,512]{3,2,1,0:T(8,128)S(1)} collective-permute-done((f32[2,4,128,512]{3,2,1,0:T(8,128)S(1)}, f32[2,4,128,512]{3,2,1,0:T(8,128)S(1)}, u32[]{:S(2)}, u32[]{:S(2)}) %collective-permute-start.6) | collective-permute-done | bytes 2097184 | tf_op jit(solution)/shard_map/ppermute | solution.py:33
  76.6 0.2 multiply_add_fusion.7
  76.8 1.8 %collective-permute-done.7 = f32[2,4,128,512]{3,2,1,0:T(8,128)S(1)} collective-permute-done((f32[2,4,128,512]{3,2,1,0:T(8,128)S(1)}, f32[2,4,128,512]{3,2,1,0:T(8,128)S(1)}, u32[]{:S(2)}, u32[]{:S(2)}) %collective-permute-start.7) | collective-permute-done | bytes 2097184 | tf_op jit(solution)/shard_map/ppermute | solution.py:33
  78.6 0.2 multiply_add_fusion.6
  78.8 0.1 fusion.93
  78.9 1.1 %fusion.9 = f32[4,128,512]{2,1,0:T(8,128)S(1)} fusion(f32[4,128,512]{2,1,0:T(8,128)S(1)} %copy-done.3, f32[4,128,512]{2,1,0:T(8,128)S(1)} %copy-done.1, f32[3,128,512]{2,1,0:T(8,128)S(1)} %get-tuple-element.62, f32[4,1,512]{2,1,0:T(1,128)S(1)} %collective-permute-done.1, f32[4,1,512]{2,1,0:T(1,128)S(1)} %collective-permute-done, ...), kind=kLoop, calls=%fused_computation.28 | loop fusion | flops 5767168 | bytes 9449472 | tf_op jit(solution)/shard_map/sub | solution.py:52
  80.1 0.2 fusion.103
  80.3 0.4 fusion.102
  80.7 1.6 %collective-permute-start.8 = (f32[4,1,512]{2,1,0:T(1,128)S(1)}, f32[4,1,512]{2,1,0:T(1,128)S(1)}, u32[]{:S(2)}, u32[]{:S(2)}) collective-permute-start(f32[4,1,512]{2,1,0:T(1,128)S(1)} %get-tuple-element.27), channel_id=1, source_target_pairs={{1,0},{3,2},{5,4},{7,6},{9,8},{11,10},{13,12},{15,14},{17,16},{19,... | collective-permute-start | bytes 24584 | tf_op jit(solution)/shard_map/ppermute | solution.py:23
  82.3 1.3 %collective-permute-start.9 = (f32[4,1,512]{2,1,0:T(1,128)S(1)}, f32[4,1,512]{2,1,0:T(1,128)S(1)}, u32[]{:S(2)}, u32[]{:S(2)}) collective-permute-start(f32[4,1,512]{2,1,0:T(1,128)S(1)} %get-tuple-element.28), channel_id=1, source_target_pairs={{0,1},{2,3},{4,5},{6,7},{8,9},{10,11},{12,13},{14,15},{16,17},{18,... | collective-permute-start | bytes 24584 | tf_op jit(solution)/shard_map/ppermute | solution.py:21
  83.6 0.1 fusion.89
  83.8 0.0 collective-permute-done.8
  83.8 4.1 %collective-permute-done.9 = f32[4,1,512]{2,1,0:T(1,128)S(1)} collective-permute-done((f32[4,1,512]{2,1,0:T(1,128)S(1)}, f32[4,1,512]{2,1,0:T(1,128)S(1)}, u32[]{:S(2)}, u32[]{:S(2)}) %collective-permute-start.9) | collective-permute-done | bytes 8224 | tf_op jit(solution)/shard_map/ppermute | solution.py:21
  87.9 1.1 %fusion.33 = f32[4,128,512]{2,1,0:T(8,128)S(1)} fusion(f32[4,128,512]{2,1,0:T(8,128)S(1)} %copy-done, f32[4,128,512]{2,1,0:T(8,128)S(1)} %fusion.9, f32[4,128,512]{2,1,0:T(8,128)S(1)} %copy-done.1, f32[4,1,512]{2,1,0:T(1,128)S(1)} %collective-permute-done.9, f32[4,1,512]{2,1,0:T(1,128)S(1)} %collective-permute-done.8, ...), kind=kLoop, calls=%fused_computation.52 | loop fusion | flops 5767168 | bytes 9449472 | tf_op jit(solution)/shard_map/sub | solution.py:52
  89.0 0.2 fusion.100
  89.2 0.4 fusion.99
  89.6 1.6 %collective-permute-start.10 = (f32[4,1,512]{2,1,0:T(1,128)S(1)}, f32[4,1,512]{2,1,0:T(1,128)S(1)}, u32[]{:S(2)}, u32[]{:S(2)}) collective-permute-start(f32[4,1,512]{2,1,0:T(1,128)S(1)} %get-tuple-element.19), channel_id=1, source_target_pairs={{1,0},{3,2},{5,4},{7,6},{9,8},{11,10},{13,12},{15,14},{17,16},{19,... | collective-permute-start | bytes 24584 | tf_op jit(solution)/shard_map/ppermute | solution.py:23
  91.2 1.5 %collective-permute-start.11 = (f32[4,1,512]{2,1,0:T(1,128)S(1)}, f32[4,1,512]{2,1,0:T(1,128)S(1)}, u32[]{:S(2)}, u32[]{:S(2)}) collective-permute-start(f32[4,1,512]{2,1,0:T(1,128)S(1)} %get-tuple-element.20), channel_id=1, source_target_pairs={{0,1},{2,3},{4,5},{6,7},{8,9},{10,11},{12,13},{14,15},{16,17},{18,... | collective-permute-start | bytes 24584 | tf_op jit(solution)/shard_map/ppermute | solution.py:21
  92.7 0.1 fusion.85
  92.9 3.9 %collective-permute-done.11 = f32[4,1,512]{2,1,0:T(1,128)S(1)} collective-permute-done((f32[4,1,512]{2,1,0:T(1,128)S(1)}, f32[4,1,512]{2,1,0:T(1,128)S(1)}, u32[]{:S(2)}, u32[]{:S(2)}) %collective-permute-start.11) | collective-permute-done | bytes 8224 | tf_op jit(solution)/shard_map/ppermute | solution.py:21
  96.8 1.1 %fusion.36 = f32[4,128,512]{2,1,0:T(8,128)S(1)} fusion(f32[4,128,512]{2,1,0:T(8,128)S(1)} %copy-done, f32[4,128,512]{2,1,0:T(8,128)S(1)} %fusion.33, f32[4,128,512]{2,1,0:T(8,128)S(1)} %copy-done.1, f32[4,1,512]{2,1,0:T(1,128)S(1)} %collective-permute-done.11, f32[4,1,512]{2,1,0:T(1,128)S(1)} %collective-permute-done.10, ...), kind=kLoop, calls=%fused_computation.55 | loop fusion | flops 5767168 | bytes 9449472 | tf_op jit(solution)/shard_map/sub | solution.py:52
  97.9 0.2 fusion.97
  98.1 0.4 fusion.96
  98.5 1.6 %collective-permute-start.12 = (f32[4,1,512]{2,1,0:T(1,128)S(1)}, f32[4,1,512]{2,1,0:T(1,128)S(1)}, u32[]{:S(2)}, u32[]{:S(2)}) collective-permute-start(f32[4,1,512]{2,1,0:T(1,128)S(1)} %get-tuple-element.11), channel_id=1, source_target_pairs={{1,0},{3,2},{5,4},{7,6},{9,8},{11,10},{13,12},{15,14},{17,16},{19,... | collective-permute-start | bytes 24584 | tf_op jit(solution)/shard_map/ppermute | solution.py:23
  100.2 1.3 %collective-permute-start.13 = (f32[4,1,512]{2,1,0:T(1,128)S(1)}, f32[4,1,512]{2,1,0:T(1,128)S(1)}, u32[]{:S(2)}, u32[]{:S(2)}) collective-permute-start(f32[4,1,512]{2,1,0:T(1,128)S(1)} %get-tuple-element.12), channel_id=1, source_target_pairs={{0,1},{2,3},{4,5},{6,7},{8,9},{10,11},{12,13},{14,15},{16,17},{18,... | collective-permute-start | bytes 24584 | tf_op jit(solution)/shard_map/ppermute | solution.py:21
  101.5 0.1 fusion.81
  101.6 0.0 collective-permute-done.12
  101.6 4.1 %collective-permute-done.13 = f32[4,1,512]{2,1,0:T(1,128)S(1)} collective-permute-done((f32[4,1,512]{2,1,0:T(1,128)S(1)}, f32[4,1,512]{2,1,0:T(1,128)S(1)}, u32[]{:S(2)}, u32[]{:S(2)}) %collective-permute-start.13) | collective-permute-done | bytes 8224 | tf_op jit(solution)/shard_map/ppermute | solution.py:21
  105.7 2.1 %fusion.39 = f32[4,128,512]{2,1,0:T(8,128)} fusion(f32[4,128,512]{2,1,0:T(8,128)S(1)} %copy-done, f32[4,128,512]{2,1,0:T(8,128)S(1)} %fusion.36, f32[4,128,512]{2,1,0:T(8,128)S(1)} %copy-done.1, f32[4,1,512]{2,1,0:T(1,128)S(1)} %collective-permute-done.13, f32[4,1,512]{2,1,0:T(1,128)S(1)} %collective-permute-done.12, ...), kind=kLoop, calls=%fused_computation.58 | loop fusion | flops 5767168 | bytes 9449472 | tf_op jit(solution)/shard_map/sub | solution.py:52
  (11 shorter events, 0.1 us)
Async XLA Ops:
  0.0 6.2 %copy-start.3 = (f32[4,128,512]{2,1,0:T(8,128)S(1)}, f32[4,128,512]{2,1,0:T(8,128)}, u32[]{:S(2)}) copy-start(f32[4,128,512]{2,1,0:T(8,128)} %param.4) | copy-start | bytes 3145732
  1.0 5.8 %collective-permute-start = (f32[4,1,512]{2,1,0:T(1,128)S(1)}, f32[4,1,512]{2,1,0:T(1,128)S(1)}, u32[]{:S(2)}, u32[]{:S(2)}) collective-permute-start(f32[4,1,512]{2,1,0:T(1,128)S(1)} %get-tuple-element.63), channel_id=1, source_target_pairs={{1,0},{3,2},{5,4},{7,6},{9,8},{11,10},{13,12},{15,14},{17,16},{19,... | collective-permute-start | bytes 24584 | tf_op jit(solution)/shard_map/ppermute | solution.py:23
  3.4 5.5 %collective-permute-start.1 = (f32[4,1,512]{2,1,0:T(1,128)S(1)}, f32[4,1,512]{2,1,0:T(1,128)S(1)}, u32[]{:S(2)}, u32[]{:S(2)}) collective-permute-start(f32[4,1,512]{2,1,0:T(1,128)S(1)} %get-tuple-element.64), channel_id=1, source_target_pairs={{0,1},{2,3},{4,5},{6,7},{8,9},{10,11},{12,13},{14,15},{16,17},{18,... | collective-permute-start | bytes 24584 | tf_op jit(solution)/shard_map/ppermute | solution.py:21
  6.2 2.7 %copy-start = (f32[4,128,512]{2,1,0:T(8,128)S(1)}, f32[4,128,512]{2,1,0:T(8,128)}, u32[]{:S(2)}) copy-start(f32[4,128,512]{2,1,0:T(8,128)} %param.7) | copy-start | bytes 3145732
  6.2 2.7 %copy-start.1 = (f32[4,128,512]{2,1,0:T(8,128)S(1)}, f32[4,128,512]{2,1,0:T(8,128)}, u32[]{:S(2)}) copy-start(f32[4,128,512]{2,1,0:T(8,128)} %param.5) | copy-start | bytes 3145732
  6.2 2.7 %copy-start.2 = (f32[4,128,512]{2,1,0:T(8,128)S(1)}, f32[4,128,512]{2,1,0:T(8,128)}, u32[]{:S(2)}) copy-start(f32[4,128,512]{2,1,0:T(8,128)} %param.6) | copy-start | bytes 3145732
  10.7 5.1 %collective-permute-start.2 = (f32[4,1,512]{2,1,0:T(1,128)S(1)}, f32[4,1,512]{2,1,0:T(1,128)S(1)}, u32[]{:S(2)}, u32[]{:S(2)}) collective-permute-start(f32[4,1,512]{2,1,0:T(1,128)S(1)} %get-tuple-element.57), channel_id=1, source_target_pairs={{1,0},{3,2},{5,4},{7,6},{9,8},{11,10},{13,12},{15,14},{17,16},{19,... | collective-permute-start | bytes 24584 | tf_op jit(solution)/shard_map/ppermute | solution.py:23
  14.3 5.5 %collective-permute-start.3 = (f32[4,1,512]{2,1,0:T(1,128)S(1)}, f32[4,1,512]{2,1,0:T(1,128)S(1)}, u32[]{:S(2)}, u32[]{:S(2)}) collective-permute-start(f32[4,1,512]{2,1,0:T(1,128)S(1)} %get-tuple-element.58), channel_id=1, source_target_pairs={{0,1},{2,3},{4,5},{6,7},{8,9},{10,11},{12,13},{14,15},{16,17},{18,... | collective-permute-start | bytes 24584 | tf_op jit(solution)/shard_map/ppermute | solution.py:21
  21.6 3.1 %collective-permute-start.4 = (f32[4,1,512]{2,1,0:T(1,128)S(1)}, f32[4,1,512]{2,1,0:T(1,128)S(1)}, u32[]{:S(2)}, u32[]{:S(2)}) collective-permute-start(f32[4,1,512]{2,1,0:T(1,128)S(1)} %get-tuple-element.51), channel_id=1, source_target_pairs={{1,0},{3,2},{5,4},{7,6},{9,8},{11,10},{13,12},{15,14},{17,16},{19,... | collective-permute-start | bytes 24584 | tf_op jit(solution)/shard_map/ppermute | solution.py:23
  23.3 5.5 %collective-permute-start.5 = (f32[4,1,512]{2,1,0:T(1,128)S(1)}, f32[4,1,512]{2,1,0:T(1,128)S(1)}, u32[]{:S(2)}, u32[]{:S(2)}) collective-permute-start(f32[4,1,512]{2,1,0:T(1,128)S(1)} %get-tuple-element.52), channel_id=1, source_target_pairs={{0,1},{2,3},{4,5},{6,7},{8,9},{10,11},{12,13},{14,15},{16,17},{18,... | collective-permute-start | bytes 24584 | tf_op jit(solution)/shard_map/ppermute | solution.py:21
  30.5 46.1 %collective-permute-start.6 = (f32[2,4,128,512]{3,2,1,0:T(8,128)S(1)}, f32[2,4,128,512]{3,2,1,0:T(8,128)S(1)}, u32[]{:S(2)}, u32[]{:S(2)}) collective-permute-start(f32[2,4,128,512]{3,2,1,0:T(8,128)S(1)} %pad_maximum_fusion), channel_id=1, source_target_pairs={{0,30},{2,0},{4,2},{6,4},{8,6},{10,8},{12,10},{14,12},{16,14},{18,... | collective-permute-start | bytes 6291464 | tf_op jit(solution)/shard_map/ppermute | solution.py:33
  31.0 47.6 %collective-permute-start.7 = (f32[2,4,128,512]{3,2,1,0:T(8,128)S(1)}, f32[2,4,128,512]{3,2,1,0:T(8,128)S(1)}, u32[]{:S(2)}, u32[]{:S(2)}) collective-permute-start(f32[2,4,128,512]{3,2,1,0:T(8,128)S(1)} %pad_maximum_fusion.1), channel_id=1, source_target_pairs={{0,2},{2,4},{4,6},{6,8},{8,10},{10,12},{12,14},{14,16},{16,18},{18... | collective-permute-start | bytes 6291464 | tf_op jit(solution)/shard_map/ppermute | solution.py:33
  80.7 3.1 %collective-permute-start.8 = (f32[4,1,512]{2,1,0:T(1,128)S(1)}, f32[4,1,512]{2,1,0:T(1,128)S(1)}, u32[]{:S(2)}, u32[]{:S(2)}) collective-permute-start(f32[4,1,512]{2,1,0:T(1,128)S(1)} %get-tuple-element.27), channel_id=1, source_target_pairs={{1,0},{3,2},{5,4},{7,6},{9,8},{11,10},{13,12},{15,14},{17,16},{19,... | collective-permute-start | bytes 24584 | tf_op jit(solution)/shard_map/ppermute | solution.py:23
  82.3 5.5 %collective-permute-start.9 = (f32[4,1,512]{2,1,0:T(1,128)S(1)}, f32[4,1,512]{2,1,0:T(1,128)S(1)}, u32[]{:S(2)}, u32[]{:S(2)}) collective-permute-start(f32[4,1,512]{2,1,0:T(1,128)S(1)} %get-tuple-element.28), channel_id=1, source_target_pairs={{0,1},{2,3},{4,5},{6,7},{8,9},{10,11},{12,13},{14,15},{16,17},{18,... | collective-permute-start | bytes 24584 | tf_op jit(solution)/shard_map/ppermute | solution.py:21
  89.6 3.3 %collective-permute-start.10 = (f32[4,1,512]{2,1,0:T(1,128)S(1)}, f32[4,1,512]{2,1,0:T(1,128)S(1)}, u32[]{:S(2)}, u32[]{:S(2)}) collective-permute-start(f32[4,1,512]{2,1,0:T(1,128)S(1)} %get-tuple-element.19), channel_id=1, source_target_pairs={{1,0},{3,2},{5,4},{7,6},{9,8},{11,10},{13,12},{15,14},{17,16},{19,... | collective-permute-start | bytes 24584 | tf_op jit(solution)/shard_map/ppermute | solution.py:23
  91.2 5.5 %collective-permute-start.11 = (f32[4,1,512]{2,1,0:T(1,128)S(1)}, f32[4,1,512]{2,1,0:T(1,128)S(1)}, u32[]{:S(2)}, u32[]{:S(2)}) collective-permute-start(f32[4,1,512]{2,1,0:T(1,128)S(1)} %get-tuple-element.20), channel_id=1, source_target_pairs={{0,1},{2,3},{4,5},{6,7},{8,9},{10,11},{12,13},{14,15},{16,17},{18,... | collective-permute-start | bytes 24584 | tf_op jit(solution)/shard_map/ppermute | solution.py:21
  98.5 3.1 %collective-permute-start.12 = (f32[4,1,512]{2,1,0:T(1,128)S(1)}, f32[4,1,512]{2,1,0:T(1,128)S(1)}, u32[]{:S(2)}, u32[]{:S(2)}) collective-permute-start(f32[4,1,512]{2,1,0:T(1,128)S(1)} %get-tuple-element.11), channel_id=1, source_target_pairs={{1,0},{3,2},{5,4},{7,6},{9,8},{11,10},{13,12},{15,14},{17,16},{19,... | collective-permute-start | bytes 24584 | tf_op jit(solution)/shard_map/ppermute | solution.py:23
  100.2 5.5 %collective-permute-start.13 = (f32[4,1,512]{2,1,0:T(1,128)S(1)}, f32[4,1,512]{2,1,0:T(1,128)S(1)}, u32[]{:S(2)}, u32[]{:S(2)}) collective-permute-start(f32[4,1,512]{2,1,0:T(1,128)S(1)} %get-tuple-element.12), channel_id=1, source_target_pairs={{0,1},{2,3},{4,5},{6,7},{8,9},{10,11},{12,13},{14,15},{16,17},{18,... | collective-permute-start | bytes 24584 | tf_op jit(solution)/shard_map/ppermute | solution.py:21
where the time goes:
time: 108 us
  waiting for transfers between devices  69.4 us (64%)
  starting transfers between devices  21.2 us (20%)
  other arithmetic  11 us (10%)
  local copies, waits for them, and re-layouts  5.83 us (5%)
    ppermute x2, waiting for transfers between devices, passed_along(): return lax.ppermute(value, axis, pairs)  46.8 us
    ppermute x6, waiting for transfers between devices, extended(): lax.ppermute(tail, axis, [(i, (i + 1) % count) for i in range(ends)])  22.5 us
    ppermute x6, starting transfers between devices, extended(): lax.ppermute(head, axis, [((i + 1) % count, i) for i in range(ends)])  12.7 us
    sub x7, other arithmetic, stencil(): return center + kappa * lap - velocity * (center - minus_x) - react  8.74 us
    ppermute x6, starting transfers between devices, extended(): lax.ppermute(tail, axis, [(i, (i + 1) % count) for i in range(ends)])  7.93 us
    slice x6, local copies, waits for them, and re-layouts, advance(): minus_x = jnp.concatenate([ghost_left[None], field[:-1]], axis=0)  2.51 us
    slice x6, local copies, waits for them, and re-layouts, stencil(): plus_z = jnp.pad(center[:, :, 1:], ((0, 0), (0, 0), (0, 1)))  2.25 us
  transfers between devices with their start and end apart: 14, of which 8 were waited for; matrix products, arithmetic and copies ran while one was open for 3% of the time, Pallas kernels for 0%

commit v1 on v0

v1 whole, which is shorter than its diff:
```python
import functools

import jax
import jax.numpy as jnp
from jax import lax
from jax.experimental import pallas as pl
from jax.experimental.pallas import tpu as pltpu
from jax.sharding import PartitionSpec as P

robin_p = 0.6
own = (1.0 - robin_p / 2) / (1.0 + robin_p / 2)
far = ((1.0 - own) + robin_p * (1.0 + own) / 2) / (1.0 + robin_p / 2)

VMEM = pl.BlockSpec(memory_space=pltpu.VMEM)
ANY = pl.BlockSpec(memory_space=pl.ANY)
HALO = 4
ROWS = 8
LANES = 128


def parity(axis):
    return lax.rem(lax.axis_index(axis), 2)


def plane_at(d, odd):
    return d + odd * (3 - 2 * d)


def pick(odd, yes, no):
    return jnp.where(jnp.broadcast_to(odd == 1, yes.shape), yes, no)


def load(ref, index, tile):
    rows = pl.ds(tile * ROWS if isinstance(tile, int) else pl.multiple_of(tile * ROWS, ROWS), ROWS)
    return [ref[*index, rows, k : k + LANES] for k in range(0, ref.shape[-1], LANES)]


def store(ref, index, tile, pieces):
    rows = pl.ds(tile * ROWS if isinstance(tile, int) else pl.multiple_of(tile * ROWS, ROWS), ROWS)
    for k, piece in enumerate(pieces):
        ref[*index, rows, k * LANES : (k + 1) * LANES] = piece


def ghost(mine, received=None):
    if received is None:
        return [m * own for m in mine]
    return [r * far + m * own for r, m in zip(received, mine)]


def updated(odd, cur, before, after, toward, away, kappa, velocity, rate):
    row = lax.broadcasted_iota(jnp.int32, (ROWS, LANES), 0)
    lane = lax.broadcasted_iota(jnp.int32, (ROWS, LANES), 1)
    zero = jnp.zeros((ROWS, LANES), jnp.float32)
    out = []
    for k, c in enumerate(cur):
        up = pltpu.roll(jnp.where(row == ROWS - 1, before[k], c), 1, 0)
        down = pltpu.roll(jnp.where(row == 0, after[k], c), ROWS - 1, 0)
        low = cur[k - 1] if k else zero
        high = cur[k + 1] if k + 1 < len(cur) else zero
        left = pltpu.roll(jnp.where(lane == LANES - 1, low, c), 1, 1)
        right = pltpu.roll(jnp.where(lane == 0, high, c), LANES - 1, 1)
        minus_x = pick(odd, away[k], toward[k]) if toward is not None else away[k]
        lap = away[k] + toward[k]
        lap = lap + up + down
        lap = lap + left + right
        lap = lap - 6.0 * c
        square = c * c
        bottom = 1.0 + square
        inverse = pl.reciprocal(bottom, approx=True)
        inverse = inverse * (2.0 - bottom * inverse)
        react = rate[k] * c * (square * inverse)
        out.append(c + kappa[k] * lap - velocity[k] * (c - minus_x) - react)
    return out


def sweep(odd, wanted, source, coefs, margins, near, distant, sink, edge=True):
    needed = sorted({e for d in wanted for e in (d - 1, d, d + 1) if 0 <= e <= 3})
    tiles = source(wanted[0])[0].shape[-2] // ROWS
    last = tiles - 1

    def body(tile, edge_tile):
        if edge_tile:
            before, after = last - 1, 0
        else:
            before, after = lax.select(tile == 0, last, tile - 1), tile + 1
        state = {d: load(*source(d), tile) for d in needed}
        for d in wanted:
            cur = state[d]
            toward = state[d - 1] if d > 0 else ghost(cur, near(tile))
            away = state[d + 1] if d < 3 else ghost(cur, distant(tile))
            p = plane_at(d, odd)
            kvr = [load(ref, (*lead, p), 0 if edge_tile else tile) for ref, lead in (margins if edge_tile else coefs)]
            sink(d, tile, updated(odd, cur, load(*source(d), before), load(*source(d), after), toward, away, *kvr))

    def loop(tile, carry):
        body(tile, False)
        return carry

    lax.fori_loop(0, last, loop, 0)
    if edge:
        body(last, True)


def none(tile):
    return None


def pack_kernel(n_halo, initial, kappa, velocity, rate, plane, *rest):
    halos, (tiles, sems) = rest[:n_halo], rest[n_halo:]
    odd_x, odd_y = parity("gx"), parity("gy")
    rows = initial.shape[1]
    copies = [pltpu.make_async_copy(initial.at[plane_at(0, odd_x)], plane, sems.at[0])]
    for f, field in enumerate((initial, kappa, velocity, rate)):
        copies.append(pltpu.make_async_copy(field.at[:, :ROWS, :], tiles.at[f, 0], sems.at[1 + 2 * f]))
        copies.append(pltpu.make_async_copy(field.at[:, rows - ROWS :, :], tiles.at[f, 1], sems.at[2 + 2 * f]))
    for copy in copies:
        copy.start()
    for copy in copies[1:]:
        copy.wait()
    for f in range(4):
        first, last = tiles[f, 0, :, :HALO], tiles[f, 1, :, ROWS - HALO :]
        halos[0][4 * f : 4 * f + 4] = pick(odd_y, first, last)
        if n_halo > 1:
            halos[1][4 * f : 4 * f + 4] = pick(odd_y, last, first)
    copies[0].wait()


def first_kernel(n_halo, initial, kappa, velocity, rate, *rest):
    halos, (u0, u1, margin, message) = rest[:n_halo], rest[n_halo:]
    odd, odd_y = parity("gx"), parity("gy")
    rows = initial.shape[1]
    for f in range(4):
        one = halos[0][4 * f : 4 * f + 4]
        two = halos[1][4 * f : 4 * f + 4] if n_halo > 1 else jnp.zeros_like(one)
        edge = jnp.concatenate([pick(odd_y, two, one), pick(odd_y, one, two)], axis=1)
        if f == 0:
            u0[:, rows:, :] = edge
        else:
            margin[f - 1] = edge

    def copy(tile, carry):
        for p in range(4):
            store(u0, (p,), tile, load(initial, (p,), tile))
        return carry

    lax.fori_loop(0, rows // ROWS, copy, 0)

    def sink(d, tile, pieces):
        store(u1, (plane_at(d, odd),), tile, pieces)

    coefs = [(ref, ()) for ref in (kappa, velocity, rate)]
    margins = [(margin, (i,)) for i in range(3)]
    sweep(odd, [0, 1, 2, 3], lambda d: (u0, (plane_at(d, odd),)), coefs, margins, none, none, sink)
    p = plane_at(0, odd)
    message[:rows] = u1[p, :rows]
    zero = u0[p, rows:]
    one = u1[p, rows:]
    if n_halo > 1:
        message[rows : rows + ROWS] = zero
        message[rows + ROWS :] = one
    else:
        half = lax.broadcasted_iota(jnp.int32, zero.shape, 0) // HALO
        message[rows:] = jnp.where(half == odd_y, zero, pltpu.roll(one, HALO, 0))


def second_kernel(u0, u1, margin, kappa, velocity, rate, message2, message3, beside, u2):
    odd = parity("gx")
    rows = kappa.shape[1]
    coefs = [(ref, ()) for ref in (kappa, velocity, rate)]
    margins = [(margin, (i,)) for i in range(3)]

    def sink2(d, tile, pieces):
        store(u2, (plane_at(d, odd),), tile, pieces)
        if d == 0:
            store(message2, (), tile, pieces)
        if d == 3:
            store(beside, (2,), tile, pieces)

    sweep(odd, [0, 1, 2, 3], lambda d: (u1, (plane_at(d, odd),)), coefs, margins, none, none, sink2)

    def sink3(d, tile, pieces):
        if d == 0:
            store(message3, (), tile, pieces)
        if d == 3:
            store(beside, (3,), tile, pieces)

    sweep(odd, [0, 3], lambda d: (u2, (plane_at(d, odd),)), coefs, margins, none, none, sink3, edge=False)
    beside[3, rows:] = jnp.zeros(beside[3, rows:].shape, jnp.float32)
    beside[0] = u0[plane_at(3, odd)]
    beside[1] = u1[plane_at(3, odd)]


def third_kernel(n_halo, u0, u1, margin, kappa, velocity, rate, near0, near1, beside,
                 out, state, v1, v2, v3, edges, done, sems):
    odd, odd_y = parity("gx"), parity("gy")
    rows = kappa.shape[1]
    coefs = [(ref, ()) for ref in (kappa, velocity, rate)]
    margins = [(margin, (i,)) for i in range(3)]
    if n_halo > 1:
        edges[0] = near1[rows : rows + ROWS]
        edges[1] = near1[rows + ROWS :]
    else:
        edges[0] = near1[rows:]
        edges[1] = pltpu.roll(near1[rows:], HALO, 0)

    def near(step, ref):
        last = rows // ROWS
        return lambda tile: load(edges, (step,), 0) if isinstance(tile, int) and tile == last else load(ref, (), tile)

    def distant(step):
        return lambda tile: load(beside, (step,), tile)

    def sink1(d, tile, pieces):
        store(v1, (d // 3,), tile, pieces)

    def source1(d):
        return (v1, (d // 3,)) if d in (0, 3) else (u1, (plane_at(d, odd),))

    def sink2(d, tile, pieces):
        if d < 2:
            store(state, (d,), tile, pieces)
        else:
            store(v2, (d - 2,), tile, pieces)

    def source2(d):
        return (state, (d,)) if d < 2 else (v2, (d - 2,))

    def sink3(d, tile, pieces):
        if d < 3:
            store(state, (d + 1,), tile, pieces)
        else:
            store(v3, (), tile, pieces)

    def source3(d):
        return (state, (d + 1,)) if d < 3 else (v3, ())

    def sink4(d, tile, pieces):
        store(done, (d - 2,), tile, pieces)

    sweep(odd, [0, 3], lambda d: (u0, (plane_at(d, odd),)), coefs, margins, near(0, near0), distant(0), sink1)
    sweep(odd, [0, 1, 2, 3], source1, coefs, margins, near(1, near1), distant(1), sink2)
    sweep(odd, [1, 2, 3], source2, coefs, margins, none, distant(2), sink3)
    sweep(odd, [2, 3], source3, coefs, margins, none, distant(3), sink4, edge=False)
    copies = [pltpu.make_async_copy(done.at[d - 2], out.at[plane_at(d, odd)], sems.at[d - 2]) for d in (2, 3)]
    for copy in copies:
        copy.start()
    for copy in copies:
        copy.wait()


def fourth_kernel(state, margin, kappa, velocity, rate, near2, out_in, out, base, gain, v3, done, sem):
    del out_in
    odd = parity("gx")
    rows = kappa.shape[1]
    coefs = [(ref, ()) for ref in (kappa, velocity, rate)]
    margins = [(margin, (i,)) for i in range(3)]

    def sink3(d, tile, pieces):
        store(v3, (), tile, pieces)

    sweep(odd, [0], lambda d: (state, (d,)), coefs, margins, lambda tile: load(near2, (), tile), none, sink3)

    def source3(d):
        return (v3, ()) if d == 0 else (state, (d + 1,))

    def sink4(d, tile, pieces):
        store(done if d else base, (), tile, pieces)

    sweep(odd, [0, 1], source3, coefs, margins, none, none, sink4, edge=False)
    copy = pltpu.make_async_copy(done, out.at[plane_at(1, odd)], sem)
    copy.start()
    p = plane_at(0, odd)

    def gains(tile, carry):
        both = zip(load(kappa, (p,), tile), load(velocity, (p,), tile))
        store(gain, (), tile, [far * (k + pick(odd, jnp.zeros_like(v), v)) for k, v in both])
        return carry

    lax.fori_loop(0, rows // ROWS, gains, 0)
    copy.wait()


def last_kernel(base, gain, near3, out_in, out, done, sem):
    del out_in
    odd = parity("gx")
    done[...] = base[...] + gain[...] * near3[...]
    copy = pltpu.make_async_copy(done, out.at[plane_at(0, odd)], sem)
    copy.start()
    copy.wait()


def pairs(count, first, wrap):
    out = []
    for i in range(first, count, 2):
        if i + 1 < count or wrap:
            out += [(i, (i + 1) % count), ((i + 1) % count, i)]
    return out


def f32(*shape):
    return jax.ShapeDtypeStruct(shape, jnp.float32)


def call(kernel, out_shape, in_specs, out_specs, scratch=(), aliases=None, cells=0):
    return pl.pallas_call(
        kernel,
        out_shape=out_shape,
        in_specs=in_specs,
        out_specs=out_specs,
        scratch_shapes=scratch,
        input_output_aliases=aliases or {},
        cost_estimate=pl.CostEstimate(flops=25 * cells, bytes_accessed=16 * cells, transcendentals=cells),
        compiler_params=pltpu.CompilerParams(vmem_limit_bytes=24 * 1024 * 1024),
    )


def local(initial, kappa, velocity, rate):
    planes, rows, lanes = initial.shape
    full = rows + ROWS
    count_y = lax.axis_size("gy")
    count_x = lax.axis_size("gx")
    n_halo = 1 if count_y == 2 else 2
    plane = rows * lanes
    chips = pairs(count_x, 1, True)
    cores = pairs(count_x, 0, False)
    rows_pairs = [pairs(count_y, 0, False), pairs(count_y, 1, False)][:n_halo]

    plane0, *halos = call(
        functools.partial(pack_kernel, n_halo),
        [f32(rows, lanes)] + [f32(16, HALO, lanes)] * n_halo,
        [ANY] * 4,
        [ANY] + [VMEM] * n_halo,
        [pltpu.VMEM((4, 2, planes, ROWS, lanes), jnp.float32), pltpu.SemaphoreType.DMA((9,))],
        cells=plane // 2,
    )(initial, kappa, velocity, rate)
    near0 = lax.ppermute(plane0, "gx", chips)
    halos = [lax.ppermute(halo, "gy", which) for halo, which in zip(halos, rows_pairs)]
    u0, u1, margin, message1 = call(
        functools.partial(first_kernel, n_halo),
        [f32(planes, full, lanes), f32(planes, full, lanes), f32(3, planes, ROWS, lanes), f32(rows + ROWS * n_halo, lanes)],
        [VMEM] * (4 + n_halo),
        [VMEM] * 4,
        cells=4 * plane,
    )(initial, kappa, velocity, rate, *halos)
    near1 = lax.ppermute(message1, "gx", chips)
    message2, message3, beside = call(
        second_kernel,
        [f32(full, lanes), f32(rows, lanes), f32(4, full, lanes)],
        [VMEM] * 6,
        [VMEM] * 3,
        [pltpu.VMEM((planes, full, lanes), jnp.float32)],
        cells=6 * plane,
    )(u0, u1, margin, kappa, velocity, rate)
    beside = lax.ppermute(beside, "gx", cores)
    message2, near0 = lax.optimization_barrier((message2, near0))
    near2 = lax.ppermute(message2, "gx", chips)
    message3, near1 = lax.optimization_barrier((message3, near1))
    near3 = lax.ppermute(message3, "gx", chips)
    extra = pltpu.VMEM((2, full, lanes), jnp.float32)
    out, state = call(
        functools.partial(third_kernel, n_halo),
        [f32(planes, rows, lanes), f32(4, full, lanes)],
        [VMEM] * 9,
        [ANY, VMEM],
        [extra, extra, pltpu.VMEM((full, lanes), jnp.float32), pltpu.VMEM((2, ROWS, lanes), jnp.float32),
         pltpu.VMEM((2, rows, lanes), jnp.float32), pltpu.SemaphoreType.DMA((2,))],
        cells=11 * plane,
    )(u0, u1, margin, kappa, velocity, rate, near0, near1, beside)
    out, base, gain = call(
        fourth_kernel,
        [f32(planes, rows, lanes), f32(rows, lanes), f32(rows, lanes)],
        [VMEM] * 6 + [ANY],
        [ANY, VMEM, VMEM],
        [pltpu.VMEM((full, lanes), jnp.float32), pltpu.VMEM((rows, lanes), jnp.float32), pltpu.SemaphoreType.DMA],
        {6: 0},
        cells=3 * plane,
    )(state, margin, kappa, velocity, rate, near2, out)
    return call(
        last_kernel,
        f32(planes, rows, lanes),
        [VMEM] * 3 + [ANY],
        ANY,
        [pltpu.VMEM((rows, lanes), jnp.float32), pltpu.SemaphoreType.DMA],
        {3: 0},
        cells=plane // 8,
    )(base, gain, near3, out)


def solution(mesh):
    placed = P("gx", "gy", None)
    return jax.shard_map(local, mesh=mesh, in_specs=(placed,) * 4, out_specs=placed, check_vma=False)
```

time: 108 us -> 51.3 us (0.47)
  the two profiles are of different devices: /device:TPU:14 before, /device:TPU:1 now
where the time goes in v1:
time: 51.3 us; the launch traced here: 51 us
  Pallas kernels  17.6 us (34%)
  starting transfers between devices  15.9 us (31%)
  waiting for transfers between devices  12.5 us (24%)
  local copies, waits for them, and re-layouts  4.92 us (10%)
    ppermute x1, waiting for transfers between devices, local(): near0 = lax.ppermute(plane0, 'gx', chips)  8.77 us
    ppermute x1, starting transfers between devices, local(): near2 = lax.ppermute(message2, 'gx', chips)  8.26 us
    pallas_call x1, Pallas kernels, local(): call(functools.partial(third_kernel, n_halo), [f32(planes, rows, lanes),...  7.39 us
    unnamed x14, local copies, waits for them, and re-layouts  4.92 us
    pallas_call x1, Pallas kernels, local(): call(fourth_kernel, [f32(planes, rows, lanes), f32(rows, lanes), f32(rows...  3.65 us
    pallas_call x1, Pallas kernels, local(): call(second_kernel, [f32(full, lanes), f32(rows, lanes), f32(4, full, lan...  3.4 us
    ppermute x1, waiting for transfers between devices, local(): lax.ppermute(halo, 'gy', which)  3.22 us
    ppermute x1, starting transfers between devices, local(): near3 = lax.ppermute(message3, 'gx', chips)  2.48 us
  transfers between devices with their start and end apart: 6, of which 3 were waited for; matrix products, arithmetic and copies ran while one was open for 0% of the time, Pallas kernels for 22%

profile of v1, /device:TPU:1, one launch (start us, length us, event | category | flops | bytes accessed | tf_op | source)
XLA Modules:
  0.0 51.0 jit_solution(14855439752008489032)
XLA Ops:
  0.0 0.0 copy-start
  0.0 1.2 %copy-done = f32[4,128,512]{2,1,0:T(8,128)S(1)} copy-done((f32[4,128,512]{2,1,0:T(8,128)S(1)}, f32[4,128,512]{2,1,0:T(8,128)}, u32[]{:S(2)}) %copy-start) | copy-done | bytes 1048600
  1.2 0.0 copy-start.2
  1.2 1.2 %copy-done.2 = f32[4,128,512]{2,1,0:T(8,128)S(1)} copy-done((f32[4,128,512]{2,1,0:T(8,128)S(1)}, f32[4,128,512]{2,1,0:T(8,128)}, u32[]{:S(2)}) %copy-start.2) | copy-done | bytes 1048600
  2.5 0.0 copy-start.4
  2.5 1.2 %copy-done.4 = f32[4,128,512]{2,1,0:T(8,128)S(1)} copy-done((f32[4,128,512]{2,1,0:T(8,128)S(1)}, f32[4,128,512]{2,1,0:T(8,128)}, u32[]{:S(2)}) %copy-start.4) | copy-done | bytes 1048600
  3.7 0.0 copy-start.6
  3.7 1.2 %copy-done.6 = f32[4,128,512]{2,1,0:T(8,128)S(1)} copy-done((f32[4,128,512]{2,1,0:T(8,128)S(1)}, f32[4,128,512]{2,1,0:T(8,128)}, u32[]{:S(2)}) %copy-start.6) | copy-done | bytes 1048600
  4.9 0.3 shard_map.46
  5.2 0.0 copy-start.1
  5.2 0.0 copy-start.3
  5.2 0.0 copy-start.5
  5.3 2.1 %collective-permute-start = (f32[16,4,512]{2,1,0:T(4,128)S(1)}, f32[16,4,512]{2,1,0:T(4,128)S(1)}, u32[]{:S(2)}, u32[]{:S(2)}) collective-permute-start(f32[16,4,512]{2,1,0:T(4,128)S(1)} %get-tuple-element.23), channel_id=1, source_target_pairs={{0,1},{1,0},{2,3},{3,2},{4,5},{5,4},{6,7},{7,6},{8,9},{9,8},{10,11... | collective-permute-start | bytes 393224 | tf_op jit(solution)/shard_map/ppermute | solution.py:337
  7.4 3.2 %collective-permute-done.rest_0_ = f32[16,4,512]{2,1,0:T(4,128)S(1)} collective-permute-done((f32[16,4,512]{2,1,0:T(4,128)S(1)}, f32[16,4,512]{2,1,0:T(4,128)S(1)}, u32[]{:S(2)}, u32[]{:S(2)}) %collective-permute-start) | collective-permute-done | bytes 131104 | tf_op jit(solution)/shard_map/ppermute | solution.py:337
  10.6 2.1 %shard_map.47 = (f32[4,136,512]{2,1,0:T(8,128)S(1)}, f32[4,136,512]{2,1,0:T(8,128)S(1)}, f32[3,4,8,512]{3,2,1,0:T(8,128)S(1)}, f32[136,512]{1,0:T(8,128)S(1)}) custom-call(f32[4,128,512]{2,1,0:T(8,128)S(1)} %copy-done.6, f32[4,128,512]{2,1,0:T(8,128)S(1)} %copy-done, f32[4,128,512]{2,1,0:T(8,128)S(1)} %copy-done.2, f32[4,128,512]{2,1,0:T(8,128)S(1)} %copy-done.4, ...), custom_call_target="tpu_custom_call" | custom-call | flops 6553600 | bytes 4194304 | tf_op jit(solution)/shard_map/pallas_call | solution.py:338
  12.7 0.0 copy-done.1
  12.7 0.0 copy-done.3
  12.7 0.0 copy-done.5
  12.7 3.4 %shard_map.48 = (f32[136,512]{1,0:T(8,128)S(1)}, f32[128,512]{1,0:T(8,128)S(1)}, f32[4,136,512]{2,1,0:T(8,128)S(1)}) custom-call(f32[4,136,512]{2,1,0:T(8,128)S(1)} %get-tuple-element.24.u0, f32[4,136,512]{2,1,0:T(8,128)S(1)} %get-tuple-element.25.u1, f32[3,4,8,512]{3,2,1,0:T(8,128)S(1)} %get-tuple-element.26.margin, f32[4,128,512]{2,1,0:T(8,128)S(1)} %copy-done.1, ...), custom_call_target="tpu_custom_call" | custom-call | flops 9830400 | bytes 6291456 | tf_op jit(solution)/shard_map/pallas_call | solution.py:346
  16.1 1.3 %collective-permute-start.3 = (f32[4,136,512]{2,1,0:T(8,128)S(1)}, f32[4,136,512]{2,1,0:T(8,128)S(1)}, u32[]{:S(2)}, u32[]{:S(2)}) collective-permute-start(f32[4,136,512]{2,1,0:T(8,128)S(1)} %get-tuple-element.33), channel_id=1, source_target_pairs={{0,2},{2,0},{4,6},{6,4},{8,10},{10,8},{12,14},{14,12},{16,18},{18,... | collective-permute-start | bytes 3342344 | tf_op jit(solution)/shard_map/ppermute | solution.py:354
  17.4 1.4 %collective-permute-start.1 = (f32[128,512]{1,0:T(8,128)S(1)}, f32[128,512]{1,0:T(8,128)S(1)}, u32[]{:S(2)}, u32[]{:S(2)}) collective-permute-start(f32[128,512]{1,0:T(8,128)S(1)} %get-tuple-element.28), channel_id=1, source_target_pairs={{2,4},{4,2},{6,8},{8,6},{10,12},{12,10},{14,16},{16,14},{18,20},{2... | collective-permute-start | bytes 786440 | tf_op jit(solution)/shard_map/ppermute | solution.py:336
  18.8 0.4 collective-permute-start.2
  19.2 8.8 %collective-permute-done.1.near0 = f32[128,512]{1,0:T(8,128)S(1)} collective-permute-done((f32[128,512]{1,0:T(8,128)S(1)}, f32[128,512]{1,0:T(8,128)S(1)}, u32[]{:S(2)}, u32[]{:S(2)}) %collective-permute-start.1) | collective-permute-done | bytes 262176 | tf_op jit(solution)/shard_map/ppermute | solution.py:336
  27.9 8.3 %collective-permute-start.4 = (f32[136,512]{1,0:T(8,128)S(1)}, f32[136,512]{1,0:T(8,128)S(1)}, u32[]{:S(2)}, u32[]{:S(2)}) collective-permute-start(f32[136,512]{1,0:T(8,128)S(1)} %get-tuple-element.35), channel_id=1, source_target_pairs={{2,4},{4,2},{6,8},{8,6},{10,12},{12,10},{14,16},{16,14},{18,20},{2... | collective-permute-start | bytes 835592 | tf_op jit(solution)/shard_map/ppermute | solution.py:356
  36.2 0.5 collective-permute-done.2.near1
  36.7 2.5 %collective-permute-start.5 = (f32[128,512]{1,0:T(8,128)S(1)}, f32[128,512]{1,0:T(8,128)S(1)}, u32[]{:S(2)}, u32[]{:S(2)}) collective-permute-start(f32[128,512]{1,0:T(8,128)S(1)} %get-tuple-element.39), channel_id=1, source_target_pairs={{2,4},{4,2},{6,8},{8,6},{10,12},{12,10},{14,16},{16,14},{18,20},{2... | collective-permute-start | bytes 786440 | tf_op jit(solution)/shard_map/ppermute | solution.py:358
  39.2 0.0 collective-permute-done.3.beside
  39.2 7.4 %shard_map.49 = (f32[4,128,512]{2,1,0:T(8,128)}, f32[4,136,512]{2,1,0:T(8,128)S(1)}) custom-call(f32[4,136,512]{2,1,0:T(8,128)S(1)} %get-tuple-element.24.u0, f32[4,136,512]{2,1,0:T(8,128)S(1)} %get-tuple-element.25.u1, f32[3,4,8,512]{3,2,1,0:T(8,128)S(1)} %get-tuple-element.26.margin, f32[4,128,512]{2,1,0:T(8,128)S(1)} %copy-done.1, ...), custom_call_target="tpu_custom_call" | custom-call | flops 18022400 | bytes 11534336 | tf_op jit(solution)/shard_map/pallas_call | solution.py:360
  46.6 0.0 collective-permute-done.4.near2
  46.6 3.6 %shard_map.50 = (f32[4,128,512]{2,1,0:T(8,128)}, f32[128,512]{1,0:T(8,128)S(1)}, f32[128,512]{1,0:T(8,128)S(1)}) custom-call(f32[4,136,512]{2,1,0:T(8,128)S(1)} %get-tuple-element.34.state, f32[3,4,8,512]{3,2,1,0:T(8,128)S(1)} %get-tuple-element.26.margin, f32[4,128,512]{2,1,0:T(8,128)S(1)} %copy-done.1, ...), custom_call_target="tpu_custom_call", output_to_operand_aliasing={{0}: (6, {})} | custom-call | flops 4915200 | bytes 3145728 | tf_op jit(solution)/shard_map/pallas_call | solution.py:369
  50.3 0.0 collective-permute-done.5.near3
  50.3 0.8 %shard_map.51 = f32[4,128,512]{2,1,0:T(8,128)} custom-call(f32[128,512]{1,0:T(8,128)S(1)} %get-tuple-element.37.base, f32[128,512]{1,0:T(8,128)S(1)} %get-tuple-element.38.gain, f32[128,512]{1,0:T(8,128)S(1)} %collective-permute-done.5.near3, f32[4,128,512]{2,1,0:T(8,128)} %get-tuple-element.40.out_in), custom_call_target="tpu_custom_call", output_to_operand_aliasing={{}: (3, {})} | custom-call | flops 204800 | bytes 131072 | tf_op jit(solution)/shard_map/pallas_call | solution.py:378
Async XLA Ops:
  0.0 1.2 %copy-start = (f32[4,128,512]{2,1,0:T(8,128)S(1)}, f32[4,128,512]{2,1,0:T(8,128)}, u32[]{:S(2)}) copy-start(f32[4,128,512]{2,1,0:T(8,128)} %kappa.9) | copy-start | bytes 3145732
  1.2 1.2 %copy-start.2 = (f32[4,128,512]{2,1,0:T(8,128)S(1)}, f32[4,128,512]{2,1,0:T(8,128)}, u32[]{:S(2)}) copy-start(f32[4,128,512]{2,1,0:T(8,128)} %velocity.9) | copy-start | bytes 3145732
  2.5 1.2 %copy-start.4 = (f32[4,128,512]{2,1,0:T(8,128)S(1)}, f32[4,128,512]{2,1,0:T(8,128)}, u32[]{:S(2)}) copy-start(f32[4,128,512]{2,1,0:T(8,128)} %rate.9) | copy-start | bytes 3145732
  3.7 1.2 %copy-start.6 = (f32[4,128,512]{2,1,0:T(8,128)S(1)}, f32[4,128,512]{2,1,0:T(8,128)}, u32[]{:S(2)}) copy-start(f32[4,128,512]{2,1,0:T(8,128)} %initial.3) | copy-start | bytes 3145732
  5.2 7.5 %copy-start.1 = (f32[4,128,512]{2,1,0:T(8,128)S(1)}, f32[4,128,512]{2,1,0:T(8,128)}, u32[]{:S(2)}) copy-start(f32[4,128,512]{2,1,0:T(8,128)} %kappa.9) | copy-start | bytes 3145732
  5.2 7.5 %copy-start.3 = (f32[4,128,512]{2,1,0:T(8,128)S(1)}, f32[4,128,512]{2,1,0:T(8,128)}, u32[]{:S(2)}) copy-start(f32[4,128,512]{2,1,0:T(8,128)} %velocity.9) | copy-start | bytes 3145732
  5.2 7.5 %copy-start.5 = (f32[4,128,512]{2,1,0:T(8,128)S(1)}, f32[4,128,512]{2,1,0:T(8,128)}, u32[]{:S(2)}) copy-start(f32[4,128,512]{2,1,0:T(8,128)} %rate.9) | copy-start | bytes 3145732
  5.3 5.4 %collective-permute-start = (f32[16,4,512]{2,1,0:T(4,128)S(1)}, f32[16,4,512]{2,1,0:T(4,128)S(1)}, u32[]{:S(2)}, u32[]{:S(2)}) collective-permute-start(f32[16,4,512]{2,1,0:T(4,128)S(1)} %get-tuple-element.23), channel_id=1, source_target_pairs={{0,1},{1,0},{2,3},{3,2},{4,5},{5,4},{6,7},{7,6},{8,9},{9,8},{10,11... | collective-permute-start | bytes 393224 | tf_op jit(solution)/shard_map/ppermute | solution.py:337
  16.1 23.1 %collective-permute-start.3 = (f32[4,136,512]{2,1,0:T(8,128)S(1)}, f32[4,136,512]{2,1,0:T(8,128)S(1)}, u32[]{:S(2)}, u32[]{:S(2)}) collective-permute-start(f32[4,136,512]{2,1,0:T(8,128)S(1)} %get-tuple-element.33), channel_id=1, source_target_pairs={{0,2},{2,0},{4,6},{6,4},{8,10},{10,8},{12,14},{14,12},{16,18},{18,... | collective-permute-start | bytes 3342344 | tf_op jit(solution)/shard_map/ppermute | solution.py:354
  17.4 10.5 %collective-permute-start.1 = (f32[128,512]{1,0:T(8,128)S(1)}, f32[128,512]{1,0:T(8,128)S(1)}, u32[]{:S(2)}, u32[]{:S(2)}) collective-permute-start(f32[128,512]{1,0:T(8,128)S(1)} %get-tuple-element.28), channel_id=1, source_target_pairs={{2,4},{4,2},{6,8},{8,6},{10,12},{12,10},{14,16},{16,14},{18,20},{2... | collective-permute-start | bytes 786440 | tf_op jit(solution)/shard_map/ppermute | solution.py:336
  18.8 17.9 %collective-permute-start.2 = (f32[136,512]{1,0:T(8,128)S(1)}, f32[136,512]{1,0:T(8,128)S(1)}, u32[]{:S(2)}, u32[]{:S(2)}) collective-permute-start(f32[136,512]{1,0:T(8,128)S(1)} %get-tuple-element.31), channel_id=1, source_target_pairs={{2,4},{4,2},{6,8},{8,6},{10,12},{12,10},{14,16},{16,14},{18,20},{2... | collective-permute-start | bytes 835592 | tf_op jit(solution)/shard_map/ppermute | solution.py:345
  27.9 18.7 %collective-permute-start.4 = (f32[136,512]{1,0:T(8,128)S(1)}, f32[136,512]{1,0:T(8,128)S(1)}, u32[]{:S(2)}, u32[]{:S(2)}) collective-permute-start(f32[136,512]{1,0:T(8,128)S(1)} %get-tuple-element.35), channel_id=1, source_target_pairs={{2,4},{4,2},{6,8},{8,6},{10,12},{12,10},{14,16},{16,14},{18,20},{2... | collective-permute-start | bytes 835592 | tf_op jit(solution)/shard_map/ppermute | solution.py:356
  36.7 13.6 %collective-permute-start.5 = (f32[128,512]{1,0:T(8,128)S(1)}, f32[128,512]{1,0:T(8,128)S(1)}, u32[]{:S(2)}, u32[]{:S(2)}) collective-permute-start(f32[128,512]{1,0:T(8,128)S(1)} %get-tuple-element.39), channel_id=1, source_target_pairs={{2,4},{4,2},{6,8},{8,6},{10,12},{12,10},{14,16},{16,14},{18,20},{2... | collective-permute-start | bytes 786440 | tf_op jit(solution)/shard_map/ppermute | solution.py:358

commit v2 on v1

v2 whole, which is shorter than its diff:
```python
import functools

import jax
import jax.numpy as jnp
from jax import lax
from jax.experimental import pallas as pl
from jax.experimental.pallas import tpu as pltpu
from jax.sharding import PartitionSpec as P

robin_p = 0.6
own = (1.0 - robin_p / 2) / (1.0 + robin_p / 2)
far = ((1.0 - own) + robin_p * (1.0 + own) / 2) / (1.0 + robin_p / 2)

VMEM = pl.BlockSpec(memory_space=pltpu.VMEM)
ANY = pl.BlockSpec(memory_space=pl.ANY)
HBM = pl.BlockSpec(memory_space=pltpu.HBM)
HALO = 4
ROWS = 8
LANES = 128


def parity(axis):
    return lax.rem(lax.axis_index(axis), 2)


def plane_at(d, odd):
    return d + odd * (3 - 2 * d)


def pick(odd, yes, no):
    return jnp.where(jnp.broadcast_to(odd == 1, yes.shape), yes, no)


def load(ref, index, tile):
    rows = pl.ds(tile * ROWS if isinstance(tile, int) else pl.multiple_of(tile * ROWS, ROWS), ROWS)
    return [ref[*index, rows, k : k + LANES] for k in range(0, ref.shape[-1], LANES)]


def store(ref, index, tile, pieces):
    rows = pl.ds(tile * ROWS if isinstance(tile, int) else pl.multiple_of(tile * ROWS, ROWS), ROWS)
    for k, piece in enumerate(pieces):
        ref[*index, rows, k * LANES : (k + 1) * LANES] = piece


def ghost(mine, received=None):
    if received is None:
        return [m * own for m in mine]
    return [r * far + m * own for r, m in zip(received, mine)]


def updated(odd, cur, before, after, toward, away, kappa, velocity, rate):
    row = lax.broadcasted_iota(jnp.int32, (ROWS, LANES), 0)
    lane = lax.broadcasted_iota(jnp.int32, (ROWS, LANES), 1)
    zero = jnp.zeros((ROWS, LANES), jnp.float32)
    out = []
    for k, c in enumerate(cur):
        up = pltpu.roll(jnp.where(row == ROWS - 1, before[k], c), 1, 0)
        down = pltpu.roll(jnp.where(row == 0, after[k], c), ROWS - 1, 0)
        low = cur[k - 1] if k else zero
        high = cur[k + 1] if k + 1 < len(cur) else zero
        left = pltpu.roll(jnp.where(lane == LANES - 1, low, c), 1, 1)
        right = pltpu.roll(jnp.where(lane == 0, high, c), LANES - 1, 1)
        minus_x = pick(odd, away[k], toward[k]) if toward is not None else away[k]
        lap = away[k] + toward[k]
        lap = lap + up + down
        lap = lap + left + right
        lap = lap - 6.0 * c
        square = c * c
        bottom = 1.0 + square
        inverse = pl.reciprocal(bottom, approx=True)
        inverse = inverse * (2.0 - bottom * inverse)
        react = rate[k] * c * (square * inverse)
        out.append(c + kappa[k] * lap - velocity[k] * (c - minus_x) - react)
    return out


def sweep(odd, wanted, source, coefs, margins, near, distant, sink, inner, edges, unroll):
    needed = sorted({e for d in wanted for e in (d - 1, d, d + 1) if 0 <= e <= 3})
    last = source(wanted[0])[0].shape[-2] // ROWS - 1

    def body(tile):
        if isinstance(tile, int):
            before, after = (tile or last + 1) - 1, (tile + 1) % (last + 1)
        elif inner[0] > 0:
            before, after = tile - 1, tile + 1
        else:
            before, after = lax.select(tile == 0, last, tile - 1), tile + 1
        refs, at = (margins, 0) if isinstance(tile, int) and tile == last else (coefs, tile)
        state = {d: load(*source(d), tile) for d in needed}
        for d in wanted:
            cur = state[d]
            toward = state[d - 1] if d > 0 else ghost(cur, near(tile))
            away = state[d + 1] if d < 3 else ghost(cur, distant(tile))
            p = plane_at(d, odd)
            kvr = [load(ref, (*lead, p), at) for ref, lead in refs]
            sink(d, tile, updated(odd, cur, load(*source(d), before), load(*source(d), after), toward, away, *kvr))

    def loop(tile, carry):
        body(tile)
        return carry

    if inner[1] > inner[0]:
        lax.fori_loop(inner[0], inner[1], loop, 0, unroll=unroll)
    for tile in edges:
        body(tile)


def coefficients(margin, kappa, velocity, rate):
    return [(ref, ()) for ref in (kappa, velocity, rate)], [(margin, (i,)) for i in range(3)]


def none(tile):
    return None


def pack_kernel(n_halo, initial, kappa, velocity, rate, plane, *rest):
    halos, (tiles, sems) = rest[:n_halo], rest[n_halo:]
    odd_x, odd_y = parity("gx"), parity("gy")
    rows = initial.shape[1]
    copies = [pltpu.make_async_copy(initial.at[plane_at(0, odd_x)], plane, sems.at[0])]
    for f, field in enumerate((initial, kappa, velocity, rate)):
        copies.append(pltpu.make_async_copy(field.at[:, :ROWS, :], tiles.at[f, 0], sems.at[1 + 2 * f]))
        copies.append(pltpu.make_async_copy(field.at[:, rows - ROWS :, :], tiles.at[f, 1], sems.at[2 + 2 * f]))
    for copy in copies:
        copy.start()
    for copy in copies[1:]:
        copy.wait()
    for f in range(4):
        first, last = tiles[f, 0, :, :HALO], tiles[f, 1, :, ROWS - HALO :]
        halos[0][4 * f : 4 * f + 4] = pick(odd_y, first, last)
        if n_halo > 1:
            halos[1][4 * f : 4 * f + 4] = pick(odd_y, last, first)
    copies[0].wait()


def load_kernel(initial, kappa, velocity, rate, u0, u1, kappa_v, velocity_v, rate_v, sems):
    odd = parity("gx")
    planes, rows = initial.shape[:2]
    own_rows = pl.ds(0, rows)
    fields = [(initial, u0), (kappa, kappa_v), (velocity, velocity_v), (rate, rate_v)]
    copies = {}
    for d in range(planes):
        p = plane_at(d, odd)
        copies[0, d] = pltpu.make_async_copy(initial.at[p], u0.at[p, own_rows], sems.at[0, d])
    for d in range(planes):
        p = plane_at(d, odd)
        for f in range(1, 4):
            copies[f, d] = pltpu.make_async_copy(fields[f][0].at[p], fields[f][1].at[p], sems.at[f, d])
    for copy in copies.values():
        copy.start()
    for d in range(planes):
        copies[0, d].wait()

    def sink(d, tile, pieces):
        store(u1, (plane_at(d, odd),), tile, pieces)

    coefs = [(ref, ()) for ref in (kappa_v, velocity_v, rate_v)]
    tiles = rows // ROWS
    for d in range(planes):
        for f in range(1, 4):
            copies[f, d].wait()
        sweep(odd, [d], lambda e: (u0, (plane_at(e, odd),)), coefs, None, none, none, sink,
              (1, tiles - 1), (), 7 if (tiles - 2) % 7 == 0 else 1)


def first_kernel(n_halo, u0_in, u1_in, kappa, velocity, rate, *rest):
    del u0_in, u1_in
    halos, (u0, u1, margin, message) = rest[:n_halo], rest[n_halo:]
    odd, odd_y = parity("gx"), parity("gy")
    rows = kappa.shape[1]
    for f in range(4):
        one = halos[0][4 * f : 4 * f + 4]
        two = halos[1][4 * f : 4 * f + 4] if n_halo > 1 else jnp.zeros_like(one)
        edge = jnp.concatenate([pick(odd_y, two, one), pick(odd_y, one, two)], axis=1)
        if f == 0:
            u0[:, rows:, :] = edge
        else:
            margin[f - 1] = edge

    def sink(d, tile, pieces):
        store(u1, (plane_at(d, odd),), tile, pieces)

    tiles = rows // ROWS
    sweep(odd, [0, 1, 2, 3], lambda d: (u0, (plane_at(d, odd),)), *coefficients(margin, kappa, velocity, rate),
          none, none, sink, (0, 0), (0, tiles - 1, tiles), 1)
    p = plane_at(0, odd)
    message[:rows] = u1[p, :rows]
    zero = u0[p, rows:]
    one = u1[p, rows:]
    if n_halo > 1:
        message[rows : rows + ROWS] = zero
        message[rows + ROWS :] = one
    else:
        half = lax.broadcasted_iota(jnp.int32, zero.shape, 0) // HALO
        message[rows:] = jnp.where(half == odd_y, zero, pltpu.roll(one, HALO, 0))


def second_kernel(u0, u1, margin, kappa, velocity, rate, message2, message3, beside, u2):
    odd = parity("gx")
    rows = kappa.shape[1]
    coefs, margins = coefficients(margin, kappa, velocity, rate)
    tiles = rows // ROWS

    def sink2(d, tile, pieces):
        store(u2, (plane_at(d, odd),), tile, pieces)
        if d == 0:
            store(message2, (), tile, pieces)
        if d == 3:
            store(beside, (2,), tile, pieces)

    def sink3(d, tile, pieces):
        if d == 0:
            store(message3, (), tile, pieces)
        if d == 3:
            store(beside, (3,), tile, pieces)

    sweep(odd, [0, 1, 2, 3], lambda d: (u1, (plane_at(d, odd),)), coefs, margins, none, none, sink2,
          (0, tiles), (tiles,), 4)
    sweep(odd, [0, 3], lambda d: (u2, (plane_at(d, odd),)), coefs, margins, none, none, sink3, (0, tiles), (), 4)
    beside[3, rows:] = jnp.zeros(beside[3, rows:].shape, jnp.float32)
    beside[0] = u0[plane_at(3, odd)]
    beside[1] = u1[plane_at(3, odd)]


def near_kernel(n_halo, u0, u1, margin, kappa, velocity, rate, near0, near1, state, v1, edges):
    odd = parity("gx")
    rows = kappa.shape[1]
    coefs, margins = coefficients(margin, kappa, velocity, rate)
    tiles = rows // ROWS
    if n_halo > 1:
        edges[0] = near1[rows : rows + ROWS]
        edges[1] = near1[rows + ROWS :]
    else:
        edges[0] = near1[rows:]
        edges[1] = pltpu.roll(near1[rows:], HALO, 0)

    def near(step, ref):
        return lambda tile: load(edges, (step,), 0) if isinstance(tile, int) and tile == tiles else load(ref, (), tile)

    def sink1(d, tile, pieces):
        store(v1, (), tile, pieces)

    def sink2(d, tile, pieces):
        store(state, (d,), tile, pieces)

    def source1(d):
        return (v1, ()) if d == 0 else (u1, (plane_at(d, odd),))

    sweep(odd, [0], lambda d: (u0, (plane_at(d, odd),)), coefs, margins, near(0, near0), none, sink1,
          (0, tiles), (tiles,), 4)
    sweep(odd, [0, 1], source1, coefs, margins, near(1, near1), none, sink2, (0, tiles), (tiles,), 4)


def third_kernel(u0, u1, margin, kappa, velocity, rate, begun, beside, out, state, v1, v2, v3, done, sems):
    odd = parity("gx")
    rows = kappa.shape[1]
    coefs, margins = coefficients(margin, kappa, velocity, rate)
    tiles = rows // ROWS

    def distant(step):
        return lambda tile: load(beside, (step,), tile)

    def sink1(d, tile, pieces):
        store(v1, (), tile, pieces)

    def source1(d):
        return (v1, ()) if d == 3 else (u1, (plane_at(d, odd),))

    def sink2(d, tile, pieces):
        store(v2, (d - 2,), tile, pieces)

    def source2(d):
        return (begun, (d,)) if d < 2 else (v2, (d - 2,))

    def sink3(d, tile, pieces):
        if d < 3:
            store(state, (d - 1,), tile, pieces)
        else:
            store(v3, (), tile, pieces)

    def source3(d):
        return (state, (d - 1,)) if d < 3 else (v3, ())

    def sink4(d, tile, pieces):
        store(done, (d - 2,), tile, pieces)

    whole = ((0, tiles), (tiles,), 4)
    sweep(odd, [3], lambda d: (u0, (plane_at(d, odd),)), coefs, margins, none, distant(0), sink1, *whole)
    sweep(odd, [2, 3], source1, coefs, margins, none, distant(1), sink2, *whole)
    sweep(odd, [1, 2, 3], source2, coefs, margins, none, distant(2), sink3, *whole)
    sweep(odd, [2, 3], source3, coefs, margins, none, distant(3), sink4, (0, tiles), (), 4)
    copies = [pltpu.make_async_copy(done.at[d - 2], out.at[plane_at(d, odd)], sems.at[d - 2]) for d in (2, 3)]
    for copy in copies:
        copy.start()
    for copy in copies:
        copy.wait()


def fourth_kernel(begun, state, margin, kappa, velocity, rate, near2, out_in, out, base, gain, v3, done, sem):
    del out_in
    odd = parity("gx")
    rows = kappa.shape[1]
    coefs, margins = coefficients(margin, kappa, velocity, rate)
    tiles = rows // ROWS

    def sink3(d, tile, pieces):
        store(v3, (), tile, pieces)

    sweep(odd, [0], lambda d: (begun, (d,)), coefs, margins, lambda tile: load(near2, (), tile), none, sink3,
          (0, tiles), (tiles,), 4)

    def source3(d):
        return (v3, ()) if d == 0 else (state, (d - 1,))

    def sink4(d, tile, pieces):
        store(done if d else base, (), tile, pieces)

    sweep(odd, [0, 1], source3, coefs, margins, none, none, sink4, (0, tiles), (), 4)
    copy = pltpu.make_async_copy(done, out.at[plane_at(1, odd)], sem)
    copy.start()
    p = plane_at(0, odd)

    def gains(tile, carry):
        both = zip(load(kappa, (p,), tile), load(velocity, (p,), tile))
        store(gain, (), tile, [far * (k + pick(odd, jnp.zeros_like(v), v)) for k, v in both])
        return carry

    lax.fori_loop(0, tiles, gains, 0)
    copy.wait()


def last_kernel(base, gain, near3, out_in, out, done, sem):
    del out_in
    odd = parity("gx")
    done[...] = base[...] + gain[...] * near3[...]
    copy = pltpu.make_async_copy(done, out.at[plane_at(0, odd)], sem)
    copy.start()
    copy.wait()


def pairs(count, first, wrap):
    out = []
    for i in range(first, count, 2):
        if i + 1 < count or wrap:
            out += [(i, (i + 1) % count), ((i + 1) % count, i)]
    return out


def f32(*shape):
    return jax.ShapeDtypeStruct(shape, jnp.float32)


def call(kernel, out_shape, in_specs, out_specs, scratch=(), aliases=None, weight=0, limit=12):
    return pl.pallas_call(
        kernel,
        out_shape=out_shape,
        in_specs=in_specs,
        out_specs=out_specs,
        scratch_shapes=scratch,
        input_output_aliases=aliases or {},
        cost_estimate=pl.CostEstimate(flops=int(weight * 1e9), bytes_accessed=int(weight * 3.0e6), transcendentals=0),
        compiler_params=pltpu.CompilerParams(vmem_limit_bytes=limit * 1024 * 1024),
    )


def local(initial, kappa, velocity, rate):
    planes, rows, lanes = initial.shape
    full = rows + ROWS
    count_y = lax.axis_size("gy")
    count_x = lax.axis_size("gx")
    n_halo = 1 if count_y == 2 else 2
    chips = pairs(count_x, 1, True)
    cores = pairs(count_x, 0, False)
    rows_pairs = [pairs(count_y, 0, False), pairs(count_y, 1, False)][:n_halo]
    block, wide = f32(planes, rows, lanes), f32(planes, full, lanes)
    wide_plane = pltpu.VMEM((full, lanes), jnp.float32)

    plane0, *halos = call(
        functools.partial(pack_kernel, n_halo),
        [f32(rows, lanes)] + [f32(16, HALO, lanes)] * n_halo,
        [HBM] * 4,
        [ANY] + [VMEM] * n_halo,
        [pltpu.VMEM((4, 2, planes, ROWS, lanes), jnp.float32), pltpu.SemaphoreType.DMA((9,))],
        weight=1,
    )(*[pltpu.with_memory_space_constraint(x, pltpu.HBM) for x in (initial, kappa, velocity, rate)])
    near0 = lax.ppermute(plane0, "gx", chips)
    halos = [lax.ppermute(halo, "gy", which) for halo, which in zip(halos, rows_pairs)]
    u0, u1, *coefs = call(
        load_kernel,
        [wide, wide, block, block, block],
        [HBM] * 4,
        [VMEM] * 5,
        [pltpu.SemaphoreType.DMA((4, planes))],
        weight=20,
    )(*[pltpu.with_memory_space_constraint(x, pltpu.HBM) for x in (initial, kappa, velocity, rate)])
    u0, u1, margin, message1 = call(
        functools.partial(first_kernel, n_halo),
        [wide, wide, f32(3, planes, ROWS, lanes), f32(rows + ROWS * n_halo, lanes)],
        [VMEM] * (5 + n_halo),
        [VMEM] * 4,
        aliases={0: 0, 1: 1},
        weight=1,
    )(u0, u1, *coefs, *halos)
    near1 = lax.ppermute(message1, "gx", chips)
    u1, near0 = lax.optimization_barrier((u1, near0))
    message2, message3, beside = call(
        second_kernel,
        [f32(full, lanes), f32(rows, lanes), f32(4, full, lanes)],
        [VMEM] * 6,
        [VMEM] * 3,
        [pltpu.VMEM((planes, full, lanes), jnp.float32)],
        weight=20,
    )(u0, u1, margin, *coefs)
    near2 = lax.ppermute(message2, "gx", chips)
    beside = lax.ppermute(beside, "gx", cores)
    message3, near1 = lax.optimization_barrier((message3, near1))
    near3 = lax.ppermute(message3, "gx", chips)
    begun = call(
        functools.partial(near_kernel, n_halo),
        f32(2, full, lanes),
        [VMEM] * 8,
        VMEM,
        [wide_plane, pltpu.VMEM((2, ROWS, lanes), jnp.float32)],
        weight=20,
    )(u0, u1, margin, *coefs, near0, near1)
    out, state = call(
        third_kernel,
        [block, f32(2, full, lanes)],
        [VMEM] * 8,
        [ANY, VMEM],
        [wide_plane, pltpu.VMEM((2, full, lanes), jnp.float32), wide_plane,
         pltpu.VMEM((2, rows, lanes), jnp.float32), pltpu.SemaphoreType.DMA((2,))],
        weight=20,
    )(u0, u1, margin, *coefs, begun, beside)
    out, base, gain = call(
        fourth_kernel,
        [block, f32(rows, lanes), f32(rows, lanes)],
        [VMEM] * 7 + [ANY],
        [ANY, VMEM, VMEM],
        [wide_plane, pltpu.VMEM((rows, lanes), jnp.float32), pltpu.SemaphoreType.DMA],
        {7: 0},
        weight=20,
    )(begun, state, margin, *coefs, near2, out)
    return call(
        last_kernel,
        block,
        [VMEM] * 3 + [ANY],
        ANY,
        [pltpu.VMEM((rows, lanes), jnp.float32), pltpu.SemaphoreType.DMA],
        {3: 0},
        weight=1,
    )(base, gain, near3, out)


def solution(mesh):
    placed = P("gx", "gy", None)
    return jax.shard_map(local, mesh=mesh, in_specs=(placed,) * 4, out_specs=placed, check_vma=False)
```

time: 51.3 us -> 33.3 us (0.65)
  local copies, waits for them, and re-layouts: 4.92 us -> 0 us
  waiting for transfers between devices: 12.5 us -> 7.71 us
  Pallas kernels: 17.6 us -> 13.4 us
  starting transfers between devices: 15.9 us -> 12 us
    ppermute x1, starting transfers between devices: 8.26 us -> 1.67 us  [local(): near2 = lax.ppermute(message2, 'gx', chips)]
    ppermute x1, waiting for transfers between devices: 8.77 us -> 2.94 us  [local(): near0 = lax.ppermute(plane0, 'gx', chips)]
    unnamed x14 -> x0, local copies, waits for them, and re-layouts: 4.92 us -> none
    ppermute x1, waiting for transfers between devices: 0.5 us -> 4.76 us  [local(): near1 = lax.ppermute(message1, 'gx', chips)]
    pallas_call x4 -> x6, Pallas kernels: 13.9 us -> 10.3 us  [the longest x1 3.56 us: local(): call(third_kernel, [block, f32(2, full, lanes)], [VMEM] * 8, [ANY, VMEM],...]
    ppermute x1, waiting for transfers between devices: 3.22 us -> 0.01 us  [local(): lax.ppermute(halo, 'gy', which)]
    pallas_call x1, Pallas kernels: 3.4 us -> 1.86 us  [local(): call(second_kernel, [f32(full, lanes), f32(rows, lanes), f32(4, full, lan...]
    ppermute x1, starting transfers between devices: 1.29 us -> 2.59 us  [local(): beside = lax.ppermute(beside, 'gx', cores)]
  transfers between devices with their start and end apart: 6 -> 6, of which waited for: 3 -> 2; matrix products, arithmetic and copies ran while one was open for 0% -> 0% of each run, Pallas kernels for 22% -> 34%
where the time goes in v2:
time: 33.3 us; the launch traced here: 33.2 us
  Pallas kernels  13.4 us (40%)
  starting transfers between devices  12 us (36%)
  waiting for transfers between devices  7.71 us (23%)
    ppermute x1, waiting for transfers between devices, local(): near1 = lax.ppermute(message1, 'gx', chips)  4.76 us
    pallas_call x1, Pallas kernels, local(): call(third_kernel, [block, f32(2, full, lanes)], [VMEM] * 8, [ANY, VMEM],...  3.56 us
    ppermute x1, waiting for transfers between devices, local(): near0 = lax.ppermute(plane0, 'gx', chips)  2.94 us
    pallas_call x1, Pallas kernels, local(): call(load_kernel, [wide, wide, block, block, block], [HBM] * 4, [VMEM] *...  2.7 us
    ppermute x1, starting transfers between devices, local(): beside = lax.ppermute(beside, 'gx', cores)  2.59 us
    ppermute x1, starting transfers between devices, local(): near3 = lax.ppermute(message3, 'gx', chips)  2.48 us
    ppermute x1, starting transfers between devices, local(): lax.ppermute(halo, 'gy', which)  2.13 us
    ppermute x1, starting transfers between devices, local(): near0 = lax.ppermute(plane0, 'gx', chips)  2.05 us
  transfers between devices with their start and end apart: 6, of which 2 were waited for; matrix products, arithmetic and copies ran while one was open for 0% of the time, Pallas kernels for 34%

profile of v2, /device:TPU:1, one launch (start us, length us, event | category | flops | bytes accessed | tf_op | source)
XLA Modules:
  0.0 33.2 jit_solution(16351235207149275473)
XLA Ops:
  0.0 1.2 %shard_map.47 = (f32[128,512]{1,0:T(8,128)S(1)}, f32[16,4,512]{2,1,0:T(4,128)S(1)}) custom-call(f32[4,128,512]{2,1,0:T(8,128)} %initial.3, f32[4,128,512]{2,1,0:T(8,128)} %kappa.3, f32[4,128,512]{2,1,0:T(8,128)} %velocity.3, f32[4,128,512]{2,1,0:T(8,128)} %rate.3), custom_call_target="tpu_custom_call" | custom-call | flops 1000000000 | bytes 3000000 | tf_op jit(solution)/shard_map/pallas_call | solution.py:378
  1.2 2.1 %collective-permute-start = (f32[16,4,512]{2,1,0:T(4,128)S(1)}, f32[16,4,512]{2,1,0:T(4,128)S(1)}, u32[]{:S(2)}, u32[]{:S(2)}) collective-permute-start(f32[16,4,512]{2,1,0:T(4,128)S(1)} %get-tuple-element.33), channel_id=1, source_target_pairs={{0,1},{1,0},{2,3},{3,2},{4,5},{5,4},{6,7},{7,6},{8,9},{9,8},{10,11... | collective-permute-start | bytes 393224 | tf_op jit(solution)/shard_map/ppermute | solution.py:387
  3.4 2.1 %collective-permute-start.1 = (f32[128,512]{1,0:T(8,128)S(1)}, f32[128,512]{1,0:T(8,128)S(1)}, u32[]{:S(2)}, u32[]{:S(2)}) collective-permute-start(f32[128,512]{1,0:T(8,128)S(1)} %get-tuple-element.36), channel_id=1, source_target_pairs={{2,4},{4,2},{6,8},{8,6},{10,12},{12,10},{14,16},{16,14},{18,20},{2... | collective-permute-start | bytes 786440 | tf_op jit(solution)/shard_map/ppermute | solution.py:386
  5.4 2.7 %shard_map.46 = (f32[4,136,512]{2,1,0:T(8,128)S(1)}, f32[4,136,512]{2,1,0:T(8,128)S(1)}, f32[4,128,512]{2,1,0:T(8,128)S(1)}, f32[4,128,512]{2,1,0:T(8,128)S(1)}, f32[4,128,512]{2,1,0:T(8,128)S(1)}) custom-call(f32[4,128,512]{2,1,0:T(8,128)} %initial.3, f32[4,128,512]{2,1,0:T(8,128)} %kappa.3, f32[4,128,512]{2,1,0:T(8,128)} %velocity.3, f32[4,128,512]{2,1,0:T(8,128)} %rate.3), custom_call_target="tpu_custom_call" | custom-call | flops 20000000000 | bytes 60000000 | tf_op jit(solution)/shard_map/pallas_call | solution.py:388
  8.1 0.0 collective-permute-done.rest_0_
  8.1 0.3 shard_map.48
  8.4 1.0 %collective-permute-start.2 = (f32[136,512]{1,0:T(8,128)S(1)}, f32[136,512]{1,0:T(8,128)S(1)}, u32[]{:S(2)}, u32[]{:S(2)}) collective-permute-start(f32[136,512]{1,0:T(8,128)S(1)} %get-tuple-element.41), channel_id=1, source_target_pairs={{2,4},{4,2},{6,8},{8,6},{10,12},{12,10},{14,16},{16,14},{18,20},{2... | collective-permute-start | bytes 835592 | tf_op jit(solution)/shard_map/ppermute | solution.py:404
  9.5 2.9 %collective-permute-done.1.near0 = f32[128,512]{1,0:T(8,128)S(1)} collective-permute-done((f32[128,512]{1,0:T(8,128)S(1)}, f32[128,512]{1,0:T(8,128)S(1)}, u32[]{:S(2)}, u32[]{:S(2)}) %collective-permute-start.1) | collective-permute-done | bytes 262176 | tf_op jit(solution)/shard_map/ppermute | solution.py:386
  12.4 1.9 %shard_map.49 = (f32[136,512]{1,0:T(8,128)S(1)}, f32[128,512]{1,0:T(8,128)S(1)}, f32[4,136,512]{2,1,0:T(8,128)S(1)}) custom-call(f32[4,136,512]{2,1,0:T(8,128)S(1)} %get-tuple-element.34.u0, f32[4,136,512]{2,1,0:T(8,128)S(1)} %get-tuple-element.37.u1, f32[3,4,8,512]{3,2,1,0:T(8,128)S(1)} %get-tuple-element.38.margin, ...), custom_call_target="tpu_custom_call" | custom-call | flops 20000000000 | bytes 60000000 | tf_op jit(solution)/shard_map/pallas_call | solution.py:406
  14.3 1.7 %collective-permute-start.4 = (f32[136,512]{1,0:T(8,128)S(1)}, f32[136,512]{1,0:T(8,128)S(1)}, u32[]{:S(2)}, u32[]{:S(2)}) collective-permute-start(f32[136,512]{1,0:T(8,128)S(1)} %get-tuple-element.45), channel_id=1, source_target_pairs={{2,4},{4,2},{6,8},{8,6},{10,12},{12,10},{14,16},{16,14},{18,20},{2... | collective-permute-start | bytes 835592 | tf_op jit(solution)/shard_map/ppermute | solution.py:414
  16.0 2.6 %collective-permute-start.3 = (f32[4,136,512]{2,1,0:T(8,128)S(1)}, f32[4,136,512]{2,1,0:T(8,128)S(1)}, u32[]{:S(2)}, u32[]{:S(2)}) collective-permute-start(f32[4,136,512]{2,1,0:T(8,128)S(1)} %get-tuple-element.43), channel_id=1, source_target_pairs={{0,2},{2,0},{4,6},{6,4},{8,10},{10,8},{12,14},{14,12},{16,18},{18,... | collective-permute-start | bytes 3342344 | tf_op jit(solution)/shard_map/ppermute | solution.py:415
  18.5 4.8 %collective-permute-done.2.near1 = f32[136,512]{1,0:T(8,128)S(1)} collective-permute-done((f32[136,512]{1,0:T(8,128)S(1)}, f32[136,512]{1,0:T(8,128)S(1)}, u32[]{:S(2)}, u32[]{:S(2)}) %collective-permute-start.2) | collective-permute-done | bytes 278560 | tf_op jit(solution)/shard_map/ppermute | solution.py:404
  23.3 2.5 %collective-permute-start.5 = (f32[128,512]{1,0:T(8,128)S(1)}, f32[128,512]{1,0:T(8,128)S(1)}, u32[]{:S(2)}, u32[]{:S(2)}) collective-permute-start(f32[128,512]{1,0:T(8,128)S(1)} %get-tuple-element.49), channel_id=1, source_target_pairs={{2,4},{4,2},{6,8},{8,6},{10,12},{12,10},{14,16},{16,14},{18,20},{2... | collective-permute-start | bytes 786440 | tf_op jit(solution)/shard_map/ppermute | solution.py:417
  25.8 1.2 %shard_map.50.begun = f32[2,136,512]{2,1,0:T(8,128)S(1)} custom-call(f32[4,136,512]{2,1,0:T(8,128)S(1)} %get-tuple-element.34.u0, f32[4,136,512]{2,1,0:T(8,128)S(1)} %get-tuple-element.37.u1, f32[3,4,8,512]{3,2,1,0:T(8,128)S(1)} %get-tuple-element.38.margin, f32[4,128,512]{2,1,0:T(8,128)S(1)} %get-tuple-element.30.kappa, ...), custom_call_target="tpu_custom_call" | custom-call | flops 20000000000 | bytes 60000000 | tf_op jit(solution)/shard_map/pallas_call | solution.py:418
  27.0 0.0 collective-permute-done.3.beside
  27.0 3.6 %shard_map.51 = (f32[4,128,512]{2,1,0:T(8,128)}, f32[2,136,512]{2,1,0:T(8,128)S(1)}) custom-call(f32[4,136,512]{2,1,0:T(8,128)S(1)} %get-tuple-element.34.u0, f32[4,136,512]{2,1,0:T(8,128)S(1)} %get-tuple-element.37.u1, f32[3,4,8,512]{3,2,1,0:T(8,128)S(1)} %get-tuple-element.38.margin, f32[4,128,512]{2,1,0:T(8,128)S(1)} %get-tuple-element.30.kappa, ...), custom_call_target="tpu_custom_call" | custom-call | flops 20000000000 | bytes 60000000 | tf_op jit(solution)/shard_map/pallas_call | solution.py:426
  30.6 0.0 collective-permute-done.4.near2
  30.6 1.8 %shard_map.52 = (f32[4,128,512]{2,1,0:T(8,128)}, f32[128,512]{1,0:T(8,128)S(1)}, f32[128,512]{1,0:T(8,128)S(1)}) custom-call(f32[2,136,512]{2,1,0:T(8,128)S(1)} %shard_map.50.begun, f32[2,136,512]{2,1,0:T(8,128)S(1)} %get-tuple-element.44.state, f32[3,4,8,512]{3,2,1,0:T(8,128)S(1)} %get-tuple-element.38.margin, ...), custom_call_target="tpu_custom_call", output_to_operand_aliasing={{0}: (7, {})} | custom-call | flops 20000000000 | bytes 60000000 | tf_op jit(solution)/shard_map/pallas_call | solution.py:435
  32.4 0.0 collective-permute-done.5.near3
  32.4 0.8 %shard_map.53 = f32[4,128,512]{2,1,0:T(8,128)} custom-call(f32[128,512]{1,0:T(8,128)S(1)} %get-tuple-element.47.base, f32[128,512]{1,0:T(8,128)S(1)} %get-tuple-element.48.gain, f32[128,512]{1,0:T(8,128)S(1)} %collective-permute-done.5.near3, f32[4,128,512]{2,1,0:T(8,128)} %get-tuple-element.50.out_in), custom_call_target="tpu_custom_call", output_to_operand_aliasing={{}: (3, {})} | custom-call | flops 1000000000 | bytes 3000000 | tf_op jit(solution)/shard_map/pallas_call | solution.py:444
Async XLA Ops:
  1.2 6.9 %collective-permute-start = (f32[16,4,512]{2,1,0:T(4,128)S(1)}, f32[16,4,512]{2,1,0:T(4,128)S(1)}, u32[]{:S(2)}, u32[]{:S(2)}) collective-permute-start(f32[16,4,512]{2,1,0:T(4,128)S(1)} %get-tuple-element.33), channel_id=1, source_target_pairs={{0,1},{1,0},{2,3},{3,2},{4,5},{5,4},{6,7},{7,6},{8,9},{9,8},{10,11... | collective-permute-start | bytes 393224 | tf_op jit(solution)/shard_map/ppermute | solution.py:387
  3.4 9.1 %collective-permute-start.1 = (f32[128,512]{1,0:T(8,128)S(1)}, f32[128,512]{1,0:T(8,128)S(1)}, u32[]{:S(2)}, u32[]{:S(2)}) collective-permute-start(f32[128,512]{1,0:T(8,128)S(1)} %get-tuple-element.36), channel_id=1, source_target_pairs={{2,4},{4,2},{6,8},{8,6},{10,12},{12,10},{14,16},{16,14},{18,20},{2... | collective-permute-start | bytes 786440 | tf_op jit(solution)/shard_map/ppermute | solution.py:386
  8.4 14.9 %collective-permute-start.2 = (f32[136,512]{1,0:T(8,128)S(1)}, f32[136,512]{1,0:T(8,128)S(1)}, u32[]{:S(2)}, u32[]{:S(2)}) collective-permute-start(f32[136,512]{1,0:T(8,128)S(1)} %get-tuple-element.41), channel_id=1, source_target_pairs={{2,4},{4,2},{6,8},{8,6},{10,12},{12,10},{14,16},{16,14},{18,20},{2... | collective-permute-start | bytes 835592 | tf_op jit(solution)/shard_map/ppermute | solution.py:404
  14.3 16.3 %collective-permute-start.4 = (f32[136,512]{1,0:T(8,128)S(1)}, f32[136,512]{1,0:T(8,128)S(1)}, u32[]{:S(2)}, u32[]{:S(2)}) collective-permute-start(f32[136,512]{1,0:T(8,128)S(1)} %get-tuple-element.45), channel_id=1, source_target_pairs={{2,4},{4,2},{6,8},{8,6},{10,12},{12,10},{14,16},{16,14},{18,20},{2... | collective-permute-start | bytes 835592 | tf_op jit(solution)/shard_map/ppermute | solution.py:414
  16.0 11.0 %collective-permute-start.3 = (f32[4,136,512]{2,1,0:T(8,128)S(1)}, f32[4,136,512]{2,1,0:T(8,128)S(1)}, u32[]{:S(2)}, u32[]{:S(2)}) collective-permute-start(f32[4,136,512]{2,1,0:T(8,128)S(1)} %get-tuple-element.43), channel_id=1, source_target_pairs={{0,2},{2,0},{4,6},{6,4},{8,10},{10,8},{12,14},{14,12},{16,18},{18,... | collective-permute-start | bytes 3342344 | tf_op jit(solution)/shard_map/ppermute | solution.py:415
  23.3 9.1 %collective-permute-start.5 = (f32[128,512]{1,0:T(8,128)S(1)}, f32[128,512]{1,0:T(8,128)S(1)}, u32[]{:S(2)}, u32[]{:S(2)}) collective-permute-start(f32[128,512]{1,0:T(8,128)S(1)} %get-tuple-element.49), channel_id=1, source_target_pairs={{2,4},{4,2},{6,8},{8,6},{10,12},{12,10},{14,16},{16,14},{18,20},{2... | collective-permute-start | bytes 786440 | tf_op jit(solution)/shard_map/ppermute | solution.py:417

commit v3 on v2

--- a/solution.py
+++ b/solution.py
@@ -15,8 +15,10 @@
 ANY = pl.BlockSpec(memory_space=pl.ANY)
 HBM = pl.BlockSpec(memory_space=pltpu.HBM)
 HALO = 4
+WEIGHTS = (1, 20, 1, 60, 20, 1, 1, 1, 1)
 ROWS = 8
 LANES = 128
+UNROLL = 4
 
 
 def parity(axis):
@@ -121,11 +123,11 @@
     for f, field in enumerate((initial, kappa, velocity, rate)):
         copies.append(pltpu.make_async_copy(field.at[:, :ROWS, :], tiles.at[f, 0], sems.at[1 + 2 * f]))
         copies.append(pltpu.make_async_copy(field.at[:, rows - ROWS :, :], tiles.at[f, 1], sems.at[2 + 2 * f]))
-    for copy in copies:
+    for copy in copies[1:] + copies[:1]:
         copy.start()
-    for copy in copies[1:]:
-        copy.wait()
     for f in range(4):
+        copies[1 + 2 * f].wait()
+        copies[2 + 2 * f].wait()
         first, last = tiles[f, 0, :, :HALO], tiles[f, 1, :, ROWS - HALO :]
         halos[0][4 * f : 4 * f + 4] = pick(odd_y, first, last)
         if n_halo > 1:
@@ -137,15 +139,15 @@
     odd = parity("gx")
     planes, rows = initial.shape[:2]
     own_rows = pl.ds(0, rows)
-    fields = [(initial, u0), (kappa, kappa_v), (velocity, velocity_v), (rate, rate_v)]
+    fields = [(kappa, kappa_v), (velocity, velocity_v), (rate, rate_v)]
     copies = {}
     for d in range(planes):
         p = plane_at(d, odd)
         copies[0, d] = pltpu.make_async_copy(initial.at[p], u0.at[p, own_rows], sems.at[0, d])
     for d in range(planes):
         p = plane_at(d, odd)
-        for f in range(1, 4):
-            copies[f, d] = pltpu.make_async_copy(fields[f][0].at[p], fields[f][1].at[p], sems.at[f, d])
+        for f, (field, held) in enumerate(fields):
+            copies[f + 1, d] = pltpu.make_async_copy(field.at[p], held.at[p], sems.at[f + 1, d])
     for copy in copies.values():
         copy.start()
     for d in range(planes):
@@ -160,7 +162,7 @@
         for f in range(1, 4):
             copies[f, d].wait()
         sweep(odd, [d], lambda e: (u0, (plane_at(e, odd),)), coefs, None, none, none, sink,
-              (1, tiles - 1), (), 7 if (tiles - 2) % 7 == 0 else 1)
+              (1, tiles - 1), (), 7 if tiles % 7 == 2 else 1)
 
 
 def first_kernel(n_halo, u0_in, u1_in, kappa, velocity, rate, *rest):
@@ -215,14 +217,66 @@
             store(beside, (3,), tile, pieces)
 
     sweep(odd, [0, 1, 2, 3], lambda d: (u1, (plane_at(d, odd),)), coefs, margins, none, none, sink2,
-          (0, tiles), (tiles,), 4)
-    sweep(odd, [0, 3], lambda d: (u2, (plane_at(d, odd),)), coefs, margins, none, none, sink3, (0, tiles), (), 4)
+          (0, tiles), (tiles,), UNROLL)
+    sweep(odd, [0, 3], lambda d: (u2, (plane_at(d, odd),)), coefs, margins, none, none, sink3, (0, tiles), (), UNROLL)
     beside[3, rows:] = jnp.zeros(beside[3, rows:].shape, jnp.float32)
     beside[0] = u0[plane_at(3, odd)]
     beside[1] = u1[plane_at(3, odd)]
 
 
-def near_kernel(n_halo, u0, u1, margin, kappa, velocity, rate, near0, near1, state, v1, edges):
+def gain_kernel(kappa, velocity, gain):
+    odd = parity("gx")
+    p = plane_at(0, odd)
+
+    def body(tile, carry):
+        both = zip(load(kappa, (p,), tile), load(velocity, (p,), tile))
+        store(gain, (), tile, [far * (k + pick(odd, jnp.zeros_like(v), v)) for k, v in both])
+        return carry
+
+    lax.fori_loop(0, kappa.shape[1] // ROWS, body, 0, unroll=UNROLL)
+
+
+STATE = {(2, 2): 0, (2, 3): 1, (3, 3): 2}
+MORE = {(2, 0): 0, (2, 1): 1, (3, 1): 2, (3, 2): 3}
+
+
+def stages(odd, u0, u1, state, more, others):
+    def at(step, d):
+        if (step, d) in others:
+            return others[step, d]
+        if (step, d) in STATE:
+            return state, (STATE[step, d],)
+        if (step, d) in MORE:
+            return more, (MORE[step, d],)
+        return (u0, u1)[step], (plane_at(d, odd),)
+
+    def sink(step):
+        def put(d, tile, pieces):
+            ref, index = at(step, d)
+            store(ref, index, tile, pieces)
+
+        return put
+
+    return lambda step: functools.partial(at, step), sink
+
+
+def far_kernel(u0, u1, margin, kappa, velocity, rate, beside, state, v1):
+    odd = parity("gx")
+    tiles = kappa.shape[1] // ROWS
+    coefs, margins = coefficients(margin, kappa, velocity, rate)
+    source, sink = stages(odd, u0, u1, state, None, {(1, 3): (v1, ())})
+    whole = ((0, tiles), (tiles,), UNROLL)
+
+    def distant(step):
+        return lambda tile: load(beside, (step,), tile)
+
+    sweep(odd, [3], source(0), coefs, margins, none, distant(0), sink(1), *whole)
+    sweep(odd, [2, 3], source(1), coefs, margins, none, distant(1), sink(2), *whole)
+    sweep(odd, [3], source(2), coefs, margins, none, distant(2), sink(3), *whole)
+
+
+def near_kernel(n_halo, u0, u1, margin, kappa, velocity, rate, near0, near1, beside, state, out, more, almost,
+                v1, edges, done, sem):
     odd = parity("gx")
     rows = kappa.shape[1]
     coefs, margins = coefficients(margin, kappa, velocity, rate)
@@ -233,109 +287,61 @@
     else:
         edges[0] = near1[rows:]
         edges[1] = pltpu.roll(near1[rows:], HALO, 0)
+    source, sink = stages(odd, u0, u1, state, more, {(1, 0): (v1, ())})
+    whole = ((0, tiles), (tiles,), UNROLL)
 
     def near(step, ref):
         return lambda tile: load(edges, (step,), 0) if isinstance(tile, int) and tile == tiles else load(ref, (), tile)
 
-    def sink1(d, tile, pieces):
-        store(v1, (), tile, pieces)
-
-    def sink2(d, tile, pieces):
-        store(state, (d,), tile, pieces)
-
-    def source1(d):
-        return (v1, ()) if d == 0 else (u1, (plane_at(d, odd),))
-
-    sweep(odd, [0], lambda d: (u0, (plane_at(d, odd),)), coefs, margins, near(0, near0), none, sink1,
-          (0, tiles), (tiles,), 4)
-    sweep(odd, [0, 1], source1, coefs, margins, near(1, near1), none, sink2, (0, tiles), (tiles,), 4)
-
-
-def third_kernel(u0, u1, margin, kappa, velocity, rate, begun, beside, out, state, v1, v2, v3, done, sems):
-    odd = parity("gx")
-    rows = kappa.shape[1]
+    def distant(tile):
+        return load(beside, (3,), tile)
+
+    def finish(d, tile, pieces):
+        store(done if d == 3 else almost, (), tile, pieces)
+
+    sweep(odd, [0], source(0), coefs, margins, near(0, near0), none, sink(1), *whole)
+    sweep(odd, [0, 1], source(1), coefs, margins, near(1, near1), none, sink(2), *whole)
+    sweep(odd, [1, 2], source(2), coefs, margins, none, none, sink(3), *whole)
+    sweep(odd, [2, 3], source(3), coefs, margins, none, distant, finish, (0, tiles), (), UNROLL)
+    copy = pltpu.make_async_copy(done, out.at[plane_at(3, odd)], sem)
+    copy.start()
+    copy.wait()
+
+
+def fourth_kernel(more, almost, margin, kappa, velocity, rate, near2, out_in, out, base, v3, done, sems):
+    del out_in
+    odd = parity("gx")
+    tiles = kappa.shape[1] // ROWS
     coefs, margins = coefficients(margin, kappa, velocity, rate)
-    tiles = rows // ROWS
-
-    def distant(step):
-        return lambda tile: load(beside, (step,), tile)
-
-    def sink1(d, tile, pieces):
-        store(v1, (), tile, pieces)
-
-    def source1(d):
-        return (v1, ()) if d == 3 else (u1, (plane_at(d, odd),))
-
-    def sink2(d, tile, pieces):
-        store(v2, (d - 2,), tile, pieces)
-
-    def source2(d):
-        return (begun, (d,)) if d < 2 else (v2, (d - 2,))
-
-    def sink3(d, tile, pieces):
-        if d < 3:
-            store(state, (d - 1,), tile, pieces)
-        else:
-            store(v3, (), tile, pieces)
-
-    def source3(d):
-        return (state, (d - 1,)) if d < 3 else (v3, ())
-
-    def sink4(d, tile, pieces):
-        store(done, (d - 2,), tile, pieces)
-
-    whole = ((0, tiles), (tiles,), 4)
-    sweep(odd, [3], lambda d: (u0, (plane_at(d, odd),)), coefs, margins, none, distant(0), sink1, *whole)
-    sweep(odd, [2, 3], source1, coefs, margins, none, distant(1), sink2, *whole)
-    sweep(odd, [1, 2, 3], source2, coefs, margins, none, distant(2), sink3, *whole)
-    sweep(odd, [2, 3], source3, coefs, margins, none, distant(3), sink4, (0, tiles), (), 4)
-    copies = [pltpu.make_async_copy(done.at[d - 2], out.at[plane_at(d, odd)], sems.at[d - 2]) for d in (2, 3)]
-    for copy in copies:
-        copy.start()
+    copies = [pltpu.make_async_copy(almost, out.at[plane_at(2, odd)], sems.at[0]),
+              pltpu.make_async_copy(done, out.at[plane_at(1, odd)], sems.at[1])]
+    copies[0].start()
+    source, sink = stages(odd, None, None, None, more, {(3, 0): (v3, ())})
+
+    def finish(d, tile, pieces):
+        store(done if d else base, (), tile, pieces)
+
+    sweep(odd, [0], source(2), coefs, margins, lambda tile: load(near2, (), tile), none, sink(3),
+          (0, tiles), (tiles,), UNROLL)
+    sweep(odd, [0, 1], source(3), coefs, margins, none, none, finish, (0, tiles), (), UNROLL)
+    copies[1].start()
     for copy in copies:
         copy.wait()
 
 
-def fourth_kernel(begun, state, margin, kappa, velocity, rate, near2, out_in, out, base, gain, v3, done, sem):
+def last_kernel(base, gain, near3, out_in, out, done, sems):
     del out_in
     odd = parity("gx")
-    rows = kappa.shape[1]
-    coefs, margins = coefficients(margin, kappa, velocity, rate)
-    tiles = rows // ROWS
-
-    def sink3(d, tile, pieces):
-        store(v3, (), tile, pieces)
-
-    sweep(odd, [0], lambda d: (begun, (d,)), coefs, margins, lambda tile: load(near2, (), tile), none, sink3,
-          (0, tiles), (tiles,), 4)
-
-    def source3(d):
-        return (v3, ()) if d == 0 else (state, (d - 1,))
-
-    def sink4(d, tile, pieces):
-        store(done if d else base, (), tile, pieces)
-
-    sweep(odd, [0, 1], source3, coefs, margins, none, none, sink4, (0, tiles), (), 4)
-    copy = pltpu.make_async_copy(done, out.at[plane_at(1, odd)], sem)
-    copy.start()
-    p = plane_at(0, odd)
-
-    def gains(tile, carry):
-        both = zip(load(kappa, (p,), tile), load(velocity, (p,), tile))
-        store(gain, (), tile, [far * (k + pick(odd, jnp.zeros_like(v), v)) for k, v in both])
-        return carry
-
-    lax.fori_loop(0, tiles, gains, 0)
-    copy.wait()
-
-
-def last_kernel(base, gain, near3, out_in, out, done, sem):
-    del out_in
-    odd = parity("gx")
-    done[...] = base[...] + gain[...] * near3[...]
-    copy = pltpu.make_async_copy(done, out.at[plane_at(0, odd)], sem)
-    copy.start()
-    copy.wait()
+    rows = base.shape[0]
+    part = rows // 4
+    copies = []
+    for i in range(4):
+        span = pl.ds(i * part, part)
+        done[span] = base[span] + gain[span] * near3[span]
+        copies.append(pltpu.make_async_copy(done.at[span], out.at[plane_at(0, odd), span], sems.at[i]))
+        copies[-1].start()
+    for copy in copies:
+        copy.wait()
 
 
 def pairs(count, first, wrap):
@@ -372,18 +378,21 @@
     chips = pairs(count_x, 1, True)
     cores = pairs(count_x, 0, False)
     rows_pairs = [pairs(count_y, 0, False), pairs(count_y, 1, False)][:n_halo]
-    block, wide = f32(planes, rows, lanes), f32(planes, full, lanes)
-    wide_plane = pltpu.VMEM((full, lanes), jnp.float32)
-
-    plane0, *halos = call(
+    block, wide, plane, wide_plane = f32(planes, rows, lanes), f32(planes, full, lanes), f32(rows, lanes), f32(full, lanes)
+
+    def scratch(*shape):
+        return pltpu.VMEM(shape, jnp.float32)
+
+    fields = [pltpu.with_memory_space_constraint(x, pltpu.HBM) for x in (initial, kappa, velocity, rate)]
+    message0, *halos = call(
         functools.partial(pack_kernel, n_halo),
-        [f32(rows, lanes)] + [f32(16, HALO, lanes)] * n_halo,
+        [plane] + [f32(16, HALO, lanes)] * n_halo,
         [HBM] * 4,
         [ANY] + [VMEM] * n_halo,
-        [pltpu.VMEM((4, 2, planes, ROWS, lanes), jnp.float32), pltpu.SemaphoreType.DMA((9,))],
-        weight=1,
-    )(*[pltpu.with_memory_space_constraint(x, pltpu.HBM) for x in (initial, kappa, velocity, rate)])
-    near0 = lax.ppermute(plane0, "gx", chips)
+        [scratch(4, 2, planes, ROWS, lanes), pltpu.SemaphoreType.DMA((9,))],
+        weight=WEIGHTS[0],
+    )(*fields)
+    near0 = lax.ppermute(message0, "gx", chips)
     halos = [lax.ppermute(halo, "gy", which) for halo, which in zip(halos, rows_pairs)]
     u0, u1, *coefs = call(
         load_kernel,
@@ -391,64 +400,63 @@
         [HBM] * 4,
         [VMEM] * 5,
         [pltpu.SemaphoreType.DMA((4, planes))],
-        weight=20,
-    )(*[pltpu.with_memory_space_constraint(x, pltpu.HBM) for x in (initial, kappa, velocity, rate)])
+        weight=WEIGHTS[1],
+    )(*fields)
     u0, u1, margin, message1 = call(
         functools.partial(first_kernel, n_halo),
         [wide, wide, f32(3, planes, ROWS, lanes), f32(rows + ROWS * n_halo, lanes)],
         [VMEM] * (5 + n_halo),
         [VMEM] * 4,
         aliases={0: 0, 1: 1},
-        weight=1,
+        weight=WEIGHTS[2],
     )(u0, u1, *coefs, *halos)
     near1 = lax.ppermute(message1, "gx", chips)
-    u1, near0 = lax.optimization_barrier((u1, near0))
     message2, message3, beside = call(
         second_kernel,
-        [f32(full, lanes), f32(rows, lanes), f32(4, full, lanes)],
+        [wide_plane, plane, f32(4, full, lanes)],
         [VMEM] * 6,
         [VMEM] * 3,
-        [pltpu.VMEM((planes, full, lanes), jnp.float32)],
-        weight=20,
+        [scratch(planes, full, lanes)],
+        weight=WEIGHTS[3],
     )(u0, u1, margin, *coefs)
+    beside = lax.ppermute(beside, "gx", cores)
     near2 = lax.ppermute(message2, "gx", chips)
-    beside = lax.ppermute(beside, "gx", cores)
-    message3, near1 = lax.optimization_barrier((message3, near1))
     near3 = lax.ppermute(message3, "gx", chips)
-    begun = call(
+    gain = call(gain_kernel, plane, [VMEM] * 2, VMEM, weight=WEIGHTS[4])(*coefs[:2])
+    beside, gain = lax.optimization_barrier((beside, gain))
+    state = call(
+        far_kernel,
+        f32(3, full, lanes),
+        [VMEM] * 7,
+        VMEM,
+        [scratch(full, lanes)],
+        weight=WEIGHTS[5],
+    )(u0, u1, margin, *coefs, beside)
+    out, more, almost = call(
         functools.partial(near_kernel, n_halo),
-        f32(2, full, lanes),
-        [VMEM] * 8,
-        VMEM,
-        [wide_plane, pltpu.VMEM((2, ROWS, lanes), jnp.float32)],
-        weight=20,
-    )(u0, u1, margin, *coefs, near0, near1)
-    out, state = call(
-        third_kernel,
-        [block, f32(2, full, lanes)],
-        [VMEM] * 8,
+        [block, f32(4, full, lanes), plane],
+        [VMEM] * 10,
+        [ANY, VMEM, VMEM],
+        [scratch(full, lanes), scratch(2, ROWS, lanes), scratch(rows, lanes), pltpu.SemaphoreType.DMA],
+        weight=WEIGHTS[6],
+    )(u0, u1, margin, *coefs, near0, near1, beside, state)
+    out, base = call(
+        fourth_kernel,
+        [block, plane],
+        [VMEM] * 7 + [ANY],
         [ANY, VMEM],
-        [wide_plane, pltpu.VMEM((2, full, lanes), jnp.float32), wide_plane,
-         pltpu.VMEM((2, rows, lanes), jnp.float32), pltpu.SemaphoreType.DMA((2,))],
-        weight=20,
-    )(u0, u1, margin, *coefs, begun, beside)
-    out, base, gain = call(
-        fourth_kernel,
-        [block, f32(rows, lanes), f32(rows, lanes)],
-        [VMEM] * 7 + [ANY],
-        [ANY, VMEM, VMEM],
-        [wide_plane, pltpu.VMEM((rows, lanes), jnp.float32), pltpu.SemaphoreType.DMA],
+        [scratch(full, lanes), scratch(rows, lanes), pltpu.SemaphoreType.DMA((2,))],
         {7: 0},
-        weight=20,
-    )(begun, state, margin, *coefs, near2, out)
+        weight=WEIGHTS[7],
+    )(more, almost, margin, *coefs, near2, out)
     return call(
         last_kernel,
         block,
         [VMEM] * 3 + [ANY],
         ANY,
-        [pltpu.VMEM((rows, lanes), jnp.float32), pltpu.SemaphoreType.DMA],
+        [scratch(rows, lanes), pltpu.SemaphoreType.DMA((4,))],
         {3: 0},
-        weight=1,
+        weight=WEIGHTS[8],
     )(base, gain, near3, out)
 
 

time: 33.3 us -> 30.8 us (0.925)
  waiting for transfers between devices: 7.71 us -> 3.74 us
  Pallas kernels: 13.4 us -> 15.4 us
  starting transfers between devices: 12 us -> 11.4 us
    ppermute x1, waiting for transfers between devices: 4.76 us -> 0.84 us  [local(): near1 = lax.ppermute(message1, 'gx', chips)]
    ppermute x1, waiting for transfers between devices: 2.94 us -> 0.01 us  [local(): near0 = lax.ppermute(message0, 'gx', chips)]
    ppermute x1, starting transfers between devices: 2.59 us -> 5.29 us  [local(): beside = lax.ppermute(beside, 'gx', cores)]
    ppermute x1, starting transfers between devices: 2.48 us -> 0.07 us  [local(): near3 = lax.ppermute(message3, 'gx', chips)]
    ppermute x1, waiting for transfers between devices: 0.01 us -> 2.23 us  [local(): beside = lax.ppermute(beside, 'gx', cores)]
    pallas_call x6 -> x7, Pallas kernels: 10.4 us -> 12.4 us  [the longest x1 4 us: local(): call(functools.partial(near_kernel, n_halo), [block, f32(4, full, lanes),...]
    ppermute x1, starting transfers between devices: 1.67 us -> 0.83 us  [local(): near2 = lax.ppermute(message2, 'gx', chips)]
    ppermute x1, waiting for transfers between devices: 0.01 us -> 0.66 us  [local(): near3 = lax.ppermute(message3, 'gx', chips)]
  transfers between devices with their start and end apart: 6 -> 6, of which waited for: 2 -> 3; matrix products, arithmetic and copies ran while one was open for 0% -> 0% of each run, Pallas kernels for 34% -> 44%
where the time goes in v3:
time: 30.8 us; the launch traced here: 30.7 us
  Pallas kernels  15.4 us (50%)
  starting transfers between devices  11.4 us (37%)
  waiting for transfers between devices  3.74 us (12%)
    ppermute x1, starting transfers between devices, local(): beside = lax.ppermute(beside, 'gx', cores)  5.29 us
    pallas_call x1, Pallas kernels, local(): call(functools.partial(near_kernel, n_halo), [block, f32(4, full, lanes),...  4 us
    pallas_call x1, Pallas kernels, local(): call(load_kernel, [wide, wide, block, block, block], [HBM] * 4, [VMEM] *...  2.7 us
    pallas_call x1, Pallas kernels, local(): call(far_kernel, f32(3, full, lanes), [VMEM] * 7, VMEM, [scratch(full, la...  2.61 us
    ppermute x1, waiting for transfers between devices, local(): beside = lax.ppermute(beside, 'gx', cores)  2.23 us
    ppermute x1, starting transfers between devices, local(): lax.ppermute(halo, 'gy', which)  2.13 us
    ppermute x1, starting transfers between devices, local(): near0 = lax.ppermute(message0, 'gx', chips)  2.05 us
    pallas_call x1, Pallas kernels, local(): call(second_kernel, [wide_plane, plane, f32(4, full, lanes)], [VMEM] * 6,...  1.86 us
  transfers between devices with their start and end apart: 6, of which 3 were waited for; matrix products, arithmetic and copies ran while one was open for 0% of the time, Pallas kernels for 44%

profile of v3, /device:TPU:1, one launch (start us, length us, event | category | flops | bytes accessed | tf_op | source)
XLA Modules:
  0.0 30.7 jit_solution(3193715303171404809)
XLA Ops:
  0.0 1.3 %shard_map.47 = (f32[128,512]{1,0:T(8,128)S(1)}, f32[16,4,512]{2,1,0:T(4,128)S(1)}) custom-call(f32[4,128,512]{2,1,0:T(8,128)} %initial.3, f32[4,128,512]{2,1,0:T(8,128)} %kappa.3, f32[4,128,512]{2,1,0:T(8,128)} %velocity.3, f32[4,128,512]{2,1,0:T(8,128)} %rate.3), custom_call_target="tpu_custom_call" | custom-call | flops 1000000000 | bytes 3000000 | tf_op jit(solution)/shard_map/pallas_call | solution.py:387
  1.3 2.1 %collective-permute-start = (f32[16,4,512]{2,1,0:T(4,128)S(1)}, f32[16,4,512]{2,1,0:T(4,128)S(1)}, u32[]{:S(2)}, u32[]{:S(2)}) collective-permute-start(f32[16,4,512]{2,1,0:T(4,128)S(1)} %get-tuple-element.31), channel_id=1, source_target_pairs={{0,1},{1,0},{2,3},{3,2},{4,5},{5,4},{6,7},{7,6},{8,9},{9,8},{10,11... | collective-permute-start | bytes 393224 | tf_op jit(solution)/shard_map/ppermute | solution.py:396
  3.4 2.1 %collective-permute-start.1 = (f32[128,512]{1,0:T(8,128)S(1)}, f32[128,512]{1,0:T(8,128)S(1)}, u32[]{:S(2)}, u32[]{:S(2)}) collective-permute-start(f32[128,512]{1,0:T(8,128)S(1)} %get-tuple-element.35), channel_id=1, source_target_pairs={{2,4},{4,2},{6,8},{8,6},{10,12},{12,10},{14,16},{16,14},{18,20},{2... | collective-permute-start | bytes 786440 | tf_op jit(solution)/shard_map/ppermute | solution.py:395
  5.5 2.7 %shard_map.46 = (f32[4,136,512]{2,1,0:T(8,128)S(1)}, f32[4,136,512]{2,1,0:T(8,128)S(1)}, f32[4,128,512]{2,1,0:T(8,128)S(1)}, f32[4,128,512]{2,1,0:T(8,128)S(1)}, f32[4,128,512]{2,1,0:T(8,128)S(1)}) custom-call(f32[4,128,512]{2,1,0:T(8,128)} %initial.3, f32[4,128,512]{2,1,0:T(8,128)} %kappa.3, f32[4,128,512]{2,1,0:T(8,128)} %velocity.3, f32[4,128,512]{2,1,0:T(8,128)} %rate.3), custom_call_target="tpu_custom_call" | custom-call | flops 20000000000 | bytes 60000000 | tf_op jit(solution)/shard_map/pallas_call | solution.py:397
  8.2 0.0 collective-permute-done.rest_0_
  8.2 0.3 shard_map.48
  8.5 1.0 %collective-permute-start.2 = (f32[136,512]{1,0:T(8,128)S(1)}, f32[136,512]{1,0:T(8,128)S(1)}, u32[]{:S(2)}, u32[]{:S(2)}) collective-permute-start(f32[136,512]{1,0:T(8,128)S(1)} %get-tuple-element.36), channel_id=1, source_target_pairs={{2,4},{4,2},{6,8},{8,6},{10,12},{12,10},{14,16},{16,14},{18,20},{2... | collective-permute-start | bytes 835592 | tf_op jit(solution)/shard_map/ppermute | solution.py:413
  9.6 1.9 %shard_map.49 = (f32[136,512]{1,0:T(8,128)S(1)}, f32[128,512]{1,0:T(8,128)S(1)}, f32[4,136,512]{2,1,0:T(8,128)S(1)}) custom-call(f32[4,136,512]{2,1,0:T(8,128)S(1)} %get-tuple-element.32.u0, f32[4,136,512]{2,1,0:T(8,128)S(1)} %get-tuple-element.33.u1, f32[3,4,8,512]{3,2,1,0:T(8,128)S(1)} %get-tuple-element.34.margin, ...), custom_call_target="tpu_custom_call" | custom-call | flops 60000002048 | bytes 180000000 | tf_op jit(solution)/shard_map/pallas_call | solution.py:414
  11.4 0.8 %collective-permute-start.4 = (f32[136,512]{1,0:T(8,128)S(1)}, f32[136,512]{1,0:T(8,128)S(1)}, u32[]{:S(2)}, u32[]{:S(2)}) collective-permute-start(f32[136,512]{1,0:T(8,128)S(1)} %get-tuple-element.41), channel_id=1, source_target_pairs={{2,4},{4,2},{6,8},{8,6},{10,12},{12,10},{14,16},{16,14},{18,20},{2... | collective-permute-start | bytes 835592 | tf_op jit(solution)/shard_map/ppermute | solution.py:423
  12.3 5.3 %collective-permute-start.3 = (f32[4,136,512]{2,1,0:T(8,128)S(1)}, f32[4,136,512]{2,1,0:T(8,128)S(1)}, u32[]{:S(2)}, u32[]{:S(2)}) collective-permute-start(f32[4,136,512]{2,1,0:T(8,128)S(1)} %get-tuple-element.37), channel_id=1, source_target_pairs={{0,2},{2,0},{4,6},{6,4},{8,10},{10,8},{12,14},{14,12},{16,18},{18,... | collective-permute-start | bytes 3342344 | tf_op jit(solution)/shard_map/ppermute | solution.py:422
  17.5 0.1 shard_map.50.gain
  17.6 0.1 collective-permute-start.5
  17.7 2.2 %collective-permute-done.3.beside = f32[4,136,512]{2,1,0:T(8,128)S(1)} collective-permute-done((f32[4,136,512]{2,1,0:T(8,128)S(1)}, f32[4,136,512]{2,1,0:T(8,128)S(1)}, u32[]{:S(2)}, u32[]{:S(2)}) %collective-permute-start.3) | collective-permute-done | bytes 1114144 | tf_op jit(solution)/shard_map/ppermute | solution.py:422
  19.9 2.6 %shard_map.51.state = f32[3,136,512]{2,1,0:T(8,128)S(1)} custom-call(f32[4,136,512]{2,1,0:T(8,128)S(1)} %get-tuple-element.32.u0, f32[4,136,512]{2,1,0:T(8,128)S(1)} %get-tuple-element.33.u1, f32[3,4,8,512]{3,2,1,0:T(8,128)S(1)} %get-tuple-element.34.margin, f32[4,128,512]{2,1,0:T(8,128)S(1)} %get-tuple-element.28.kappa, ...), custom_call_target="tpu_custom_call" | custom-call | flops 1000000000 | bytes 3000000 | tf_op jit(solution)/shard_map/pallas_call | solution.py:427
  22.5 0.0 collective-permute-done.1.near0
  22.5 0.8 %collective-permute-done.2.near1 = f32[136,512]{1,0:T(8,128)S(1)} collective-permute-done((f32[136,512]{1,0:T(8,128)S(1)}, f32[136,512]{1,0:T(8,128)S(1)}, u32[]{:S(2)}, u32[]{:S(2)}) %collective-permute-start.2) | collective-permute-done | bytes 278560 | tf_op jit(solution)/shard_map/ppermute | solution.py:413
  23.4 4.0 %shard_map.52 = (f32[4,128,512]{2,1,0:T(8,128)}, f32[4,136,512]{2,1,0:T(8,128)S(1)}, f32[128,512]{1,0:T(8,128)S(1)}) custom-call(f32[4,136,512]{2,1,0:T(8,128)S(1)} %get-tuple-element.32.u0, f32[4,136,512]{2,1,0:T(8,128)S(1)} %get-tuple-element.33.u1, f32[3,4,8,512]{3,2,1,0:T(8,128)S(1)} %get-tuple-element.34.margin, ...), custom_call_target="tpu_custom_call" | custom-call | flops 1000000000 | bytes 3000000 | tf_op jit(solution)/shard_map/pallas_call | solution.py:435
  27.4 0.0 collective-permute-done.4.near2
  27.4 1.8 %shard_map.53 = (f32[4,128,512]{2,1,0:T(8,128)}, f32[128,512]{1,0:T(8,128)S(1)}) custom-call(f32[4,136,512]{2,1,0:T(8,128)S(1)} %get-tuple-element.39.more, f32[128,512]{1,0:T(8,128)S(1)} %get-tuple-element.40.almost, f32[3,4,8,512]{3,2,1,0:T(8,128)S(1)} %get-tuple-element.34.margin, ...), custom_call_target="tpu_custom_call", output_to_operand_aliasing={{0}: (7, {})} | custom-call | flops 1000000000 | bytes 3000000 | tf_op jit(solution)/shard_map/pallas_call | solution.py:443
  29.3 0.7 %collective-permute-done.5.near3 = f32[128,512]{1,0:T(8,128)S(1)} collective-permute-done((f32[128,512]{1,0:T(8,128)S(1)}, f32[128,512]{1,0:T(8,128)S(1)}, u32[]{:S(2)}, u32[]{:S(2)}) %collective-permute-start.5) | collective-permute-done | bytes 262176 | tf_op jit(solution)/shard_map/ppermute | solution.py:424
  29.9 0.7 %shard_map.54 = f32[4,128,512]{2,1,0:T(8,128)} custom-call(f32[128,512]{1,0:T(8,128)S(1)} %get-tuple-element.43.base, f32[128,512]{1,0:T(8,128)S(1)} %shard_map.50.gain, f32[128,512]{1,0:T(8,128)S(1)} %collective-permute-done.5.near3, f32[4,128,512]{2,1,0:T(8,128)} %get-tuple-element.46.out_in), custom_call_target="tpu_custom_call", output_to_operand_aliasing={{}: (3, {})} | custom-call | flops 1000000000 | bytes 3000000 | tf_op jit(solution)/shard_map/pallas_call | solution.py:452
Async XLA Ops:
  1.3 6.9 %collective-permute-start = (f32[16,4,512]{2,1,0:T(4,128)S(1)}, f32[16,4,512]{2,1,0:T(4,128)S(1)}, u32[]{:S(2)}, u32[]{:S(2)}) collective-permute-start(f32[16,4,512]{2,1,0:T(4,128)S(1)} %get-tuple-element.31), channel_id=1, source_target_pairs={{0,1},{1,0},{2,3},{3,2},{4,5},{5,4},{6,7},{7,6},{8,9},{9,8},{10,11... | collective-permute-start | bytes 393224 | tf_op jit(solution)/shard_map/ppermute | solution.py:396
  3.4 19.1 %collective-permute-start.1 = (f32[128,512]{1,0:T(8,128)S(1)}, f32[128,512]{1,0:T(8,128)S(1)}, u32[]{:S(2)}, u32[]{:S(2)}) collective-permute-start(f32[128,512]{1,0:T(8,128)S(1)} %get-tuple-element.35), channel_id=1, source_target_pairs={{2,4},{4,2},{6,8},{8,6},{10,12},{12,10},{14,16},{16,14},{18,20},{2... | collective-permute-start | bytes 786440 | tf_op jit(solution)/shard_map/ppermute | solution.py:395
  8.5 14.9 %collective-permute-start.2 = (f32[136,512]{1,0:T(8,128)S(1)}, f32[136,512]{1,0:T(8,128)S(1)}, u32[]{:S(2)}, u32[]{:S(2)}) collective-permute-start(f32[136,512]{1,0:T(8,128)S(1)} %get-tuple-element.36), channel_id=1, source_target_pairs={{2,4},{4,2},{6,8},{8,6},{10,12},{12,10},{14,16},{16,14},{18,20},{2... | collective-permute-start | bytes 835592 | tf_op jit(solution)/shard_map/ppermute | solution.py:413
  11.4 16.0 %collective-permute-start.4 = (f32[136,512]{1,0:T(8,128)S(1)}, f32[136,512]{1,0:T(8,128)S(1)}, u32[]{:S(2)}, u32[]{:S(2)}) collective-permute-start(f32[136,512]{1,0:T(8,128)S(1)} %get-tuple-element.41), channel_id=1, source_target_pairs={{2,4},{4,2},{6,8},{8,6},{10,12},{12,10},{14,16},{16,14},{18,20},{2... | collective-permute-start | bytes 835592 | tf_op jit(solution)/shard_map/ppermute | solution.py:423
  12.3 7.7 %collective-permute-start.3 = (f32[4,136,512]{2,1,0:T(8,128)S(1)}, f32[4,136,512]{2,1,0:T(8,128)S(1)}, u32[]{:S(2)}, u32[]{:S(2)}) collective-permute-start(f32[4,136,512]{2,1,0:T(8,128)S(1)} %get-tuple-element.37), channel_id=1, source_target_pairs={{0,2},{2,0},{4,6},{6,4},{8,10},{10,8},{12,14},{14,12},{16,18},{18,... | collective-permute-start | bytes 3342344 | tf_op jit(solution)/shard_map/ppermute | solution.py:422
  17.6 12.3 %collective-permute-start.5 = (f32[128,512]{1,0:T(8,128)S(1)}, f32[128,512]{1,0:T(8,128)S(1)}, u32[]{:S(2)}, u32[]{:S(2)}) collective-permute-start(f32[128,512]{1,0:T(8,128)S(1)} %get-tuple-element.45), channel_id=1, source_target_pairs={{2,4},{4,2},{6,8},{8,6},{10,12},{12,10},{14,16},{16,14},{18,20},{2... | collective-permute-start | bytes 786440 | tf_op jit(solution)/shard_map/ppermute | solution.py:424

commit v4 on v3

v4 whole, which is shorter than its diff:
```python
import functools

import jax
import jax.numpy as jnp
from jax import lax
from jax.experimental import pallas as pl
from jax.experimental.pallas import tpu as pltpu
from jax.sharding import PartitionSpec as P

robin_p = 0.6
own = (1.0 - robin_p / 2) / (1.0 + robin_p / 2)
far = ((1.0 - own) + robin_p * (1.0 + own) / 2) / (1.0 + robin_p / 2)

VMEM = pl.BlockSpec(memory_space=pltpu.VMEM)
ANY = pl.BlockSpec(memory_space=pl.ANY)
HBM = pl.BlockSpec(memory_space=pltpu.HBM)
HALO = 4
WEIGHTS = (1, 1, 20, 1, 60, 20, 1, 1, 1, 1)
ROWS = 8
LANES = 128
PARTS = 4
UNROLL = 4
GROUPS = (8, 8, 4, 4)
UNROLLS = (1, 1, 1, 1)


def parity(axis):
    return lax.rem(lax.axis_index(axis), 2)


def plane_at(d, odd):
    return d + odd * (3 - 2 * d)


def pick(odd, yes, no):
    return jnp.where(jnp.broadcast_to(odd == 1, yes.shape), yes, no)


def load(ref, index, tile):
    rows = pl.ds(tile * ROWS if isinstance(tile, int) else pl.multiple_of(tile * ROWS, ROWS), ROWS)
    return [ref[*index, rows, k : k + LANES] for k in range(0, ref.shape[-1], LANES)]


def store(ref, index, tile, pieces):
    rows = pl.ds(tile * ROWS if isinstance(tile, int) else pl.multiple_of(tile * ROWS, ROWS), ROWS)
    for k, piece in enumerate(pieces):
        ref[*index, rows, k * LANES : (k + 1) * LANES] = piece


def ghost(mine, received=None):
    if received is None:
        return [m * own for m in mine]
    return [r * far + m * own for r, m in zip(received, mine)]


def updated(odd, cur, before, after, toward, away, kappa, velocity, rate):
    row = lax.broadcasted_iota(jnp.int32, (ROWS, LANES), 0)
    lane = lax.broadcasted_iota(jnp.int32, (ROWS, LANES), 1)
    zero = jnp.zeros((ROWS, LANES), jnp.float32)
    out = []
    for k, c in enumerate(cur):
        up = pltpu.roll(jnp.where(row == ROWS - 1, before[k], c), 1, 0)
        down = pltpu.roll(jnp.where(row == 0, after[k], c), ROWS - 1, 0)
        low = cur[k - 1] if k else zero
        high = cur[k + 1] if k + 1 < len(cur) else zero
        left = pltpu.roll(jnp.where(lane == LANES - 1, low, c), 1, 1)
        right = pltpu.roll(jnp.where(lane == 0, high, c), LANES - 1, 1)
        minus_x = pick(odd, away[k], toward[k]) if toward is not None else away[k]
        lap = away[k] + toward[k]
        lap = lap + up + down
        lap = lap + left + right
        lap = lap - 6.0 * c
        square = c * c
        bottom = 1.0 + square
        inverse = pl.reciprocal(bottom, approx=True)
        inverse = inverse * (2.0 - bottom * inverse)
        react = rate[k] * c * (square * inverse)
        out.append(c + kappa[k] * lap - velocity[k] * (c - minus_x) - react)
    return out


def sweep(odd, wanted, source, coefs, margins, near, distant, sink, inner, edges=()):
    needed = sorted({e for d in wanted for e in (d - 1, d, d + 1) if 0 <= e <= 3})
    last = source(wanted[0])[0].shape[-2] // ROWS - 1

    def work(tiles, together):
        state = {(d, i): load(*source(d), tile) for i, tile in enumerate(tiles) for d in needed}
        results = []
        for i, tile in enumerate(tiles):
            if isinstance(tile, int):
                before, after = (tile or last + 1) - 1, (tile + 1) % (last + 1)
            else:
                before, after = tile - 1, tile + 1
                if inner[0] == 0 and i == 0:
                    before = lax.select(tile == 0, last, before)
            refs, at = (margins, 0) if isinstance(tile, int) and tile == last else (coefs, tile)
            for d in wanted:
                cur = state[d, i]
                toward = state[d - 1, i] if d > 0 else ghost(cur, near(tile))
                away = state[d + 1, i] if d < 3 else ghost(cur, distant(tile))
                upper = state[d, i - 1] if together and i > 0 else load(*source(d), before)
                lower = state[d, i + 1] if together and i + 1 < len(tiles) else load(*source(d), after)
                p = plane_at(d, odd)
                kvr = [load(ref, (*lead, p), at) for ref, lead in refs]
                results.append((d, tile, updated(odd, cur, upper, lower, toward, away, *kvr)))
        for d, tile, pieces in results:
            sink(d, tile, pieces)

    count = inner[1] - inner[0]
    if count:
        size = max(n for n in range(1, GROUPS[len(wanted) - 1] + 1) if count % n == 0)

        def loop(index, carry):
            work([inner[0] + index * size + i for i in range(size)], True)
            return carry

        lax.fori_loop(0, count // size, loop, 0, unroll=UNROLLS[len(wanted) - 1])
    if edges:
        work(list(edges), False)


def coefficients(margin, kappa, velocity, rate):
    return [(ref, ()) for ref in (kappa, velocity, rate)], [(margin, (i,)) for i in range(3)]


def none(tile):
    return None


def plane_kernel(initial, plane, sems):
    p = plane_at(0, parity("gx"))
    part = plane.shape[0] // PARTS
    spans = [pl.ds(i * part, part) for i in range(PARTS)]
    copies = [pltpu.make_async_copy(initial.at[p, span], plane.at[span], sems.at[i]) for i, span in enumerate(spans)]
    for copy in copies:
        copy.start()
    for copy in copies:
        copy.wait()


def load_kernel(n_halo, initial, kappa, velocity, rate, u0, u1, kappa_v, velocity_v, rate_v, message, *rest):
    halos, (tiles, sems) = rest[:n_halo], rest[n_halo:]
    odd, odd_y = parity("gx"), parity("gy")
    rows = initial.shape[1]
    own_rows = pl.ds(0, rows)
    near, next_to = plane_at(0, odd), plane_at(1, odd)
    fields = (initial, kappa, velocity, rate)
    copies = [pltpu.make_async_copy(initial.at[p], u0.at[p, own_rows], sems.at[i]) for i, p in enumerate((near, next_to))]
    for f, held in enumerate((kappa_v, velocity_v, rate_v)):
        copies.append(pltpu.make_async_copy(fields[f + 1].at[near], held.at[near], sems.at[2 + f]))
    packs = []
    for f, field in enumerate(fields):
        packs.append(pltpu.make_async_copy(field.at[:, :ROWS, :], tiles.at[f, 0], sems.at[5 + 2 * f]))
        packs.append(pltpu.make_async_copy(field.at[:, rows - ROWS :, :], tiles.at[f, 1], sems.at[6 + 2 * f]))
    for copy in copies + packs:
        copy.start()
    u0[:, rows:, :] = jnp.zeros(u0[:, rows:, :].shape, jnp.float32)
    for copy in copies:
        copy.wait()

    def sink(d, tile, pieces):
        store(u1, (plane_at(d, odd),), tile, pieces)
        store(message, (), tile, pieces)

    coefs = [(ref, ()) for ref in (kappa_v, velocity_v, rate_v)]
    sweep(odd, [0], lambda d: (u0, (plane_at(d, odd),)), coefs, None, none, none, sink, (0, rows // ROWS))
    for copy in packs:
        copy.wait()
    for f in range(4):
        first, last = tiles[f, 0, :, :HALO], tiles[f, 1, :, ROWS - HALO :]
        halos[0][4 * f : 4 * f + 4] = pick(odd_y, first, last)
        if n_halo > 1:
            halos[1][4 * f : 4 * f + 4] = pick(odd_y, last, first)


def inner_kernel(initial, kappa, velocity, rate, u0_in, u1_in, kappa_in, velocity_in, rate_in,
                 u0, u1, kappa_v, velocity_v, rate_v, sems):
    del u0_in, u1_in, kappa_in, velocity_in, rate_in
    odd = parity("gx")
    planes, rows = initial.shape[:2]
    own_rows = pl.ds(0, rows)
    copies = {}
    for d in range(2, planes):
        p = plane_at(d, odd)
        copies[0, d] = pltpu.make_async_copy(initial.at[p], u0.at[p, own_rows], sems.at[0, d])
    for d in range(1, planes):
        p = plane_at(d, odd)
        for f, (field, held) in enumerate([(kappa, kappa_v), (velocity, velocity_v), (rate, rate_v)]):
            copies[f + 1, d] = pltpu.make_async_copy(field.at[p], held.at[p], sems.at[f + 1, d])
    order = [(0, 2), (1, 1), (2, 1), (3, 1), (0, 3)] + [(f, d) for d in range(2, planes) for f in range(1, 4)]
    for key in order:
        copies[key].start()

    def sink(d, tile, pieces):
        store(u1, (plane_at(d, odd),), tile, pieces)

    coefs = [(ref, ()) for ref in (kappa_v, velocity_v, rate_v)]
    for d in range(1, planes):
        if (0, d + 1) in copies:
            copies[0, d + 1].wait()
        for f in range(1, 4):
            copies[f, d].wait()
        sweep(odd, [d], lambda e: (u0, (plane_at(e, odd),)), coefs, None, none, none, sink, (0, rows // ROWS))


def first_kernel(n_halo, u0_in, u1_in, kappa, velocity, rate, *rest):
    del u0_in, u1_in
    halos, (u0, u1, margin, tail) = rest[:n_halo], rest[n_halo:]
    odd, odd_y = parity("gx"), parity("gy")
    rows = kappa.shape[1]
    for f in range(4):
        one = halos[0][4 * f : 4 * f + 4]
        two = halos[1][4 * f : 4 * f + 4] if n_halo > 1 else jnp.zeros_like(one)
        edge = jnp.concatenate([pick(odd_y, two, one), pick(odd_y, one, two)], axis=1)
        if f == 0:
            u0[:, rows:, :] = edge
        else:
            margin[f - 1] = edge

    def sink(d, tile, pieces):
        store(u1, (plane_at(d, odd),), tile, pieces)

    tiles = rows // ROWS
    sweep(odd, [0, 1, 2, 3], lambda d: (u0, (plane_at(d, odd),)), *coefficients(margin, kappa, velocity, rate),
          none, none, sink, (0, 0), (0, tiles - 1, tiles))
    p = plane_at(0, odd)
    row = lax.broadcasted_iota(jnp.int32, (ROWS, u0.shape[2]), 0)
    before = u0[p, rows:]
    before = jnp.where(row == HALO - 1, pltpu.roll(u1[p, rows - ROWS : rows], HALO, 0), before)
    tail[...] = jnp.where(row == HALO, pltpu.roll(u1[p, :ROWS], HALO, 0), before)


def packed(odd_y, n_halo, zero, one, two):
    row = lax.broadcasted_iota(jnp.int32, zero.shape, 0)
    rest = jnp.where(row == 2, pltpu.roll(two, 2, 0), jnp.where(row == 5, pltpu.roll(two, ROWS - 2, 0), one))
    if n_halo > 1:
        return [zero, rest]
    return [jnp.where(row // HALO == odd_y, zero, pltpu.roll(rest, HALO, 0))]


def unpacked(n_halo, tiles):
    zero, rest = tiles if n_halo > 1 else (tiles[0], pltpu.roll(tiles[0], HALO, 0))
    row = lax.broadcasted_iota(jnp.int32, zero.shape, 0)
    two = jnp.where(row < HALO, pltpu.roll(rest, ROWS - 2, 0), pltpu.roll(rest, 2, 0))
    return zero, rest, two


def second_kernel(n_halo, u0, u1, margin, tail, kappa, velocity, rate, message2, message3, beside, u2):
    odd, odd_y = parity("gx"), parity("gy")
    rows = kappa.shape[1]
    coefs, margins = coefficients(margin, kappa, velocity, rate)
    tiles = rows // ROWS

    def sink2(d, tile, pieces):
        store(u2, (plane_at(d, odd),), tile, pieces)
        if d == 0 and not (isinstance(tile, int) and tile == tiles):
            store(message2, (), tile, pieces)
        if d == 3:
            store(beside, (2,), tile, pieces)

    def sink3(d, tile, pieces):
        if d == 0:
            store(message3, (), tile, pieces)
        if d == 3:
            store(beside, (3,), tile, pieces)

    sweep(odd, [0, 1, 2, 3], lambda d: (u1, (plane_at(d, odd),)), coefs, margins, none, none, sink2, (0, tiles), (tiles,))
    p = plane_at(0, odd)
    for i, part in enumerate(packed(odd_y, n_halo, tail[...], u1[p, rows:], u2[p, rows:])):
        message2[rows + i * ROWS : rows + (i + 1) * ROWS] = part
    sweep(odd, [0, 3], lambda d: (u2, (plane_at(d, odd),)), coefs, margins, none, none, sink3, (0, tiles))
    beside[3, rows:] = jnp.zeros(beside[3, rows:].shape, jnp.float32)
    beside[0] = u0[plane_at(3, odd)]
    beside[1] = u1[plane_at(3, odd)]


def gain_kernel(kappa, velocity, gain):
    odd = parity("gx")
    p = plane_at(0, odd)

    def body(tile, carry):
        both = zip(load(kappa, (p,), tile), load(velocity, (p,), tile))
        store(gain, (), tile, [far * (k + pick(odd, jnp.zeros_like(v), v)) for k, v in both])
        return carry

    lax.fori_loop(0, kappa.shape[1] // ROWS, body, 0, unroll=UNROLL)


STATE = {(1, 0): 0, (2, 1): 1, (2, 2): 2, (3, 2): 3, (3, 3): 4, (2, 3): 5}
MORE = {(2, 0): 0, (3, 1): 1}


def stages(odd, u0, u1, state, more, others):
    def at(step, d):
        if (step, d) in others:
            return others[step, d]
        if (step, d) in STATE:
            return state, (STATE[step, d],)
        if (step, d) in MORE:
            return more, (MORE[step, d],)
        return (u0, u1)[step], (plane_at(d, odd),)

    def sink(step):
        def put(d, tile, pieces):
            ref, index = at(step, d)
            store(ref, index, tile, pieces)

        return put

    return lambda step: functools.partial(at, step), sink


def far_kernel(u0, u1, margin, kappa, velocity, rate, near0, beside, state, final3, v1):
    odd = parity("gx")
    tiles = kappa.shape[1] // ROWS
    coefs, margins = coefficients(margin, kappa, velocity, rate)
    source, sink = stages(odd, u0, u1, state, None, {(1, 3): (v1, ())})
    own_rows, edge = (0, tiles), ((0, 0), (tiles,))

    def near(tile):
        return load(near0, (), tile)

    def distant(step):
        return lambda tile: load(beside, (step,), tile)

    def finish(d, tile, pieces):
        store(final3, (), tile, pieces)

    sweep(odd, [0, 3], source(0), coefs, margins, near, distant(0), sink(1), own_rows)
    sweep(odd, [3], source(0), coefs, margins, none, distant(0), sink(1), *edge)
    sweep(odd, [1, 2, 3], source(1), coefs, margins, none, distant(1), sink(2), own_rows)
    sweep(odd, [2, 3], source(1), coefs, margins, none, distant(1), sink(2), *edge)
    sweep(odd, [2, 3], source(2), coefs, margins, none, distant(2), sink(3), own_rows)
    sweep(odd, [3], source(2), coefs, margins, none, distant(2), sink(3), *edge)
    sweep(odd, [3], source(3), coefs, margins, none, distant(3), finish, own_rows)


def near_kernel(kappa, velocity, rate, u1, near1, state, final3, out, more, final2, sem):
    odd = parity("gx")
    copy = pltpu.make_async_copy(final3, out.at[plane_at(3, odd)], sem)
    copy.start()
    own_rows = (0, kappa.shape[1] // ROWS)
    coefs, margins = coefficients(None, kappa, velocity, rate)
    source, sink = stages(odd, None, u1, state, more, {})

    def near(tile):
        return load(near1, (), tile)

    def finish(d, tile, pieces):
        store(final2, (), tile, pieces)

    sweep(odd, [0], source(1), coefs, margins, near, none, sink(2), own_rows)
    sweep(odd, [1], source(2), coefs, margins, none, none, sink(3), own_rows)
    sweep(odd, [2], source(3), coefs, margins, none, none, finish, own_rows)
    copy.wait()


def fourth_kernel(n_halo, margin, kappa, velocity, rate, u0, u1, near1, near2, state_in, more_in, final2_in, out_in,
                  state, more, final2, out, base, v3, edges, final1, sems):
    del state_in, more_in, final2_in, out_in
    odd, odd_y = parity("gx"), parity("gy")
    rows, lanes = kappa.shape[1:]
    tiles = rows // ROWS
    coefs, margins = coefficients(margin, kappa, velocity, rate)
    zero, one, two = unpacked(n_halo, [near2[rows + i * ROWS : rows + (i + 1) * ROWS] for i in range(n_halo)])
    row = lax.broadcasted_iota(jnp.int32, (ROWS, lanes), 0)
    top, bottom = row == 0, row == ROWS - 1
    if n_halo == 1:
        top, bottom = jnp.logical_and(top, odd_y == 1), jnp.logical_and(bottom, odd_y == 0)
    outer = pltpu.roll(zero, HALO, 0)
    edges[0] = zero
    edges[1] = one
    edges[2] = two
    edges[3] = jnp.where(top, outer, near1[:ROWS])
    edges[4] = jnp.where(bottom, outer, near1[rows - ROWS :])
    source, sink = stages(odd, u0, u1, state, more, {(3, 0): (v3, ())})
    copies = [pltpu.make_async_copy(final2, out.at[plane_at(2, odd)], sems.at[0]),
              pltpu.make_async_copy(final1, out.at[plane_at(1, odd)], sems.at[1])]

    def near(step):
        def piece(tile):
            if step == 1 and isinstance(tile, int) and tile < tiles:
                return load(edges, (4 if tile else 3,), 0)
            if isinstance(tile, int) and tile == tiles:
                return load(edges, (step,), 0)
            return load(near2, (), tile)

        return piece

    def finish(d, tile, pieces):
        store({0: base, 1: final1, 2: final2}[d], (), tile, pieces)

    own_rows, margin_only, outer_tiles = (0, tiles), ((0, 0), (tiles,)), ((0, 0), (0, tiles - 1, tiles))
    sweep(odd, [0], source(0), coefs, margins, near(0), none, sink(1), *margin_only)
    sweep(odd, [0], source(1), coefs, margins, near(1), none, sink(2), *outer_tiles)
    sweep(odd, [1], source(1), coefs, margins, none, none, sink(2), *margin_only)
    sweep(odd, [1], source(2), coefs, margins, none, none, sink(3), *outer_tiles)
    sweep(odd, [2], source(2), coefs, margins, none, none, sink(3), *margin_only)
    sweep(odd, [2], source(3), coefs, margins, none, none, finish, (0, 0), (0, tiles - 1))
    copies[0].start()
    sweep(odd, [0], source(2), coefs, margins, near(2), none, sink(3), own_rows, (tiles,))
    sweep(odd, [1], source(3), coefs, margins, none, none, finish, own_rows)
    copies[1].start()
    sweep(odd, [0], source(3), coefs, margins, none, none, finish, own_rows)
    for copy in copies:
        copy.wait()


def last_kernel(base, gain, near3, out_in, out, done, sems):
    del out_in
    odd = parity("gx")
    rows = base.shape[0]
    part = rows // PARTS
    copies = []
    for i in range(PARTS):
        span = pl.ds(i * part, part)
        done[span] = base[span] + gain[span] * near3[span]
        copies.append(pltpu.make_async_copy(done.at[span], out.at[plane_at(0, odd), span], sems.at[i]))
        copies[-1].start()
    for copy in copies:
        copy.wait()


def pairs(count, first, wrap):
    out = []
    for i in range(first, count, 2):
        if i + 1 < count or wrap:
            out += [(i, (i + 1) % count), ((i + 1) % count, i)]
    return out


def f32(*shape):
    return jax.ShapeDtypeStruct(shape, jnp.float32)


def call(kernel, out_shape, in_specs, out_specs, scratch=(), aliases=None, weight=0, limit=12):
    return pl.pallas_call(
        kernel,
        out_shape=out_shape,
        in_specs=in_specs,
        out_specs=out_specs,
        scratch_shapes=scratch,
        input_output_aliases=aliases or {},
        cost_estimate=pl.CostEstimate(flops=int(weight * 1e9), bytes_accessed=int(weight * 3.0e6), transcendentals=0),
        compiler_params=pltpu.CompilerParams(vmem_limit_bytes=limit * 1024 * 1024),
    )


def local(initial, kappa, velocity, rate):
    planes, rows, lanes = initial.shape
    full = rows + ROWS
    count_y = lax.axis_size("gy")
    count_x = lax.axis_size("gx")
    n_halo = 1 if count_y == 2 else 2
    chips = pairs(count_x, 1, True)
    cores = pairs(count_x, 0, False)
    rows_pairs = [pairs(count_y, 0, False), pairs(count_y, 1, False)][:n_halo]
    block, wide, plane, wide_plane = f32(planes, rows, lanes), f32(planes, full, lanes), f32(rows, lanes), f32(full, lanes)

    def scratch(*shape):
        return pltpu.VMEM(shape, jnp.float32)

    fields = [pltpu.with_memory_space_constraint(x, pltpu.HBM) for x in (initial, kappa, velocity, rate)]
    message0 = call(plane_kernel, plane, [HBM], ANY, [pltpu.SemaphoreType.DMA((PARTS,))], weight=WEIGHTS[0])(fields[0])
    near0 = lax.ppermute(message0, "gx", chips)
    fields[0], message0 = lax.optimization_barrier((fields[0], message0))
    u0, u1, *rest = call(
        functools.partial(load_kernel, n_halo),
        [wide, wide, block, block, block, plane] + [f32(16, HALO, lanes)] * n_halo,
        [HBM] * 4,
        [VMEM] * (6 + n_halo),
        [scratch(4, 2, planes, ROWS, lanes), pltpu.SemaphoreType.DMA((13,))],
        weight=WEIGHTS[1],
    )(*fields)
    coefs, message1, halos = rest[:3], rest[3], rest[4:]
    halos = [lax.ppermute(halo, "gy", which) for halo, which in zip(halos, rows_pairs)]
    near1 = lax.ppermute(message1, "gx", chips)
    u0, u1, *coefs = call(
        inner_kernel,
        [wide, wide, block, block, block],
        [HBM] * 4 + [VMEM] * 5,
        [VMEM] * 5,
        [pltpu.SemaphoreType.DMA((4, planes))],
        {4: 0, 5: 1, 6: 2, 7: 3, 8: 4},
        weight=WEIGHTS[2],
    )(*fields, u0, u1, *coefs)
    u0, u1, margin, tail = call(
        functools.partial(first_kernel, n_halo),
        [wide, wide, f32(3, planes, ROWS, lanes), f32(ROWS, lanes)],
        [VMEM] * (5 + n_halo),
        [VMEM] * 4,
        aliases={0: 0, 1: 1},
        weight=WEIGHTS[3],
    )(u0, u1, *coefs, *halos)
    message2, message3, beside = call(
        functools.partial(second_kernel, n_halo),
        [f32(rows + ROWS * n_halo, lanes), plane, f32(4, full, lanes)],
        [VMEM] * 7,
        [VMEM] * 3,
        [scratch(planes, full, lanes)],
        weight=WEIGHTS[4],
    )(u0, u1, margin, tail, *coefs)
    beside = lax.ppermute(beside, "gx", cores)
    near2 = lax.ppermute(message2, "gx", chips)
    near3 = lax.ppermute(message3, "gx", chips)
    gain = call(gain_kernel, plane, [VMEM] * 2, VMEM, weight=WEIGHTS[5])(*coefs[:2])
    beside, gain = lax.optimization_barrier((beside, gain))
    state, final3 = call(
        far_kernel,
        [f32(len(STATE), full, lanes), plane],
        [VMEM] * 8,
        [VMEM] * 2,
        [scratch(full, lanes)],
        weight=WEIGHTS[6],
    )(u0, u1, margin, *coefs, near0, beside)
    out, more, final2 = call(
        near_kernel,
        [block, f32(2, full, lanes), plane],
        [VMEM] * 7,
        [ANY, VMEM, VMEM],
        [pltpu.SemaphoreType.DMA],
        weight=WEIGHTS[7],
    )(*coefs, u1, near1, state, final3)
    state, more, final2, out, base = call(
        functools.partial(fourth_kernel, n_halo),
        [f32(len(STATE), full, lanes), f32(2, full, lanes), plane, block, plane],
        [VMEM] * 11 + [ANY],
        [VMEM] * 3 + [ANY, VMEM],
        [scratch(full, lanes), scratch(5, ROWS, lanes), scratch(rows, lanes), pltpu.SemaphoreType.DMA((2,))],
        {8: 0, 9: 1, 10: 2, 11: 3},
        weight=WEIGHTS[8],
    )(margin, *coefs, u0, u1, near1, near2, state, more, final2, out)
    return call(
        last_kernel,
        block,
        [VMEM] * 3 + [ANY],
        ANY,
        [scratch(rows, lanes), pltpu.SemaphoreType.DMA((PARTS,))],
        {3: 0},
        weight=WEIGHTS[9],
    )(base, gain, near3, out)


def solution(mesh):
    placed = P("gx", "gy", None)
    return jax.shard_map(local, mesh=mesh, in_specs=(placed,) * 4, out_specs=placed, check_vma=False)
```

time: 30.8 us -> 30.1 us (0.977)
  Pallas kernels: 15.4 us -> 13 us
  waiting for transfers between devices: 3.74 us -> 5.39 us
    pallas_call x7 -> x8, Pallas kernels: 14.4 us -> 12 us  [the longest x1 2.56 us: local(): call(far_kernel, [f32(len(STATE), full, lanes), plane], [VMEM] * 8, [VMEM...]
    ppermute x1, waiting for transfers between devices: 0.66 us -> 2.85 us  [local(): near3 = lax.ppermute(message3, 'gx', chips)]
    ppermute x1, starting transfers between devices: 0.83 us -> 1.74 us  [local(): near2 = lax.ppermute(message2, 'gx', chips)]
    ppermute x1, waiting for transfers between devices: 0.84 us -> 0.01 us  [local(): near1 = lax.ppermute(message1, 'gx', chips)]
    ppermute x1, starting transfers between devices: 2.13 us -> 1.3 us  [local(): lax.ppermute(halo, 'gy', which)]
    ppermute x1, starting transfers between devices: 1.05 us -> 0.31 us  [local(): near1 = lax.ppermute(message1, 'gx', chips)]
    ppermute x1, starting transfers between devices: 2.05 us -> 2.67 us  [local(): near0 = lax.ppermute(message0, 'gx', chips)]
  transfers between devices with their start and end apart: 6 -> 6, of which waited for: 3 -> 3; matrix products, arithmetic and copies ran while one was open for 0% -> 0% of each run, Pallas kernels for 44% -> 38%
where the time goes in v4:
time: 30.1 us; the launch traced here: 29.9 us
  Pallas kernels  13 us (43%)
  starting transfers between devices  11.4 us (38%)
  waiting for transfers between devices  5.39 us (18%)
    ppermute x1, starting transfers between devices, local(): beside = lax.ppermute(beside, 'gx', cores)  5.33 us
    ppermute x1, waiting for transfers between devices, local(): near3 = lax.ppermute(message3, 'gx', chips)  2.85 us
    ppermute x1, starting transfers between devices, local(): near0 = lax.ppermute(message0, 'gx', chips)  2.67 us
    pallas_call x1, Pallas kernels, local(): call(far_kernel, [f32(len(STATE), full, lanes), plane], [VMEM] * 8, [VMEM...  2.56 us
    pallas_call x1, Pallas kernels, local(): call(inner_kernel, [wide, wide, block, block, block], [HBM] * 4 + [VMEM]...  2.25 us
    ppermute x1, waiting for transfers between devices, local(): beside = lax.ppermute(beside, 'gx', cores)  2.23 us
    pallas_call x1, Pallas kernels, local(): call(functools.partial(second_kernel, n_halo), [f32(rows + ROWS * n_halo,...  1.85 us
    ppermute x1, starting transfers between devices, local(): near2 = lax.ppermute(message2, 'gx', chips)  1.74 us
  transfers between devices with their start and end apart: 6, of which 3 were waited for; matrix products, arithmetic and copies ran while one was open for 0% of the time, Pallas kernels for 38%

profile of v4, /device:TPU:1, one launch (start us, length us, event | category | flops | bytes accessed | tf_op | source)
XLA Modules:
  0.0 29.9 jit_solution(10229891425257128121)
XLA Ops:
  0.0 1.0 %shard_map.46 = f32[128,512]{1,0:T(8,128)S(1)} custom-call(f32[4,128,512]{2,1,0:T(8,128)} %initial.3), custom_call_target="tpu_custom_call" | custom-call | flops 1000000000 | bytes 3000000 | tf_op jit(solution)/shard_map/pallas_call | solution.py:464
  1.0 2.7 %collective-permute-start.3 = (f32[128,512]{1,0:T(8,128)S(1)}, f32[128,512]{1,0:T(8,128)S(1)}, u32[]{:S(2)}, u32[]{:S(2)}) collective-permute-start(f32[128,512]{1,0:T(8,128)S(1)} %shard_map.46), channel_id=1, source_target_pairs={{2,4},{4,2},{6,8},{8,6},{10,12},{12,10},{14,16},{16,14},{18,20},{2... | collective-permute-start | bytes 786440 | tf_op jit(solution)/shard_map/ppermute | solution.py:465
  3.6 1.7 %shard_map.47 = (f32[4,136,512]{2,1,0:T(8,128)S(1)}, f32[4,136,512]{2,1,0:T(8,128)S(1)}, f32[4,128,512]{2,1,0:T(8,128)S(1)}, f32[4,128,512]{2,1,0:T(8,128)S(1)},...) custom-call(f32[4,128,512]{2,1,0:T(8,128)} %initial.3, f32[4,128,512]{2,1,0:T(8,128)} %kappa.3, ...), custom_call_target="tpu_custom_call" | custom-call | flops 1000000000 | bytes 3000000 | tf_op jit(solution)/shard_map/pallas_call | solution.py:467
  5.4 1.3 %collective-permute-start = (f32[16,4,512]{2,1,0:T(4,128)S(1)}, f32[16,4,512]{2,1,0:T(4,128)S(1)}, u32[]{:S(2)}, u32[]{:S(2)}) collective-permute-start(f32[16,4,512]{2,1,0:T(4,128)S(1)} %get-tuple-element.45), channel_id=1, source_target_pairs={{0,1},{1,0},{2,3},{3,2},{4,5},{5,4},{6,7},{7,6},{8,9},{9,8},{10,11... | collective-permute-start | bytes 393224 | tf_op jit(solution)/shard_map/ppermute | solution.py:476
  6.7 0.3 %collective-permute-start.1 = (f32[128,512]{1,0:T(8,128)S(1)}, f32[128,512]{1,0:T(8,128)S(1)}, u32[]{:S(2)}, u32[]{:S(2)}) collective-permute-start(f32[128,512]{1,0:T(8,128)S(1)} %get-tuple-element.49), channel_id=1, source_target_pairs={{2,4},{4,2},{6,8},{8,6},{10,12},{12,10},{14,16},{16,14},{18,20},{2... | collective-permute-start | bytes 786440 | tf_op jit(solution)/shard_map/ppermute | solution.py:477
  7.0 2.2 %shard_map.48 = (f32[4,136,512]{2,1,0:T(8,128)S(1)}, f32[4,136,512]{2,1,0:T(8,128)S(1)}, f32[4,128,512]{2,1,0:T(8,128)S(1)}, f32[4,128,512]{2,1,0:T(8,128)S(1)}, f32[4,128,512]{2,1,0:T(8,128)S(1)}) custom-call(f32[4,128,512]{2,1,0:T(8,128)} %initial.3, ...), custom_call_target="tpu_custom_call", output_to_operand_aliasing={{0}: (4, {}), {1}: (5, {}), {2}: (6, {}), {3}: (7, {}), {4}... | custom-call | flops 20000000000 | bytes 60000000 | tf_op jit(solution)/shard_map/pallas_call | solution.py:478
  9.3 0.3 %collective-permute-done.rest_0_ = f32[16,4,512]{2,1,0:T(4,128)S(1)} collective-permute-done((f32[16,4,512]{2,1,0:T(4,128)S(1)}, f32[16,4,512]{2,1,0:T(4,128)S(1)}, u32[]{:S(2)}, u32[]{:S(2)}) %collective-permute-start) | collective-permute-done | bytes 131104 | tf_op jit(solution)/shard_map/ppermute | solution.py:476
  9.6 0.3 shard_map.49
  9.8 1.9 %shard_map.50 = (f32[136,512]{1,0:T(8,128)S(1)}, f32[128,512]{1,0:T(8,128)S(1)}, f32[4,136,512]{2,1,0:T(8,128)S(1)}) custom-call(f32[4,136,512]{2,1,0:T(8,128)S(1)} %get-tuple-element.47.u0, f32[4,136,512]{2,1,0:T(8,128)S(1)} %get-tuple-element.48.u1, f32[3,4,8,512]{3,2,1,0:T(8,128)S(1)} %get-tuple-element.46.margin, f32[8,512]{1,0:T(8,128)S(1)} %get-tuple-element.50.tail, ...), custom_call_target="tpu_custom_call" | custom-call | flops 60000002048 | bytes 180000000 | tf_op jit(solution)/shard_map/pallas_call | solution.py:495
  11.7 1.7 %collective-permute-start.2 = (f32[136,512]{1,0:T(8,128)S(1)}, f32[136,512]{1,0:T(8,128)S(1)}, u32[]{:S(2)}, u32[]{:S(2)}) collective-permute-start(f32[136,512]{1,0:T(8,128)S(1)} %get-tuple-element.51), channel_id=1, source_target_pairs={{2,4},{4,2},{6,8},{8,6},{10,12},{12,10},{14,16},{16,14},{18,20},{2... | collective-permute-start | bytes 835592 | tf_op jit(solution)/shard_map/ppermute | solution.py:504
  13.4 5.3 %collective-permute-start.4 = (f32[4,136,512]{2,1,0:T(8,128)S(1)}, f32[4,136,512]{2,1,0:T(8,128)S(1)}, u32[]{:S(2)}, u32[]{:S(2)}) collective-permute-start(f32[4,136,512]{2,1,0:T(8,128)S(1)} %get-tuple-element.52), channel_id=1, source_target_pairs={{0,2},{2,0},{4,6},{6,4},{8,10},{10,8},{12,14},{14,12},{16,18},{18,... | collective-permute-start | bytes 3342344 | tf_op jit(solution)/shard_map/ppermute | solution.py:503
  18.8 0.1 shard_map.51.gain
  18.8 0.1 collective-permute-start.5
  18.9 2.2 %collective-permute-done.4.beside = f32[4,136,512]{2,1,0:T(8,128)S(1)} collective-permute-done((f32[4,136,512]{2,1,0:T(8,128)S(1)}, f32[4,136,512]{2,1,0:T(8,128)S(1)}, u32[]{:S(2)}, u32[]{:S(2)}) %collective-permute-start.4) | collective-permute-done | bytes 1114144 | tf_op jit(solution)/shard_map/ppermute | solution.py:503
  21.2 0.0 collective-permute-done.3.near0
  21.2 2.6 %shard_map.52 = (f32[6,136,512]{2,1,0:T(8,128)S(1)}, f32[128,512]{1,0:T(8,128)S(1)}) custom-call(f32[4,136,512]{2,1,0:T(8,128)S(1)} %get-tuple-element.47.u0, f32[4,136,512]{2,1,0:T(8,128)S(1)} %get-tuple-element.48.u1, f32[3,4,8,512]{3,2,1,0:T(8,128)S(1)} %get-tuple-element.46.margin, f32[4,128,512]{2,1,0:T(8,128)S(1)} %get-tuple-element.42.kappa, ...), custom_call_target="tpu_custom_call" | custom-call | flops 1000000000 | bytes 3000000 | tf_op jit(solution)/shard_map/pallas_call | solution.py:508
  23.7 0.0 collective-permute-done.1.near1
  23.7 0.9 %shard_map.53 = (f32[4,128,512]{2,1,0:T(8,128)}, f32[2,136,512]{2,1,0:T(8,128)S(1)}, f32[128,512]{1,0:T(8,128)S(1)}) custom-call(f32[4,128,512]{2,1,0:T(8,128)S(1)} %get-tuple-element.42.kappa, f32[4,128,512]{2,1,0:T(8,128)S(1)} %get-tuple-element.43.velocity, f32[4,128,512]{2,1,0:T(8,128)S(1)} %get-tuple-element.44.rate, ...), custom_call_target="tpu_custom_call" | custom-call | flops 1000000000 | bytes 3000000 | tf_op jit(solution)/shard_map/pallas_call | solution.py:516
  24.7 0.0 collective-permute-done.2.near2
  24.7 1.6 %shard_map.54 = (f32[6,136,512]{2,1,0:T(8,128)S(1)}, f32[2,136,512]{2,1,0:T(8,128)S(1)}, f32[128,512]{1,0:T(8,128)S(1)}, f32[4,128,512]{2,1,0:T(8,128)}, f32[128,512]{1,0:T(8,128)S(1)}) custom-call(f32[3,4,8,512]{3,2,1,0:T(8,128)S(1)} %get-tuple-element.46.margin, ...), custom_call_target="tpu_custom_call", output_to_operand_aliasing={{0}: (8, {}), {1}: (9, {}), {2}: (10, {}), {3}: (11, {})} | custom-call | flops 1000000000 | bytes 3000000 | tf_op jit(solution)/shard_map/pallas_call | solution.py:524
  26.3 2.8 %collective-permute-done.5.near3 = f32[128,512]{1,0:T(8,128)S(1)} collective-permute-done((f32[128,512]{1,0:T(8,128)S(1)}, f32[128,512]{1,0:T(8,128)S(1)}, u32[]{:S(2)}, u32[]{:S(2)}) %collective-permute-start.5) | collective-permute-done | bytes 262176 | tf_op jit(solution)/shard_map/ppermute | solution.py:505
  29.2 0.7 %shard_map.55 = f32[4,128,512]{2,1,0:T(8,128)} custom-call(f32[128,512]{1,0:T(8,128)S(1)} %get-tuple-element.59.base, f32[128,512]{1,0:T(8,128)S(1)} %shard_map.51.gain, f32[128,512]{1,0:T(8,128)S(1)} %collective-permute-done.5.near3, f32[4,128,512]{2,1,0:T(8,128)} %get-tuple-element.62.out_in), custom_call_target="tpu_custom_call", output_to_operand_aliasing={{}: (3, {})} | custom-call | flops 1000000000 | bytes 3000000 | tf_op jit(solution)/shard_map/pallas_call | solution.py:533
Async XLA Ops:
  1.0 20.2 %collective-permute-start.3 = (f32[128,512]{1,0:T(8,128)S(1)}, f32[128,512]{1,0:T(8,128)S(1)}, u32[]{:S(2)}, u32[]{:S(2)}) collective-permute-start(f32[128,512]{1,0:T(8,128)S(1)} %shard_map.46), channel_id=1, source_target_pairs={{2,4},{4,2},{6,8},{8,6},{10,12},{12,10},{14,16},{16,14},{18,20},{2... | collective-permute-start | bytes 786440 | tf_op jit(solution)/shard_map/ppermute | solution.py:465
  5.4 4.2 %collective-permute-start = (f32[16,4,512]{2,1,0:T(4,128)S(1)}, f32[16,4,512]{2,1,0:T(4,128)S(1)}, u32[]{:S(2)}, u32[]{:S(2)}) collective-permute-start(f32[16,4,512]{2,1,0:T(4,128)S(1)} %get-tuple-element.45), channel_id=1, source_target_pairs={{0,1},{1,0},{2,3},{3,2},{4,5},{5,4},{6,7},{7,6},{8,9},{9,8},{10,11... | collective-permute-start | bytes 393224 | tf_op jit(solution)/shard_map/ppermute | solution.py:476
  6.7 17.0 %collective-permute-start.1 = (f32[128,512]{1,0:T(8,128)S(1)}, f32[128,512]{1,0:T(8,128)S(1)}, u32[]{:S(2)}, u32[]{:S(2)}) collective-permute-start(f32[128,512]{1,0:T(8,128)S(1)} %get-tuple-element.49), channel_id=1, source_target_pairs={{2,4},{4,2},{6,8},{8,6},{10,12},{12,10},{14,16},{16,14},{18,20},{2... | collective-permute-start | bytes 786440 | tf_op jit(solution)/shard_map/ppermute | solution.py:477
  11.7 13.0 %collective-permute-start.2 = (f32[136,512]{1,0:T(8,128)S(1)}, f32[136,512]{1,0:T(8,128)S(1)}, u32[]{:S(2)}, u32[]{:S(2)}) collective-permute-start(f32[136,512]{1,0:T(8,128)S(1)} %get-tuple-element.51), channel_id=1, source_target_pairs={{2,4},{4,2},{6,8},{8,6},{10,12},{12,10},{14,16},{16,14},{18,20},{2... | collective-permute-start | bytes 835592 | tf_op jit(solution)/shard_map/ppermute | solution.py:504
  13.4 7.7 %collective-permute-start.4 = (f32[4,136,512]{2,1,0:T(8,128)S(1)}, f32[4,136,512]{2,1,0:T(8,128)S(1)}, u32[]{:S(2)}, u32[]{:S(2)}) collective-permute-start(f32[4,136,512]{2,1,0:T(8,128)S(1)} %get-tuple-element.52), channel_id=1, source_target_pairs={{0,2},{2,0},{4,6},{6,4},{8,10},{10,8},{12,14},{14,12},{16,18},{18,... | collective-permute-start | bytes 3342344 | tf_op jit(solution)/shard_map/ppermute | solution.py:503
  18.8 10.3 %collective-permute-start.5 = (f32[128,512]{1,0:T(8,128)S(1)}, f32[128,512]{1,0:T(8,128)S(1)}, u32[]{:S(2)}, u32[]{:S(2)}) collective-permute-start(f32[128,512]{1,0:T(8,128)S(1)} %get-tuple-element.61), channel_id=1, source_target_pairs={{2,4},{4,2},{6,8},{8,6},{10,12},{12,10},{14,16},{16,14},{18,20},{2... | collective-permute-start | bytes 786440 | tf_op jit(solution)/shard_map/ppermute | solution.py:505

commit v5 on v4

--- a/solution.py
+++ b/solution.py
@@ -15,13 +15,12 @@
 ANY = pl.BlockSpec(memory_space=pl.ANY)
 HBM = pl.BlockSpec(memory_space=pltpu.HBM)
 HALO = 4
-WEIGHTS = (1, 1, 20, 1, 60, 20, 1, 1, 1, 1)
+WEIGHTS = (1, 1, 20, 1, 60, 20, 0, 0, 0, 0)
 ROWS = 8
 LANES = 128
 PARTS = 4
 UNROLL = 4
 GROUPS = (8, 8, 4, 4)
-UNROLLS = (1, 1, 1, 1)
 
 
 def parity(axis):
@@ -114,7 +113,7 @@
             work([inner[0] + index * size + i for i in range(size)], True)
             return carry
 
-        lax.fori_loop(0, count // size, loop, 0, unroll=UNROLLS[len(wanted) - 1])
+        lax.fori_loop(0, count // size, loop, 0)
     if edges:
         work(list(edges), False)
 
@@ -174,7 +173,7 @@
 
 
 def inner_kernel(initial, kappa, velocity, rate, u0_in, u1_in, kappa_in, velocity_in, rate_in,
-                 u0, u1, kappa_v, velocity_v, rate_v, sems):
+                 u0, u1, kappa_v, velocity_v, rate_v, u2, sems):
     del u0_in, u1_in, kappa_in, velocity_in, rate_in
     odd = parity("gx")
     planes, rows = initial.shape[:2]
@@ -202,10 +201,15 @@
             copies[f, d].wait()
         sweep(odd, [d], lambda e: (u0, (plane_at(e, odd),)), coefs, None, none, none, sink, (0, rows // ROWS))
 
-
-def first_kernel(n_halo, u0_in, u1_in, kappa, velocity, rate, *rest):
-    del u0_in, u1_in
-    halos, (u0, u1, margin, tail) = rest[:n_halo], rest[n_halo:]
+    def sink2(d, tile, pieces):
+        store(u2, (plane_at(d, odd),), tile, pieces)
+
+    sweep(odd, [0, 1, 2, 3], lambda d: (u1, (plane_at(d, odd),)), coefs, None, none, none, sink2, (1, rows // ROWS - 1))
+
+
+def first_kernel(n_halo, u0_in, u1_in, u2_in, kappa, velocity, rate, *rest):
+    del u0_in, u1_in, u2_in
+    halos, (u0, u1, u2, margin, message) = rest[:n_halo], rest[n_halo:]
     odd, odd_y = parity("gx"), parity("gy")
     rows = kappa.shape[1]
     for f in range(4):
@@ -220,14 +224,22 @@
     def sink(d, tile, pieces):
         store(u1, (plane_at(d, odd),), tile, pieces)
 
+    def sink2(d, tile, pieces):
+        store(u2, (plane_at(d, odd),), tile, pieces)
+
     tiles = rows // ROWS
-    sweep(odd, [0, 1, 2, 3], lambda d: (u0, (plane_at(d, odd),)), *coefficients(margin, kappa, velocity, rate),
-          none, none, sink, (0, 0), (0, tiles - 1, tiles))
+    outer, every = ((0, 0), (0, tiles - 1, tiles)), [0, 1, 2, 3]
+    coefs, margins = coefficients(margin, kappa, velocity, rate)
+    sweep(odd, every, lambda d: (u0, (plane_at(d, odd),)), coefs, margins, none, none, sink, *outer)
+    sweep(odd, every, lambda d: (u1, (plane_at(d, odd),)), coefs, margins, none, none, sink2, *outer)
     p = plane_at(0, odd)
     row = lax.broadcasted_iota(jnp.int32, (ROWS, u0.shape[2]), 0)
     before = u0[p, rows:]
     before = jnp.where(row == HALO - 1, pltpu.roll(u1[p, rows - ROWS : rows], HALO, 0), before)
-    tail[...] = jnp.where(row == HALO, pltpu.roll(u1[p, :ROWS], HALO, 0), before)
+    before = jnp.where(row == HALO, pltpu.roll(u1[p, :ROWS], HALO, 0), before)
+    message[:rows] = u2[p, :rows]
+    for i, part in enumerate(packed(odd_y, n_halo, before, u1[p, rows:], u2[p, rows:])):
+        message[rows + i * ROWS : rows + (i + 1) * ROWS] = part
 
 
 def packed(odd_y, n_halo, zero, one, two):
@@ -245,33 +257,21 @@
     return zero, rest, two
 
 
-def second_kernel(n_halo, u0, u1, margin, tail, kappa, velocity, rate, message2, message3, beside, u2):
-    odd, odd_y = parity("gx"), parity("gy")
+def second_kernel(u0, u1, u2, margin, kappa, velocity, rate, message3, beside):
+    odd = parity("gx")
     rows = kappa.shape[1]
     coefs, margins = coefficients(margin, kappa, velocity, rate)
-    tiles = rows // ROWS
-
-    def sink2(d, tile, pieces):
-        store(u2, (plane_at(d, odd),), tile, pieces)
-        if d == 0 and not (isinstance(tile, int) and tile == tiles):
-            store(message2, (), tile, pieces)
-        if d == 3:
-            store(beside, (2,), tile, pieces)
-
-    def sink3(d, tile, pieces):
+
+    def sink(d, tile, pieces):
         if d == 0:
             store(message3, (), tile, pieces)
-        if d == 3:
+        else:
             store(beside, (3,), tile, pieces)
 
-    sweep(odd, [0, 1, 2, 3], lambda d: (u1, (plane_at(d, odd),)), coefs, margins, none, none, sink2, (0, tiles), (tiles,))
-    p = plane_at(0, odd)
-    for i, part in enumerate(packed(odd_y, n_halo, tail[...], u1[p, rows:], u2[p, rows:])):
-        message2[rows + i * ROWS : rows + (i + 1) * ROWS] = part
-    sweep(odd, [0, 3], lambda d: (u2, (plane_at(d, odd),)), coefs, margins, none, none, sink3, (0, tiles))
+    sweep(odd, [0, 3], lambda d: (u2, (plane_at(d, odd),)), coefs, margins, none, none, sink, (0, rows // ROWS))
     beside[3, rows:] = jnp.zeros(beside[3, rows:].shape, jnp.float32)
-    beside[0] = u0[plane_at(3, odd)]
-    beside[1] = u1[plane_at(3, odd)]
+    for step, field in enumerate((u0, u1, u2)):
+        beside[step] = field[plane_at(3, odd)]
 
 
 def gain_kernel(kappa, velocity, gain):
@@ -475,36 +475,35 @@
     coefs, message1, halos = rest[:3], rest[3], rest[4:]
     halos = [lax.ppermute(halo, "gy", which) for halo, which in zip(halos, rows_pairs)]
     near1 = lax.ppermute(message1, "gx", chips)
-    u0, u1, *coefs = call(
+    u0, u1, *coefs, u2 = call(
         inner_kernel,
-        [wide, wide, block, block, block],
+        [wide, wide, block, block, block, wide],
         [HBM] * 4 + [VMEM] * 5,
-        [VMEM] * 5,
+        [VMEM] * 6,
         [pltpu.SemaphoreType.DMA((4, planes))],
         {4: 0, 5: 1, 6: 2, 7: 3, 8: 4},
         weight=WEIGHTS[2],
     )(*fields, u0, u1, *coefs)
-    u0, u1, margin, tail = call(
+    u0, u1, u2, margin, message2 = call(
         functools.partial(first_kernel, n_halo),
-        [wide, wide, f32(3, planes, ROWS, lanes), f32(ROWS, lanes)],
-        [VMEM] * (5 + n_halo),
-        [VMEM] * 4,
-        aliases={0: 0, 1: 1},
+        [wide, wide, wide, f32(3, planes, ROWS, lanes), f32(rows + ROWS * n_halo, lanes)],
+        [VMEM] * (6 + n_halo),
+        [VMEM] * 5,
+        aliases={0: 0, 1: 1, 2: 2},
         weight=WEIGHTS[3],
-    )(u0, u1, *coefs, *halos)
-    message2, message3, beside = call(
-        functools.partial(second_kernel, n_halo),
-        [f32(rows + ROWS * n_halo, lanes), plane, f32(4, full, lanes)],
+    )(u0, u1, u2, *coefs, *halos)
+    message3, beside = call(
+        second_kernel,
+        [plane, f32(4, full, lanes)],
         [VMEM] * 7,
-        [VMEM] * 3,
-        [scratch(planes, full, lanes)],
+        [VMEM] * 2,
         weight=WEIGHTS[4],
-    )(u0, u1, margin, tail, *coefs)
+    )(u0, u1, u2, margin, *coefs)
+    beside, near0 = lax.optimization_barrier((beside, near0))
     beside = lax.ppermute(beside, "gx", cores)
     near2 = lax.ppermute(message2, "gx", chips)
     near3 = lax.ppermute(message3, "gx", chips)
     gain = call(gain_kernel, plane, [VMEM] * 2, VMEM, weight=WEIGHTS[5])(*coefs[:2])
-    beside, gain = lax.optimization_barrier((beside, gain))
     state, final3 = call(
         far_kernel,
         [f32(len(STATE), full, lanes), plane],

time: 30.1 us -> 29.2 us (0.970)
  waiting for transfers between devices: 5.39 us -> 4.02 us
  starting transfers between devices: 11.4 us -> 11.9 us
    ppermute x1, waiting for transfers between devices: 2.85 us -> 1.69 us  [local(): near3 = lax.ppermute(message3, 'gx', chips)]
    ppermute x1, starting transfers between devices: 5.33 us -> 5.73 us  [local(): beside = lax.ppermute(beside, 'gx', cores)]
    ppermute x1, starting transfers between devices: 0.07 us -> 0.38 us  [local(): near3 = lax.ppermute(message3, 'gx', chips)]
  transfers between devices with their start and end apart: 6 -> 6, of which waited for: 3 -> 2; matrix products, arithmetic and copies ran while one was open for 0% -> 0% of each run, Pallas kernels for 38% -> 39%
where the time goes in v5:
time: 29.2 us; the launch traced here: 29 us
  Pallas kernels  13 us (45%)
  starting transfers between devices  11.9 us (41%)
  waiting for transfers between devices  4.02 us (14%)
    ppermute x1, starting transfers between devices, local(): beside = lax.ppermute(beside, 'gx', cores)  5.73 us
    pallas_call x1, Pallas kernels, local(): call(inner_kernel, [wide, wide, block, block, block, wide], [HBM] * 4 + [...  3.3 us
    ppermute x1, starting transfers between devices, local(): near0 = lax.ppermute(message0, 'gx', chips)  2.67 us
    pallas_call x1, Pallas kernels, local(): call(far_kernel, [f32(len(STATE), full, lanes), plane], [VMEM] * 8, [VMEM...  2.56 us
    ppermute x1, waiting for transfers between devices, local(): beside = lax.ppermute(beside, 'gx', cores)  2.31 us
    pallas_call x1, Pallas kernels, local(): call(functools.partial(load_kernel, n_halo), [wide, wide, block, block, b...  1.74 us
    ppermute x1, waiting for transfers between devices, local(): near3 = lax.ppermute(message3, 'gx', chips)  1.69 us
    pallas_call x1, Pallas kernels, local(): call(functools.partial(fourth_kernel, n_halo), [f32(len(STATE), full, lan...  1.61 us
  transfers between devices with their start and end apart: 6, of which 2 were waited for; matrix products, arithmetic and copies ran while one was open for 0% of the time, Pallas kernels for 39%

profile of v5, /device:TPU:1, one launch (start us, length us, event | category | flops | bytes accessed | tf_op | source)
XLA Modules:
  0.0 29.0 jit_solution(3326999550379133806)
XLA Ops:
  0.0 1.0 %shard_map.46 = f32[128,512]{1,0:T(8,128)S(1)} custom-call(f32[4,128,512]{2,1,0:T(8,128)} %initial.3), custom_call_target="tpu_custom_call" | custom-call | flops 1000000000 | bytes 3000000 | tf_op jit(solution)/shard_map/pallas_call | solution.py:464
  1.0 2.7 %collective-permute-start.3 = (f32[128,512]{1,0:T(8,128)S(1)}, f32[128,512]{1,0:T(8,128)S(1)}, u32[]{:S(2)}, u32[]{:S(2)}) collective-permute-start(f32[128,512]{1,0:T(8,128)S(1)} %shard_map.46), channel_id=1, source_target_pairs={{2,4},{4,2},{6,8},{8,6},{10,12},{12,10},{14,16},{16,14},{18,20},{2... | collective-permute-start | bytes 786440 | tf_op jit(solution)/shard_map/ppermute | solution.py:465
  3.6 1.7 %shard_map.47 = (f32[4,136,512]{2,1,0:T(8,128)S(1)}, f32[4,136,512]{2,1,0:T(8,128)S(1)}, f32[4,128,512]{2,1,0:T(8,128)S(1)}, f32[4,128,512]{2,1,0:T(8,128)S(1)},...) custom-call(f32[4,128,512]{2,1,0:T(8,128)} %initial.3, f32[4,128,512]{2,1,0:T(8,128)} %kappa.3, ...), custom_call_target="tpu_custom_call" | custom-call | flops 1000000000 | bytes 3000000 | tf_op jit(solution)/shard_map/pallas_call | solution.py:467
  5.4 1.3 %collective-permute-start = (f32[16,4,512]{2,1,0:T(4,128)S(1)}, f32[16,4,512]{2,1,0:T(4,128)S(1)}, u32[]{:S(2)}, u32[]{:S(2)}) collective-permute-start(f32[16,4,512]{2,1,0:T(4,128)S(1)} %get-tuple-element.47), channel_id=1, source_target_pairs={{0,1},{1,0},{2,3},{3,2},{4,5},{5,4},{6,7},{7,6},{8,9},{9,8},{10,11... | collective-permute-start | bytes 393224 | tf_op jit(solution)/shard_map/ppermute | solution.py:476
  6.7 0.3 %collective-permute-start.1 = (f32[128,512]{1,0:T(8,128)S(1)}, f32[128,512]{1,0:T(8,128)S(1)}, u32[]{:S(2)}, u32[]{:S(2)}) collective-permute-start(f32[128,512]{1,0:T(8,128)S(1)} %get-tuple-element.51), channel_id=1, source_target_pairs={{2,4},{4,2},{6,8},{8,6},{10,12},{12,10},{14,16},{16,14},{18,20},{2... | collective-permute-start | bytes 786440 | tf_op jit(solution)/shard_map/ppermute | solution.py:477
  7.0 3.3 %shard_map.48 = (f32[4,136,512]{2,1,0:T(8,128)S(1)}, f32[4,136,512]{2,1,0:T(8,128)S(1)}, f32[4,128,512]{2,1,0:T(8,128)S(1)}, f32[4,128,512]{2,1,0:T(8,128)S(1)},...) custom-call(f32[4,128,512]{2,1,0:T(8,128)} %initial.3, ...), custom_call_target="tpu_custom_call", output_to_operand_aliasing={{0}: (4, {}), {1}: (5, {}), {2}: (6, {}), {3}: (7, {}), {4}... | custom-call | flops 20000000000 | bytes 60000000 | tf_op jit(solution)/shard_map/pallas_call | solution.py:478
  10.3 0.0 collective-permute-done.rest_0_
  10.3 0.5 %shard_map.49 = (f32[4,136,512]{2,1,0:T(8,128)S(1)}, f32[4,136,512]{2,1,0:T(8,128)S(1)}, f32[4,136,512]{2,1,0:T(8,128)S(1)}, f32[3,4,8,512]{3,2,1,0:T(8,128)S(1)}, f32[136,512]{1,0:T(8,128)S(1)}) custom-call(f32[4,136,512]{2,1,0:T(8,128)S(1)} %get-tuple-element.41.u0_in, ...), custom_call_target="tpu_custom_call", output_to_operand_aliasing={{0}: (0, {}), {1}: (1, {}), {2}: (2, {})} | custom-call | flops 1000000000 | bytes 3000000 | tf_op jit(solution)/shard_map/pallas_call | solution.py:487
  10.8 1.5 %collective-permute-start.2 = (f32[136,512]{1,0:T(8,128)S(1)}, f32[136,512]{1,0:T(8,128)S(1)}, u32[]{:S(2)}, u32[]{:S(2)}) collective-permute-start(f32[136,512]{1,0:T(8,128)S(1)} %get-tuple-element.52), channel_id=1, source_target_pairs={{2,4},{4,2},{6,8},{8,6},{10,12},{12,10},{14,16},{16,14},{18,20},{2... | collective-permute-start | bytes 835592 | tf_op jit(solution)/shard_map/ppermute | solution.py:504
  12.3 0.6 %shard_map.50 = (f32[128,512]{1,0:T(8,128)S(1)}, f32[4,136,512]{2,1,0:T(8,128)S(1)}) custom-call(f32[4,136,512]{2,1,0:T(8,128)S(1)} %get-tuple-element.49.u0, f32[4,136,512]{2,1,0:T(8,128)S(1)} %get-tuple-element.50.u1, f32[4,136,512]{2,1,0:T(8,128)S(1)} %get-tuple-element.53.u2, f32[3,4,8,512]{3,2,1,0:T(8,128)S(1)} %get-tuple-element.48.margin, ...), custom_call_target="tpu_custom_call" | custom-call | flops 60000002048 | bytes 180000000 | tf_op jit(solution)/shard_map/pallas_call | solution.py:495
  12.9 0.4 %collective-permute-start.5 = (f32[128,512]{1,0:T(8,128)S(1)}, f32[128,512]{1,0:T(8,128)S(1)}, u32[]{:S(2)}, u32[]{:S(2)}) collective-permute-start(f32[128,512]{1,0:T(8,128)S(1)} %get-tuple-element.63), channel_id=1, source_target_pairs={{2,4},{4,2},{6,8},{8,6},{10,12},{12,10},{14,16},{16,14},{18,20},{2... | collective-permute-start | bytes 786440 | tf_op jit(solution)/shard_map/ppermute | solution.py:505
  13.3 0.0 collective-permute-done.3.near0
  13.3 5.7 %collective-permute-start.4 = (f32[4,136,512]{2,1,0:T(8,128)S(1)}, f32[4,136,512]{2,1,0:T(8,128)S(1)}, u32[]{:S(2)}, u32[]{:S(2)}) collective-permute-start(f32[4,136,512]{2,1,0:T(8,128)S(1)} %get-tuple-element.56), channel_id=1, source_target_pairs={{0,2},{2,0},{4,6},{6,4},{8,10},{10,8},{12,14},{14,12},{16,18},{18,... | collective-permute-start | bytes 3342344 | tf_op jit(solution)/shard_map/ppermute | solution.py:503
  19.1 0.1 shard_map.54.gain
  19.1 2.3 %collective-permute-done.4.beside = f32[4,136,512]{2,1,0:T(8,128)S(1)} collective-permute-done((f32[4,136,512]{2,1,0:T(8,128)S(1)}, f32[4,136,512]{2,1,0:T(8,128)S(1)}, u32[]{:S(2)}, u32[]{:S(2)}) %collective-permute-start.4) | collective-permute-done | bytes 1114144 | tf_op jit(solution)/shard_map/ppermute | solution.py:503
  21.4 2.6 %shard_map.51 = (f32[6,136,512]{2,1,0:T(8,128)S(1)}, f32[128,512]{1,0:T(8,128)S(1)}) custom-call(f32[4,136,512]{2,1,0:T(8,128)S(1)} %get-tuple-element.49.u0, f32[4,136,512]{2,1,0:T(8,128)S(1)} %get-tuple-element.50.u1, f32[3,4,8,512]{3,2,1,0:T(8,128)S(1)} %get-tuple-element.48.margin, f32[4,128,512]{2,1,0:T(8,128)S(1)} %get-tuple-element.44.kappa, ...), custom_call_target="tpu_custom_call" | custom-call | tf_op jit(solution)/shard_map/pallas_call | solution.py:507
  24.0 0.0 collective-permute-done.1.near1
  24.0 0.9 %shard_map.52 = (f32[4,128,512]{2,1,0:T(8,128)}, f32[2,136,512]{2,1,0:T(8,128)S(1)}, f32[128,512]{1,0:T(8,128)S(1)}) custom-call(f32[4,128,512]{2,1,0:T(8,128)S(1)} %get-tuple-element.44.kappa, f32[4,128,512]{2,1,0:T(8,128)S(1)} %get-tuple-element.45.velocity, f32[4,128,512]{2,1,0:T(8,128)S(1)} %get-tuple-element.46.rate, ...), custom_call_target="tpu_custom_call" | custom-call | tf_op jit(solution)/shard_map/pallas_call | solution.py:515
  25.0 0.0 collective-permute-done.2.near2
  25.0 1.6 %shard_map.53 = (f32[6,136,512]{2,1,0:T(8,128)S(1)}, f32[2,136,512]{2,1,0:T(8,128)S(1)}, f32[128,512]{1,0:T(8,128)S(1)}, f32[4,128,512]{2,1,0:T(8,128)}, f32[128,512]{1,0:T(8,128)S(1)}) custom-call(f32[3,4,8,512]{3,2,1,0:T(8,128)S(1)} %get-tuple-element.48.margin, ...), custom_call_target="tpu_custom_call", output_to_operand_aliasing={{0}: (8, {}), {1}: (9, {}), {2}: (10, {}), {3}: (11, {})} | custom-call | tf_op jit(solution)/shard_map/pallas_call | solution.py:523
  26.6 1.7 %collective-permute-done.5.near3 = f32[128,512]{1,0:T(8,128)S(1)} collective-permute-done((f32[128,512]{1,0:T(8,128)S(1)}, f32[128,512]{1,0:T(8,128)S(1)}, u32[]{:S(2)}, u32[]{:S(2)}) %collective-permute-start.5) | collective-permute-done | bytes 262176 | tf_op jit(solution)/shard_map/ppermute | solution.py:505
  28.3 0.7 %shard_map.55 = f32[4,128,512]{2,1,0:T(8,128)} custom-call(f32[128,512]{1,0:T(8,128)S(1)} %get-tuple-element.62.base, f32[128,512]{1,0:T(8,128)S(1)} %shard_map.54.gain, f32[128,512]{1,0:T(8,128)S(1)} %collective-permute-done.5.near3, f32[4,128,512]{2,1,0:T(8,128)} %get-tuple-element.64.out_in), custom_call_target="tpu_custom_call", output_to_operand_aliasing={{}: (3, {})} | custom-call | tf_op jit(solution)/shard_map/pallas_call | solution.py:532
Async XLA Ops:
  1.0 12.4 %collective-permute-start.3 = (f32[128,512]{1,0:T(8,128)S(1)}, f32[128,512]{1,0:T(8,128)S(1)}, u32[]{:S(2)}, u32[]{:S(2)}) collective-permute-start(f32[128,512]{1,0:T(8,128)S(1)} %shard_map.46), channel_id=1, source_target_pairs={{2,4},{4,2},{6,8},{8,6},{10,12},{12,10},{14,16},{16,14},{18,20},{2... | collective-permute-start | bytes 786440 | tf_op jit(solution)/shard_map/ppermute | solution.py:465
  5.4 4.9 %collective-permute-start = (f32[16,4,512]{2,1,0:T(4,128)S(1)}, f32[16,4,512]{2,1,0:T(4,128)S(1)}, u32[]{:S(2)}, u32[]{:S(2)}) collective-permute-start(f32[16,4,512]{2,1,0:T(4,128)S(1)} %get-tuple-element.47), channel_id=1, source_target_pairs={{0,1},{1,0},{2,3},{3,2},{4,5},{5,4},{6,7},{7,6},{8,9},{9,8},{10,11... | collective-permute-start | bytes 393224 | tf_op jit(solution)/shard_map/ppermute | solution.py:476
  6.7 17.3 %collective-permute-start.1 = (f32[128,512]{1,0:T(8,128)S(1)}, f32[128,512]{1,0:T(8,128)S(1)}, u32[]{:S(2)}, u32[]{:S(2)}) collective-permute-start(f32[128,512]{1,0:T(8,128)S(1)} %get-tuple-element.51), channel_id=1, source_target_pairs={{2,4},{4,2},{6,8},{8,6},{10,12},{12,10},{14,16},{16,14},{18,20},{2... | collective-permute-start | bytes 786440 | tf_op jit(solution)/shard_map/ppermute | solution.py:477
  10.8 14.1 %collective-permute-start.2 = (f32[136,512]{1,0:T(8,128)S(1)}, f32[136,512]{1,0:T(8,128)S(1)}, u32[]{:S(2)}, u32[]{:S(2)}) collective-permute-start(f32[136,512]{1,0:T(8,128)S(1)} %get-tuple-element.52), channel_id=1, source_target_pairs={{2,4},{4,2},{6,8},{8,6},{10,12},{12,10},{14,16},{16,14},{18,20},{2... | collective-permute-start | bytes 835592 | tf_op jit(solution)/shard_map/ppermute | solution.py:504
  12.9 15.3 %collective-permute-start.5 = (f32[128,512]{1,0:T(8,128)S(1)}, f32[128,512]{1,0:T(8,128)S(1)}, u32[]{:S(2)}, u32[]{:S(2)}) collective-permute-start(f32[128,512]{1,0:T(8,128)S(1)} %get-tuple-element.63), channel_id=1, source_target_pairs={{2,4},{4,2},{6,8},{8,6},{10,12},{12,10},{14,16},{16,14},{18,20},{2... | collective-permute-start | bytes 786440 | tf_op jit(solution)/shard_map/ppermute | solution.py:505
  13.3 8.1 %collective-permute-start.4 = (f32[4,136,512]{2,1,0:T(8,128)S(1)}, f32[4,136,512]{2,1,0:T(8,128)S(1)}, u32[]{:S(2)}, u32[]{:S(2)}) collective-permute-start(f32[4,136,512]{2,1,0:T(8,128)S(1)} %get-tuple-element.56), channel_id=1, source_target_pairs={{0,2},{2,0},{4,6},{6,4},{8,10},{10,8},{12,14},{14,12},{16,18},{18,... | collective-permute-start | bytes 3342344 | tf_op jit(solution)/shard_map/ppermute | solution.py:503

commit v6 on v5

--- a/solution.py
+++ b/solution.py
@@ -174,10 +174,15 @@
 
 def inner_kernel(initial, kappa, velocity, rate, u0_in, u1_in, kappa_in, velocity_in, rate_in,
                  u0, u1, kappa_v, velocity_v, rate_v, u2, sems):
-    del u0_in, u1_in, kappa_in, velocity_in, rate_in
     odd = parity("gx")
+    for d in (0, 1):
+        u0[plane_at(d, odd)] = u0_in[plane_at(d, odd)]
+    for now, before in ((u1, u1_in), (kappa_v, kappa_in), (velocity_v, velocity_in), (rate_v, rate_in)):
+        now[plane_at(0, odd)] = before[plane_at(0, odd)]
     planes, rows = initial.shape[:2]
     own_rows = pl.ds(0, rows)
+    for d in range(2, planes):
+        u0[plane_at(d, odd), rows:] = jnp.zeros(u0.shape[1:], jnp.float32)[rows:]
     copies = {}
     for d in range(2, planes):
         p = plane_at(d, odd)
@@ -208,8 +213,10 @@
 
 
 def first_kernel(n_halo, u0_in, u1_in, u2_in, kappa, velocity, rate, *rest):
-    del u0_in, u1_in, u2_in
     halos, (u0, u1, u2, margin, message) = rest[:n_halo], rest[n_halo:]
+    u0[...] = u0_in[...]
+    u1[...] = u1_in[...]
+    u2[...] = u2_in[...]
     odd, odd_y = parity("gx"), parity("gy")
     rows = kappa.shape[1]
     for f in range(4):
@@ -357,7 +364,10 @@
 
 def fourth_kernel(n_halo, margin, kappa, velocity, rate, u0, u1, near1, near2, state_in, more_in, final2_in, out_in,
                   state, more, final2, out, base, v3, edges, final1, sems):
-    del state_in, more_in, final2_in, out_in
+    state[...] = state_in[...]
+    more[...] = more_in[...]
+    final2[...] = final2_in[...]
+    del out_in
     odd, odd_y = parity("gx"), parity("gy")
     rows, lanes = kappa.shape[1:]
     tiles = rows // ROWS

time: 29.2 us -> 29.8 us (1.021)
  Pallas kernels: 13 us -> 13.9 us
  waiting for transfers between devices: 4.02 us -> 3.67 us
    pallas_call x1, Pallas kernels: 0.5 us -> 0.95 us  [local(): call(functools.partial(first_kernel, n_halo), [wide, wide, wide, f32(3, p...]
    pallas_call x1, Pallas kernels: 1.61 us -> 1.96 us  [local(): call(functools.partial(fourth_kernel, n_halo), [f32(len(STATE), full, lan...]
    ppermute x1, waiting for transfers between devices: 1.69 us -> 1.35 us  [local(): near3 = lax.ppermute(message3, 'gx', chips)]
  transfers between devices with their start and end apart: 6 -> 6, of which waited for: 2 -> 2; matrix products, arithmetic and copies ran while one was open for 0% -> 0% of each run, Pallas kernels for 39% -> 41%
where the time goes in v6:
time: 29.8 us; the launch traced here: 29.6 us
  Pallas kernels  13.9 us (47%)
  starting transfers between devices  11.9 us (40%)
  waiting for transfers between devices  3.67 us (12%)
    ppermute x1, starting transfers between devices, local(): beside = lax.ppermute(beside, 'gx', cores)  5.72 us
    pallas_call x1, Pallas kernels, local(): call(inner_kernel, [wide, wide, block, block, block, wide], [HBM] * 4 + [...  3.41 us
    ppermute x1, starting transfers between devices, local(): near0 = lax.ppermute(message0, 'gx', chips)  2.67 us
    pallas_call x1, Pallas kernels, local(): call(far_kernel, [f32(len(STATE), full, lanes), plane], [VMEM] * 8, [VMEM...  2.56 us
    ppermute x1, waiting for transfers between devices, local(): beside = lax.ppermute(beside, 'gx', cores)  2.31 us
    pallas_call x1, Pallas kernels, local(): call(functools.partial(fourth_kernel, n_halo), [f32(len(STATE), full, lan...  1.96 us
    pallas_call x1, Pallas kernels, local(): call(functools.partial(load_kernel, n_halo), [wide, wide, block, block, b...  1.74 us
    ppermute x1, starting transfers between devices, local(): near2 = lax.ppermute(message2, 'gx', chips)  1.49 us
  transfers between devices with their start and end apart: 6, of which 2 were waited for; matrix products, arithmetic and copies ran while one was open for 0% of the time, Pallas kernels for 41%

profile of v6, /device:TPU:1, one launch (start us, length us, event | category | flops | bytes accessed | tf_op | source)
XLA Modules:
  0.0 29.6 jit_solution(2886038099267959506)
XLA Ops:
  0.0 1.0 %shard_map.46 = f32[128,512]{1,0:T(8,128)S(1)} custom-call(f32[4,128,512]{2,1,0:T(8,128)} %initial.3), custom_call_target="tpu_custom_call" | custom-call | flops 1000000000 | bytes 3000000 | tf_op jit(solution)/shard_map/pallas_call | solution.py:474
  1.0 2.7 %collective-permute-start.3 = (f32[128,512]{1,0:T(8,128)S(1)}, f32[128,512]{1,0:T(8,128)S(1)}, u32[]{:S(2)}, u32[]{:S(2)}) collective-permute-start(f32[128,512]{1,0:T(8,128)S(1)} %shard_map.46), channel_id=1, source_target_pairs={{2,4},{4,2},{6,8},{8,6},{10,12},{12,10},{14,16},{16,14},{18,20},{2... | collective-permute-start | bytes 786440 | tf_op jit(solution)/shard_map/ppermute | solution.py:475
  3.6 1.7 %shard_map.47 = (f32[4,136,512]{2,1,0:T(8,128)S(1)}, f32[4,136,512]{2,1,0:T(8,128)S(1)}, f32[4,128,512]{2,1,0:T(8,128)S(1)}, f32[4,128,512]{2,1,0:T(8,128)S(1)},...) custom-call(f32[4,128,512]{2,1,0:T(8,128)} %initial.3, f32[4,128,512]{2,1,0:T(8,128)} %kappa.3, ...), custom_call_target="tpu_custom_call" | custom-call | flops 1000000000 | bytes 3000000 | tf_op jit(solution)/shard_map/pallas_call | solution.py:477
  5.4 1.3 %collective-permute-start = (f32[16,4,512]{2,1,0:T(4,128)S(1)}, f32[16,4,512]{2,1,0:T(4,128)S(1)}, u32[]{:S(2)}, u32[]{:S(2)}) collective-permute-start(f32[16,4,512]{2,1,0:T(4,128)S(1)} %get-tuple-element.47), channel_id=1, source_target_pairs={{0,1},{1,0},{2,3},{3,2},{4,5},{5,4},{6,7},{7,6},{8,9},{9,8},{10,11... | collective-permute-start | bytes 393224 | tf_op jit(solution)/shard_map/ppermute | solution.py:486
  6.7 0.3 %collective-permute-start.1 = (f32[128,512]{1,0:T(8,128)S(1)}, f32[128,512]{1,0:T(8,128)S(1)}, u32[]{:S(2)}, u32[]{:S(2)}) collective-permute-start(f32[128,512]{1,0:T(8,128)S(1)} %get-tuple-element.51), channel_id=1, source_target_pairs={{2,4},{4,2},{6,8},{8,6},{10,12},{12,10},{14,16},{16,14},{18,20},{2... | collective-permute-start | bytes 786440 | tf_op jit(solution)/shard_map/ppermute | solution.py:487
  7.0 3.4 %shard_map.48 = (f32[4,136,512]{2,1,0:T(8,128)S(1)}, f32[4,136,512]{2,1,0:T(8,128)S(1)}, f32[4,128,512]{2,1,0:T(8,128)S(1)}, f32[4,128,512]{2,1,0:T(8,128)S(1)},...) custom-call(f32[4,128,512]{2,1,0:T(8,128)} %initial.3, ...), custom_call_target="tpu_custom_call", output_to_operand_aliasing={{0}: (4, {}), {1}: (5, {}), {2}: (6, {}), {3}: (7, {}), {4}... | custom-call | flops 20000000000 | bytes 60000000 | tf_op jit(solution)/shard_map/pallas_call | solution.py:488
  10.4 0.0 collective-permute-done.rest_0_
  10.4 1.0 %shard_map.49 = (f32[4,136,512]{2,1,0:T(8,128)S(1)}, f32[4,136,512]{2,1,0:T(8,128)S(1)}, f32[4,136,512]{2,1,0:T(8,128)S(1)}, f32[3,4,8,512]{3,2,1,0:T(8,128)S(1)}, f32[136,512]{1,0:T(8,128)S(1)}) custom-call(f32[4,136,512]{2,1,0:T(8,128)S(1)} %get-tuple-element.41.u0_in, ...), custom_call_target="tpu_custom_call", output_to_operand_aliasing={{0}: (0, {}), {1}: (1, {}), {2}: (2, {})} | custom-call | flops 1000000000 | bytes 3000000 | tf_op jit(solution)/shard_map/pallas_call | solution.py:497
  11.4 1.5 %collective-permute-start.2 = (f32[136,512]{1,0:T(8,128)S(1)}, f32[136,512]{1,0:T(8,128)S(1)}, u32[]{:S(2)}, u32[]{:S(2)}) collective-permute-start(f32[136,512]{1,0:T(8,128)S(1)} %get-tuple-element.52), channel_id=1, source_target_pairs={{2,4},{4,2},{6,8},{8,6},{10,12},{12,10},{14,16},{16,14},{18,20},{2... | collective-permute-start | bytes 835592 | tf_op jit(solution)/shard_map/ppermute | solution.py:514
  12.9 0.6 %shard_map.50 = (f32[128,512]{1,0:T(8,128)S(1)}, f32[4,136,512]{2,1,0:T(8,128)S(1)}) custom-call(f32[4,136,512]{2,1,0:T(8,128)S(1)} %get-tuple-element.49.u0, f32[4,136,512]{2,1,0:T(8,128)S(1)} %get-tuple-element.50.u1, f32[4,136,512]{2,1,0:T(8,128)S(1)} %get-tuple-element.53.u2, f32[3,4,8,512]{3,2,1,0:T(8,128)S(1)} %get-tuple-element.48.margin, ...), custom_call_target="tpu_custom_call" | custom-call | flops 60000002048 | bytes 180000000 | tf_op jit(solution)/shard_map/pallas_call | solution.py:505
  13.5 0.4 %collective-permute-start.5 = (f32[128,512]{1,0:T(8,128)S(1)}, f32[128,512]{1,0:T(8,128)S(1)}, u32[]{:S(2)}, u32[]{:S(2)}) collective-permute-start(f32[128,512]{1,0:T(8,128)S(1)} %get-tuple-element.63), channel_id=1, source_target_pairs={{2,4},{4,2},{6,8},{8,6},{10,12},{12,10},{14,16},{16,14},{18,20},{2... | collective-permute-start | bytes 786440 | tf_op jit(solution)/shard_map/ppermute | solution.py:515
  13.9 0.0 collective-permute-done.3.near0
  13.9 5.7 %collective-permute-start.4 = (f32[4,136,512]{2,1,0:T(8,128)S(1)}, f32[4,136,512]{2,1,0:T(8,128)S(1)}, u32[]{:S(2)}, u32[]{:S(2)}) collective-permute-start(f32[4,136,512]{2,1,0:T(8,128)S(1)} %get-tuple-element.56), channel_id=1, source_target_pairs={{0,2},{2,0},{4,6},{6,4},{8,10},{10,8},{12,14},{14,12},{16,18},{18,... | collective-permute-start | bytes 3342344 | tf_op jit(solution)/shard_map/ppermute | solution.py:513
  19.6 0.1 shard_map.54.gain
  19.7 2.3 %collective-permute-done.4.beside = f32[4,136,512]{2,1,0:T(8,128)S(1)} collective-permute-done((f32[4,136,512]{2,1,0:T(8,128)S(1)}, f32[4,136,512]{2,1,0:T(8,128)S(1)}, u32[]{:S(2)}, u32[]{:S(2)}) %collective-permute-start.4) | collective-permute-done | bytes 1114144 | tf_op jit(solution)/shard_map/ppermute | solution.py:513
  22.0 2.6 %shard_map.51 = (f32[6,136,512]{2,1,0:T(8,128)S(1)}, f32[128,512]{1,0:T(8,128)S(1)}) custom-call(f32[4,136,512]{2,1,0:T(8,128)S(1)} %get-tuple-element.49.u0, f32[4,136,512]{2,1,0:T(8,128)S(1)} %get-tuple-element.50.u1, f32[3,4,8,512]{3,2,1,0:T(8,128)S(1)} %get-tuple-element.48.margin, f32[4,128,512]{2,1,0:T(8,128)S(1)} %get-tuple-element.44.kappa, ...), custom_call_target="tpu_custom_call" | custom-call | tf_op jit(solution)/shard_map/pallas_call | solution.py:517
  24.6 0.0 collective-permute-done.1.near1
  24.6 0.9 %shard_map.52 = (f32[4,128,512]{2,1,0:T(8,128)}, f32[2,136,512]{2,1,0:T(8,128)S(1)}, f32[128,512]{1,0:T(8,128)S(1)}) custom-call(f32[4,128,512]{2,1,0:T(8,128)S(1)} %get-tuple-element.44.kappa, f32[4,128,512]{2,1,0:T(8,128)S(1)} %get-tuple-element.45.velocity, f32[4,128,512]{2,1,0:T(8,128)S(1)} %get-tuple-element.46.rate, ...), custom_call_target="tpu_custom_call" | custom-call | tf_op jit(solution)/shard_map/pallas_call | solution.py:525
  25.5 0.0 collective-permute-done.2.near2
  25.5 2.0 %shard_map.53 = (f32[6,136,512]{2,1,0:T(8,128)S(1)}, f32[2,136,512]{2,1,0:T(8,128)S(1)}, f32[128,512]{1,0:T(8,128)S(1)}, f32[4,128,512]{2,1,0:T(8,128)}, f32[128,512]{1,0:T(8,128)S(1)}) custom-call(f32[3,4,8,512]{3,2,1,0:T(8,128)S(1)} %get-tuple-element.48.margin, ...), custom_call_target="tpu_custom_call", output_to_operand_aliasing={{0}: (8, {}), {1}: (9, {}), {2}: (10, {}), {3}: (11, {})} | custom-call | tf_op jit(solution)/shard_map/pallas_call | solution.py:533
  27.5 1.3 %collective-permute-done.5.near3 = f32[128,512]{1,0:T(8,128)S(1)} collective-permute-done((f32[128,512]{1,0:T(8,128)S(1)}, f32[128,512]{1,0:T(8,128)S(1)}, u32[]{:S(2)}, u32[]{:S(2)}) %collective-permute-start.5) | collective-permute-done | bytes 262176 | tf_op jit(solution)/shard_map/ppermute | solution.py:515
  28.8 0.7 %shard_map.55 = f32[4,128,512]{2,1,0:T(8,128)} custom-call(f32[128,512]{1,0:T(8,128)S(1)} %get-tuple-element.62.base, f32[128,512]{1,0:T(8,128)S(1)} %shard_map.54.gain, f32[128,512]{1,0:T(8,128)S(1)} %collective-permute-done.5.near3, f32[4,128,512]{2,1,0:T(8,128)} %get-tuple-element.64.out_in), custom_call_target="tpu_custom_call", output_to_operand_aliasing={{}: (3, {})} | custom-call | tf_op jit(solution)/shard_map/pallas_call | solution.py:542
Async XLA Ops:
  1.0 12.9 %collective-permute-start.3 = (f32[128,512]{1,0:T(8,128)S(1)}, f32[128,512]{1,0:T(8,128)S(1)}, u32[]{:S(2)}, u32[]{:S(2)}) collective-permute-start(f32[128,512]{1,0:T(8,128)S(1)} %shard_map.46), channel_id=1, source_target_pairs={{2,4},{4,2},{6,8},{8,6},{10,12},{12,10},{14,16},{16,14},{18,20},{2... | collective-permute-start | bytes 786440 | tf_op jit(solution)/shard_map/ppermute | solution.py:475
  5.4 5.0 %collective-permute-start = (f32[16,4,512]{2,1,0:T(4,128)S(1)}, f32[16,4,512]{2,1,0:T(4,128)S(1)}, u32[]{:S(2)}, u32[]{:S(2)}) collective-permute-start(f32[16,4,512]{2,1,0:T(4,128)S(1)} %get-tuple-element.47), channel_id=1, source_target_pairs={{0,1},{1,0},{2,3},{3,2},{4,5},{5,4},{6,7},{7,6},{8,9},{9,8},{10,11... | collective-permute-start | bytes 393224 | tf_op jit(solution)/shard_map/ppermute | solution.py:486
  6.7 17.9 %collective-permute-start.1 = (f32[128,512]{1,0:T(8,128)S(1)}, f32[128,512]{1,0:T(8,128)S(1)}, u32[]{:S(2)}, u32[]{:S(2)}) collective-permute-start(f32[128,512]{1,0:T(8,128)S(1)} %get-tuple-element.51), channel_id=1, source_target_pairs={{2,4},{4,2},{6,8},{8,6},{10,12},{12,10},{14,16},{16,14},{18,20},{2... | collective-permute-start | bytes 786440 | tf_op jit(solution)/shard_map/ppermute | solution.py:487
  11.4 14.1 %collective-permute-start.2 = (f32[136,512]{1,0:T(8,128)S(1)}, f32[136,512]{1,0:T(8,128)S(1)}, u32[]{:S(2)}, u32[]{:S(2)}) collective-permute-start(f32[136,512]{1,0:T(8,128)S(1)} %get-tuple-element.52), channel_id=1, source_target_pairs={{2,4},{4,2},{6,8},{8,6},{10,12},{12,10},{14,16},{16,14},{18,20},{2... | collective-permute-start | bytes 835592 | tf_op jit(solution)/shard_map/ppermute | solution.py:514
  13.5 15.3 %collective-permute-start.5 = (f32[128,512]{1,0:T(8,128)S(1)}, f32[128,512]{1,0:T(8,128)S(1)}, u32[]{:S(2)}, u32[]{:S(2)}) collective-permute-start(f32[128,512]{1,0:T(8,128)S(1)} %get-tuple-element.63), channel_id=1, source_target_pairs={{2,4},{4,2},{6,8},{8,6},{10,12},{12,10},{14,16},{16,14},{18,20},{2... | collective-permute-start | bytes 786440 | tf_op jit(solution)/shard_map/ppermute | solution.py:515
  13.9 8.1 %collective-permute-start.4 = (f32[4,136,512]{2,1,0:T(8,128)S(1)}, f32[4,136,512]{2,1,0:T(8,128)S(1)}, u32[]{:S(2)}, u32[]{:S(2)}) collective-permute-start(f32[4,136,512]{2,1,0:T(8,128)S(1)} %get-tuple-element.56), channel_id=1, source_target_pairs={{0,2},{2,0},{4,6},{6,4},{8,10},{10,8},{12,14},{14,12},{16,18},{18,... | collective-permute-start | bytes 3342344 | tf_op jit(solution)/shard_map/ppermute | solution.py:513

commit v7 on v5

--- a/solution.py
+++ b/solution.py
@@ -78,7 +78,7 @@
     return out
 
 
-def sweep(odd, wanted, source, coefs, margins, near, distant, sink, inner, edges=()):
+def sweep(odd, wanted, source, coefs, margins, near, distant, sink, inner, edges=(), most=None):
     needed = sorted({e for d in wanted for e in (d - 1, d, d + 1) if 0 <= e <= 3})
     last = source(wanted[0])[0].shape[-2] // ROWS - 1
 
@@ -107,7 +107,7 @@
 
     count = inner[1] - inner[0]
     if count:
-        size = max(n for n in range(1, GROUPS[len(wanted) - 1] + 1) if count % n == 0)
+        size = max(n for n in range(1, (most or GROUPS[len(wanted) - 1]) + 1) if count % n == 0)
 
         def loop(index, carry):
             work([inner[0] + index * size + i for i in range(size)], True)
@@ -162,7 +162,7 @@
         store(message, (), tile, pieces)
 
     coefs = [(ref, ()) for ref in (kappa_v, velocity_v, rate_v)]
-    sweep(odd, [0], lambda d: (u0, (plane_at(d, odd),)), coefs, None, none, none, sink, (0, rows // ROWS))
+    sweep(odd, [0], lambda d: (u0, (plane_at(d, odd),)), coefs, None, none, none, sink, (0, rows // ROWS), most=16)
     for copy in packs:
         copy.wait()
     for f in range(4):
@@ -199,7 +199,7 @@
             copies[0, d + 1].wait()
         for f in range(1, 4):
             copies[f, d].wait()
-        sweep(odd, [d], lambda e: (u0, (plane_at(e, odd),)), coefs, None, none, none, sink, (0, rows // ROWS))
+        sweep(odd, [d], lambda e: (u0, (plane_at(e, odd),)), coefs, None, none, none, sink, (0, rows // ROWS), most=16)
 
     def sink2(d, tile, pieces):
         store(u2, (plane_at(d, odd),), tile, pieces)
@@ -268,7 +268,7 @@
         else:
             store(beside, (3,), tile, pieces)
 
-    sweep(odd, [0, 3], lambda d: (u2, (plane_at(d, odd),)), coefs, margins, none, none, sink, (0, rows // ROWS))
+    sweep(odd, [0, 3], lambda d: (u2, (plane_at(d, odd),)), coefs, margins, none, none, sink, (0, rows // ROWS), most=16)
     beside[3, rows:] = jnp.zeros(beside[3, rows:].shape, jnp.float32)
     for step, field in enumerate((u0, u1, u2)):
         beside[step] = field[plane_at(3, odd)]
@@ -332,7 +332,7 @@
     sweep(odd, [2, 3], source(1), coefs, margins, none, distant(1), sink(2), *edge)
     sweep(odd, [2, 3], source(2), coefs, margins, none, distant(2), sink(3), own_rows)
     sweep(odd, [3], source(2), coefs, margins, none, distant(2), sink(3), *edge)
-    sweep(odd, [3], source(3), coefs, margins, none, distant(3), finish, own_rows)
+    sweep(odd, [3], source(3), coefs, margins, none, distant(3), finish, own_rows, most=16)
 
 
 def near_kernel(kappa, velocity, rate, u1, near1, state, final3, out, more, final2, sem):

time: 29.2 us -> 29.1 us (level)
  transfers between devices with their start and end apart: 6 -> 6, of which waited for: 2 -> 2; matrix products, arithmetic and copies ran while one was open for 0% -> 0% of each run, Pallas kernels for 39% -> 38%
where the time goes in v7:
time: 29.1 us; the launch traced here: 28.9 us
  Pallas kernels  12.8 us (44%)
  starting transfers between devices  11.9 us (41%)
  waiting for transfers between devices  4.14 us (14%)
    ppermute x1, starting transfers between devices, local(): beside = lax.ppermute(beside, 'gx', cores)  5.73 us
    pallas_call x1, Pallas kernels, local(): call(inner_kernel, [wide, wide, block, block, block, wide], [HBM] * 4 + [...  3.22 us
    ppermute x1, starting transfers between devices, local(): near0 = lax.ppermute(message0, 'gx', chips)  2.67 us
    pallas_call x1, Pallas kernels, local(): call(far_kernel, [f32(len(STATE), full, lanes), plane], [VMEM] * 8, [VMEM...  2.48 us
    ppermute x1, waiting for transfers between devices, local(): beside = lax.ppermute(beside, 'gx', cores)  2.31 us
    ppermute x1, waiting for transfers between devices, local(): near3 = lax.ppermute(message3, 'gx', chips)  1.81 us
    pallas_call x1, Pallas kernels, local(): call(functools.partial(load_kernel, n_halo), [wide, wide, block, block, b...  1.7 us
    pallas_call x1, Pallas kernels, local(): call(functools.partial(fourth_kernel, n_halo), [f32(len(STATE), full, lan...  1.61 us
  transfers between devices with their start and end apart: 6, of which 2 were waited for; matrix products, arithmetic and copies ran while one was open for 0% of the time, Pallas kernels for 38%

profile of v7, /device:TPU:1, one launch (start us, length us, event | category | flops | bytes accessed | tf_op | source)
XLA Modules:
  0.0 28.9 jit_solution(13526704432225496799)
XLA Ops:
  0.0 1.0 %shard_map.46 = f32[128,512]{1,0:T(8,128)S(1)} custom-call(f32[4,128,512]{2,1,0:T(8,128)} %initial.3), custom_call_target="tpu_custom_call" | custom-call | flops 1000000000 | bytes 3000000 | tf_op jit(solution)/shard_map/pallas_call | solution.py:464
  1.0 2.7 %collective-permute-start.3 = (f32[128,512]{1,0:T(8,128)S(1)}, f32[128,512]{1,0:T(8,128)S(1)}, u32[]{:S(2)}, u32[]{:S(2)}) collective-permute-start(f32[128,512]{1,0:T(8,128)S(1)} %shard_map.46), channel_id=1, source_target_pairs={{2,4},{4,2},{6,8},{8,6},{10,12},{12,10},{14,16},{16,14},{18,20},{2... | collective-permute-start | bytes 786440 | tf_op jit(solution)/shard_map/ppermute | solution.py:465
  3.6 1.7 %shard_map.47 = (f32[4,136,512]{2,1,0:T(8,128)S(1)}, f32[4,136,512]{2,1,0:T(8,128)S(1)}, f32[4,128,512]{2,1,0:T(8,128)S(1)}, f32[4,128,512]{2,1,0:T(8,128)S(1)},...) custom-call(f32[4,128,512]{2,1,0:T(8,128)} %initial.3, f32[4,128,512]{2,1,0:T(8,128)} %kappa.3, ...), custom_call_target="tpu_custom_call" | custom-call | flops 1000000000 | bytes 3000000 | tf_op jit(solution)/shard_map/pallas_call | solution.py:467
  5.4 1.3 %collective-permute-start = (f32[16,4,512]{2,1,0:T(4,128)S(1)}, f32[16,4,512]{2,1,0:T(4,128)S(1)}, u32[]{:S(2)}, u32[]{:S(2)}) collective-permute-start(f32[16,4,512]{2,1,0:T(4,128)S(1)} %get-tuple-element.47), channel_id=1, source_target_pairs={{0,1},{1,0},{2,3},{3,2},{4,5},{5,4},{6,7},{7,6},{8,9},{9,8},{10,11... | collective-permute-start | bytes 393224 | tf_op jit(solution)/shard_map/ppermute | solution.py:476
  6.7 0.3 %collective-permute-start.1 = (f32[128,512]{1,0:T(8,128)S(1)}, f32[128,512]{1,0:T(8,128)S(1)}, u32[]{:S(2)}, u32[]{:S(2)}) collective-permute-start(f32[128,512]{1,0:T(8,128)S(1)} %get-tuple-element.51), channel_id=1, source_target_pairs={{2,4},{4,2},{6,8},{8,6},{10,12},{12,10},{14,16},{16,14},{18,20},{2... | collective-permute-start | bytes 786440 | tf_op jit(solution)/shard_map/ppermute | solution.py:477
  7.0 3.2 %shard_map.48 = (f32[4,136,512]{2,1,0:T(8,128)S(1)}, f32[4,136,512]{2,1,0:T(8,128)S(1)}, f32[4,128,512]{2,1,0:T(8,128)S(1)}, f32[4,128,512]{2,1,0:T(8,128)S(1)},...) custom-call(f32[4,128,512]{2,1,0:T(8,128)} %initial.3, ...), custom_call_target="tpu_custom_call", output_to_operand_aliasing={{0}: (4, {}), {1}: (5, {}), {2}: (6, {}), {3}: (7, {}), {4}... | custom-call | flops 20000000000 | bytes 60000000 | tf_op jit(solution)/shard_map/pallas_call | solution.py:478
  10.2 0.0 collective-permute-done.rest_0_
  10.2 0.5 %shard_map.49 = (f32[4,136,512]{2,1,0:T(8,128)S(1)}, f32[4,136,512]{2,1,0:T(8,128)S(1)}, f32[4,136,512]{2,1,0:T(8,128)S(1)}, f32[3,4,8,512]{3,2,1,0:T(8,128)S(1)}, f32[136,512]{1,0:T(8,128)S(1)}) custom-call(f32[4,136,512]{2,1,0:T(8,128)S(1)} %get-tuple-element.41.u0_in, ...), custom_call_target="tpu_custom_call", output_to_operand_aliasing={{0}: (0, {}), {1}: (1, {}), {2}: (2, {})} | custom-call | flops 1000000000 | bytes 3000000 | tf_op jit(solution)/shard_map/pallas_call | solution.py:487
  10.7 1.5 %collective-permute-start.2 = (f32[136,512]{1,0:T(8,128)S(1)}, f32[136,512]{1,0:T(8,128)S(1)}, u32[]{:S(2)}, u32[]{:S(2)}) collective-permute-start(f32[136,512]{1,0:T(8,128)S(1)} %get-tuple-element.52), channel_id=1, source_target_pairs={{2,4},{4,2},{6,8},{8,6},{10,12},{12,10},{14,16},{16,14},{18,20},{2... | collective-permute-start | bytes 835592 | tf_op jit(solution)/shard_map/ppermute | solution.py:504
  12.2 0.6 %shard_map.50 = (f32[128,512]{1,0:T(8,128)S(1)}, f32[4,136,512]{2,1,0:T(8,128)S(1)}) custom-call(f32[4,136,512]{2,1,0:T(8,128)S(1)} %get-tuple-element.49.u0, f32[4,136,512]{2,1,0:T(8,128)S(1)} %get-tuple-element.50.u1, f32[4,136,512]{2,1,0:T(8,128)S(1)} %get-tuple-element.53.u2, f32[3,4,8,512]{3,2,1,0:T(8,128)S(1)} %get-tuple-element.48.margin, ...), custom_call_target="tpu_custom_call" | custom-call | flops 60000002048 | bytes 180000000 | tf_op jit(solution)/shard_map/pallas_call | solution.py:495
  12.8 0.4 %collective-permute-start.5 = (f32[128,512]{1,0:T(8,128)S(1)}, f32[128,512]{1,0:T(8,128)S(1)}, u32[]{:S(2)}, u32[]{:S(2)}) collective-permute-start(f32[128,512]{1,0:T(8,128)S(1)} %get-tuple-element.63), channel_id=1, source_target_pairs={{2,4},{4,2},{6,8},{8,6},{10,12},{12,10},{14,16},{16,14},{18,20},{2... | collective-permute-start | bytes 786440 | tf_op jit(solution)/shard_map/ppermute | solution.py:505
  13.2 0.0 collective-permute-done.3.near0
  13.2 5.7 %collective-permute-start.4 = (f32[4,136,512]{2,1,0:T(8,128)S(1)}, f32[4,136,512]{2,1,0:T(8,128)S(1)}, u32[]{:S(2)}, u32[]{:S(2)}) collective-permute-start(f32[4,136,512]{2,1,0:T(8,128)S(1)} %get-tuple-element.56), channel_id=1, source_target_pairs={{0,2},{2,0},{4,6},{6,4},{8,10},{10,8},{12,14},{14,12},{16,18},{18,... | collective-permute-start | bytes 3342344 | tf_op jit(solution)/shard_map/ppermute | solution.py:503
  18.9 0.1 shard_map.54.gain
  19.0 2.3 %collective-permute-done.4.beside = f32[4,136,512]{2,1,0:T(8,128)S(1)} collective-permute-done((f32[4,136,512]{2,1,0:T(8,128)S(1)}, f32[4,136,512]{2,1,0:T(8,128)S(1)}, u32[]{:S(2)}, u32[]{:S(2)}) %collective-permute-start.4) | collective-permute-done | bytes 1114144 | tf_op jit(solution)/shard_map/ppermute | solution.py:503
  21.3 2.5 %shard_map.51 = (f32[6,136,512]{2,1,0:T(8,128)S(1)}, f32[128,512]{1,0:T(8,128)S(1)}) custom-call(f32[4,136,512]{2,1,0:T(8,128)S(1)} %get-tuple-element.49.u0, f32[4,136,512]{2,1,0:T(8,128)S(1)} %get-tuple-element.50.u1, f32[3,4,8,512]{3,2,1,0:T(8,128)S(1)} %get-tuple-element.48.margin, f32[4,128,512]{2,1,0:T(8,128)S(1)} %get-tuple-element.44.kappa, ...), custom_call_target="tpu_custom_call" | custom-call | tf_op jit(solution)/shard_map/pallas_call | solution.py:507
  23.8 0.0 collective-permute-done.1.near1
  23.8 0.9 %shard_map.52 = (f32[4,128,512]{2,1,0:T(8,128)}, f32[2,136,512]{2,1,0:T(8,128)S(1)}, f32[128,512]{1,0:T(8,128)S(1)}) custom-call(f32[4,128,512]{2,1,0:T(8,128)S(1)} %get-tuple-element.44.kappa, f32[4,128,512]{2,1,0:T(8,128)S(1)} %get-tuple-element.45.velocity, f32[4,128,512]{2,1,0:T(8,128)S(1)} %get-tuple-element.46.rate, ...), custom_call_target="tpu_custom_call" | custom-call | tf_op jit(solution)/shard_map/pallas_call | solution.py:515
  24.7 0.0 collective-permute-done.2.near2
  24.7 1.6 %shard_map.53 = (f32[6,136,512]{2,1,0:T(8,128)S(1)}, f32[2,136,512]{2,1,0:T(8,128)S(1)}, f32[128,512]{1,0:T(8,128)S(1)}, f32[4,128,512]{2,1,0:T(8,128)}, f32[128,512]{1,0:T(8,128)S(1)}) custom-call(f32[3,4,8,512]{3,2,1,0:T(8,128)S(1)} %get-tuple-element.48.margin, ...), custom_call_target="tpu_custom_call", output_to_operand_aliasing={{0}: (8, {}), {1}: (9, {}), {2}: (10, {}), {3}: (11, {})} | custom-call | tf_op jit(solution)/shard_map/pallas_call | solution.py:523
  26.3 1.8 %collective-permute-done.5.near3 = f32[128,512]{1,0:T(8,128)S(1)} collective-permute-done((f32[128,512]{1,0:T(8,128)S(1)}, f32[128,512]{1,0:T(8,128)S(1)}, u32[]{:S(2)}, u32[]{:S(2)}) %collective-permute-start.5) | collective-permute-done | bytes 262176 | tf_op jit(solution)/shard_map/ppermute | solution.py:505
  28.2 0.7 %shard_map.55 = f32[4,128,512]{2,1,0:T(8,128)} custom-call(f32[128,512]{1,0:T(8,128)S(1)} %get-tuple-element.62.base, f32[128,512]{1,0:T(8,128)S(1)} %shard_map.54.gain, f32[128,512]{1,0:T(8,128)S(1)} %collective-permute-done.5.near3, f32[4,128,512]{2,1,0:T(8,128)} %get-tuple-element.64.out_in), custom_call_target="tpu_custom_call", output_to_operand_aliasing={{}: (3, {})} | custom-call | tf_op jit(solution)/shard_map/pallas_call | solution.py:532
Async XLA Ops:
  1.0 12.2 %collective-permute-start.3 = (f32[128,512]{1,0:T(8,128)S(1)}, f32[128,512]{1,0:T(8,128)S(1)}, u32[]{:S(2)}, u32[]{:S(2)}) collective-permute-start(f32[128,512]{1,0:T(8,128)S(1)} %shard_map.46), channel_id=1, source_target_pairs={{2,4},{4,2},{6,8},{8,6},{10,12},{12,10},{14,16},{16,14},{18,20},{2... | collective-permute-start | bytes 786440 | tf_op jit(solution)/shard_map/ppermute | solution.py:465
  5.4 4.8 %collective-permute-start = (f32[16,4,512]{2,1,0:T(4,128)S(1)}, f32[16,4,512]{2,1,0:T(4,128)S(1)}, u32[]{:S(2)}, u32[]{:S(2)}) collective-permute-start(f32[16,4,512]{2,1,0:T(4,128)S(1)} %get-tuple-element.47), channel_id=1, source_target_pairs={{0,1},{1,0},{2,3},{3,2},{4,5},{5,4},{6,7},{7,6},{8,9},{9,8},{10,11... | collective-permute-start | bytes 393224 | tf_op jit(solution)/shard_map/ppermute | solution.py:476
  6.7 17.1 %collective-permute-start.1 = (f32[128,512]{1,0:T(8,128)S(1)}, f32[128,512]{1,0:T(8,128)S(1)}, u32[]{:S(2)}, u32[]{:S(2)}) collective-permute-start(f32[128,512]{1,0:T(8,128)S(1)} %get-tuple-element.51), channel_id=1, source_target_pairs={{2,4},{4,2},{6,8},{8,6},{10,12},{12,10},{14,16},{16,14},{18,20},{2... | collective-permute-start | bytes 786440 | tf_op jit(solution)/shard_map/ppermute | solution.py:477
  10.7 14.0 %collective-permute-start.2 = (f32[136,512]{1,0:T(8,128)S(1)}, f32[136,512]{1,0:T(8,128)S(1)}, u32[]{:S(2)}, u32[]{:S(2)}) collective-permute-start(f32[136,512]{1,0:T(8,128)S(1)} %get-tuple-element.52), channel_id=1, source_target_pairs={{2,4},{4,2},{6,8},{8,6},{10,12},{12,10},{14,16},{16,14},{18,20},{2... | collective-permute-start | bytes 835592 | tf_op jit(solution)/shard_map/ppermute | solution.py:504
  12.8 15.4 %collective-permute-start.5 = (f32[128,512]{1,0:T(8,128)S(1)}, f32[128,512]{1,0:T(8,128)S(1)}, u32[]{:S(2)}, u32[]{:S(2)}) collective-permute-start(f32[128,512]{1,0:T(8,128)S(1)} %get-tuple-element.63), channel_id=1, source_target_pairs={{2,4},{4,2},{6,8},{8,6},{10,12},{12,10},{14,16},{16,14},{18,20},{2... | collective-permute-start | bytes 786440 | tf_op jit(solution)/shard_map/ppermute | solution.py:505
  13.2 8.1 %collective-permute-start.4 = (f32[4,136,512]{2,1,0:T(8,128)S(1)}, f32[4,136,512]{2,1,0:T(8,128)S(1)}, u32[]{:S(2)}, u32[]{:S(2)}) collective-permute-start(f32[4,136,512]{2,1,0:T(8,128)S(1)} %get-tuple-element.56), channel_id=1, source_target_pairs={{0,2},{2,0},{4,6},{6,4},{8,10},{10,8},{12,14},{14,12},{16,18},{18,... | collective-permute-start | bytes 3342344 | tf_op jit(solution)/shard_map/ppermute | solution.py:503
